TPU v7x, 32 devices: a whole 2x2x4 slice. The times are simulated.
32 devices in a mesh: dp: 4 (over y, core), feat: 8 (over z, x).
Axes of the slice: x: 2, y: 2, z: 4, core: 2. Of those that a mesh axis runs over, the one named last changes fastest.
Arguments:
- resid: bfloat16 [16384, 768], P(('dp', 'feat')), may hold values from -6 to 6
- segments: int32 [16, 1024], P('dp'), may hold values from 0 to 15, never falling along the last dimension, each value on 1 to 128 neighbouring positions
- keep: int32 [16384], P('dp'), may hold values from 0 to 1, as said below
- ln_gain: bfloat16 [768], replicated, may hold values from 0.5 to 1.5
- ln_bias: bfloat16 [768], replicated, may hold values from -0.625 to 0.625
- qkv_weight: bfloat16 [768, 2304], replicated, may hold values from -0.21875 to 0.21875
- qkv_bias: bfloat16 [2304], replicated
- enc_weight: float32 [768, 24576], P('dp', 'feat'), may hold values from -0.21875 to 0.21875
- enc_bias: float32 [24576], P('feat'), may hold values from -0.5 to 0
- dec_weight: float32 [24576, 768], P('feat', 'dp'), may hold values from -0.0390625 to 0.0390625
- dec_bias: float32 [768], replicated, may hold values from -4 to 4
- enc_weight_m: float32 [768, 24576], P('dp', 'feat')
- enc_weight_v: float32 [768, 24576], P('dp', 'feat')
- enc_bias_m: float32 [24576], P('feat')
- enc_bias_v: float32 [24576], P('feat')
- dec_weight_m: float32 [24576, 768], P('feat', 'dp')
- dec_weight_v: float32 [24576, 768], P('feat', 'dp')
- dec_bias_m: float32 [768], replicated
- dec_bias_v: float32 [768], replicated
Outputs:
- objective_accumulate_tally: float32 [2], replicated
- overall_derivative_length: float32 [], replicated
- feature_fire: float32 [24576], P('feat')
- enc_weight_new: float32 [768, 24576], P('dp', 'feat')
- enc_weight_m_new: float32 [768, 24576], P('dp', 'feat')
- enc_weight_v_new: float32 [768, 24576], P('dp', 'feat')
- enc_bias_new: float32 [24576], P('feat')
- enc_bias_m_new: float32 [24576], P('feat')
- enc_bias_v_new: float32 [24576], P('feat')
- dec_weight_new: float32 [24576, 768], P('feat', 'dp')
- dec_weight_m_new: float32 [24576, 768], P('feat', 'dp')
- dec_weight_v_new: float32 [24576, 768], P('feat', 'dp')
- dec_bias_new: float32 [768], replicated
- dec_bias_m_new: float32 [768], replicated
- dec_bias_v_new: float32 [768], replicated
Inputs may be any that keep to these rules, and one draw needn't show every extreme that they name: `segments`: within each row of 1024 tokens the context number never falls and each context holds 1 to 128 tokens, one exactly 128. `keep`: the first token of each row is 0 and the second is 1.
All inputs are finite; a program needn't handle non-finite values.
Results may differ from a plain program's by a relative error of at most 0.0018.
Values may be sent and summed in bfloat16 or wider, within the bound.
No kernel may reach another device: no remote copies, remote signals or barrier semaphores. Data moves between devices by JAX's collectives and lax.ppermute only.
A program may use at most 256 MiB of HBM per device.

v0:
```python
import math

import jax
import jax.numpy as jnp
from jax import lax
from jax.sharding import PartitionSpec as P

HEAD = 64
ROW_LEN = 1024
CTX = 128
STEP = 10


LAMBDA = 0.001
CLIP_NORM = 0.004
LEARN = 0.02
BETA_ONE = 0.9
BETA_TWO = 0.999
EPSILON = 1e-08
DECAY = 0.01


def passed_along(block, axis, distance):
    devices = range(lax.axis_size(axis))
    route = [(i - distance, i) for i in devices if i - distance in devices]
    return lax.ppermute(block, axis, route)


def attend(resid, seg_all, ln_gain, ln_bias, qkv_weight, qkv_bias):
    own_rows = resid.shape[0]
    width = resid.shape[1]
    heads = width // HEAD
    offset = lax.axis_index("feat") * own_rows
    values_in = resid.astype(jnp.float32)
    average = jnp.mean(values_in, axis=1, keepdims=True)
    centred = values_in - average
    variance = jnp.mean(centred * centred, axis=1, keepdims=True)
    normed = (
        centred * lax.rsqrt(variance + 1e-05) * ln_gain.astype(jnp.float32)
        + ln_bias.astype(jnp.float32)
    ).astype(jnp.bfloat16)
    projected = (
        jnp.dot(normed, qkv_weight, preferred_element_type=jnp.float32)
        + qkv_bias.astype(jnp.float32)
    ).astype(jnp.bfloat16)
    query = projected[:, :width].reshape(own_rows, heads, HEAD)
    pairs = projected[:, width:]
    tail = passed_along(pairs[own_rows - CTX :], "feat", 1)
    key_rows = jnp.concatenate([tail, pairs], axis=0)
    keys = key_rows[:, :width].reshape(CTX + own_rows, heads, HEAD)
    values = key_rows[:, width:].reshape(CTX + own_rows, heads, HEAD)
    places = offset + jnp.arange(own_rows, dtype=jnp.int32)
    tail_places = offset - CTX + jnp.arange(CTX, dtype=jnp.int32)
    own_seg = lax.dynamic_slice_in_dim(seg_all, offset, own_rows)
    tail_seg = lax.dynamic_slice_in_dim(seg_all, jnp.maximum(offset - CTX, 0), CTX)
    key_places = jnp.concatenate([tail_places, places])
    key_seg = jnp.concatenate([tail_seg, own_seg])
    allowed = (
        (key_seg[None, :] == own_seg[:, None])
        & (key_places[None, :] <= places[:, None])
        & (key_places[None, :] >= 0)
    )
    scores = jnp.einsum(
        "qhd,khd->hqk", query, keys, preferred_element_type=jnp.float32
    ) / math.sqrt(HEAD)
    scores = jnp.where(allowed[None], scores, -1e30)
    highest = jnp.max(scores, axis=2, keepdims=True)
    expo = jnp.exp(scores - highest)
    probs = (expo / jnp.sum(expo, axis=2, keepdims=True)).astype(jnp.bfloat16)
    mixed = jnp.einsum("hqk,khd->qhd", probs, values, preferred_element_type=jnp.float32)
    return (mixed.reshape(own_rows, width).astype(jnp.bfloat16), offset)


def adamw(weight, grad, first, second, decay):
    first = BETA_ONE * first + (1.0 - BETA_ONE) * grad
    second = BETA_TWO * second + (1.0 - BETA_TWO) * grad * grad
    hat_first = first / (1.0 - BETA_ONE**STEP)
    hat_second = second / (1.0 - BETA_TWO**STEP)
    weight = weight - LEARN * (hat_first / (jnp.sqrt(hat_second) + EPSILON) + decay * weight)
    return (weight, first, second)


def shards(
    resid,
    segments,
    keep,
    ln_gain,
    ln_bias,
    qkv_weight,
    qkv_bias,
    enc_weight,
    enc_bias,
    dec_weight,
    dec_bias,
    enc_weight_m,
    enc_weight_v,
    enc_bias_m,
    enc_bias_v,
    dec_weight_m,
    dec_weight_v,
    dec_bias_m,
    dec_bias_v,
):
    group = keep.shape[0]
    row_ids = jnp.arange(group, dtype=jnp.int32)
    seg_all = segments.reshape(group) + row_ids // ROW_LEN * ROW_LEN
    tokens_z, offset = attend(resid, seg_all, ln_gain, ln_bias, qkv_weight, qkv_bias)
    own_rows = resid.shape[0]
    width = resid.shape[1]
    keep_mask_full = keep.astype(jnp.float32)
    own_keep = lax.dynamic_slice_in_dim(keep_mask_full, offset, own_rows)
    hidden_code_float32 = tokens_z.astype(jnp.float32)
    counted, squares = lax.psum(
        (
            jnp.sum(own_keep),
            jnp.sum(own_keep * jnp.sum(hidden_code_float32 * hidden_code_float32, axis=1)),
        ),
        ("dp", "feat"),
    )
    mean_square = squares / (counted * width) + 1e-06
    z_group = lax.all_gather(tokens_z, "feat", axis=0, tiled=True)
    enc_full, dec_full = (
        lax.all_gather(enc_weight.astype(jnp.bfloat16), "dp", axis=0, tiled=True),
        lax.all_gather(dec_weight.astype(jnp.bfloat16), "dp", axis=1, tiled=True),
    )
    encoded = jnp.dot(z_group, enc_full, preferred_element_type=jnp.float32)
    preact = encoded + enc_bias
    dictionary_response = jax.nn.softplus(preact)
    act_low = dictionary_response.astype(jnp.bfloat16)
    dec_float = dec_full.astype(jnp.float32)
    row_norm = jnp.sqrt(jnp.sum(dec_float * dec_float, axis=1))
    keep_column = keep_mask_full[:, None]
    act_sum = jnp.sum(keep_column * dictionary_response, axis=0)
    nonzero_fraction = jnp.sum(keep_column * jnp.tanh(dictionary_response), axis=0)
    lasso_part = LAMBDA * jnp.sum(act_sum * row_norm)
    unit = 2.0 / (width * mean_square * counted)
    partial_value = lax.psum_scatter(
        jnp.dot(act_low, dec_full, preferred_element_type=jnp.float32),
        "feat",
        scatter_dimension=0,
        tiled=True,
    )
    residue = partial_value + dec_bias - hidden_code_float32
    grad_out = own_keep[:, None] * residue * unit
    fit_part = jnp.sum(own_keep * jnp.sum(residue * residue, axis=1)) / (width * mean_square)
    bias_part = jnp.sum(grad_out, axis=0)
    grad_group = lax.all_gather(grad_out.astype(jnp.bfloat16), "feat", axis=0, tiled=True)
    loss_part = fit_part + lasso_part
    loss_total = lax.psum(loss_part, ("dp", "feat"))
    grad_act = lax.dot_general(
        grad_group, dec_full, (((1,), (1,)), ((), ())), preferred_element_type=jnp.float32
    )
    grad_act = grad_act + LAMBDA / counted * keep_column * row_norm[None, :]
    grad_pre = grad_act * jax.nn.sigmoid(preact)
    intake_offset_share = jnp.sum(grad_pre, axis=0)
    enc_part = lax.dot_general(
        z_group,
        grad_pre.astype(jnp.bfloat16),
        (((0,), (0,)), ((), ())),
        preferred_element_type=jnp.float32,
    )
    dec_part = lax.dot_general(
        act_low, grad_group, (((0,), (0,)), ((), ())), preferred_element_type=jnp.float32
    )
    dec_part = dec_part + LAMBDA / counted * act_sum[:, None] * dec_float / row_norm[:, None]
    enc_grad, dec_grad = (
        lax.psum_scatter(enc_part, "dp", scatter_dimension=0, tiled=True),
        lax.psum_scatter(dec_part, "dp", scatter_dimension=1, tiled=True),
    )
    intake_offset_derivative, nonzero_tallies = lax.psum(
        (intake_offset_share, nonzero_fraction), "dp"
    )
    dec_bias_grad = lax.psum(bias_part, ("dp", "feat"))
    first_dp = lax.axis_index("dp") == 0
    first_both = first_dp & (lax.axis_index("feat") == 0)
    own_squares = jnp.sum(enc_grad * enc_grad) + jnp.sum(dec_grad * dec_grad)
    own_squares = own_squares + jnp.where(
        first_dp, jnp.sum(intake_offset_derivative * intake_offset_derivative), 0.0
    )
    own_squares = own_squares + jnp.where(first_both, jnp.sum(dec_bias_grad * dec_bias_grad), 0.0)
    total_squares = lax.psum(own_squares, ("dp", "feat"))
    overall_derivative_length = jnp.sqrt(total_squares)
    factor = jnp.minimum(1.0, CLIP_NORM / (overall_derivative_length + 1e-06))
    intake_matrix_revised, intake_matrix_mean_estimate, intake_matrix_square_estimate = adamw(
        enc_weight, enc_grad * factor, enc_weight_m, enc_weight_v, DECAY
    )
    intake_offset_revised, intake_offset_mean_estimate, intake_offset_square_estimate = adamw(
        enc_bias, intake_offset_derivative * factor, enc_bias_m, enc_bias_v, 0.0
    )
    readout_matrix_revised, readout_matrix_mean_estimate, readout_matrix_square_estimate = adamw(
        dec_weight, dec_grad * factor, dec_weight_m, dec_weight_v, DECAY
    )
    readout_offset_revised, readout_offset_mean_estimate, readout_offset_square_estimate = adamw(
        dec_bias, dec_bias_grad * factor, dec_bias_m, dec_bias_v, 0.0
    )
    row_squares = lax.psum(jnp.sum(readout_matrix_revised * readout_matrix_revised, axis=1), "dp")
    readout_matrix_revised = readout_matrix_revised * lax.rsqrt(row_squares + 1e-12)[:, None]
    objective_accumulate_tally = jnp.stack([loss_total, counted])
    return (
        objective_accumulate_tally,
        overall_derivative_length,
        nonzero_tallies,
        intake_matrix_revised,
        intake_matrix_mean_estimate,
        intake_matrix_square_estimate,
        intake_offset_revised,
        intake_offset_mean_estimate,
        intake_offset_square_estimate,
        readout_matrix_revised,
        readout_matrix_mean_estimate,
        readout_matrix_square_estimate,
        readout_offset_revised,
        readout_offset_mean_estimate,
        readout_offset_square_estimate,
    )


def solution(mesh):
    return jax.shard_map(
        shards,
        mesh=mesh,
        in_specs=(
            P(("dp", "feat"), None),
            P("dp", None),
            P("dp"),
            P(),
            P(),
            P(),
            P(),
            P("dp", "feat"),
            P("feat"),
            P("feat", "dp"),
            P(),
            P("dp", "feat"),
            P("dp", "feat"),
            P("feat"),
            P("feat"),
            P("feat", "dp"),
            P("feat", "dp"),
            P(),
            P(),
        ),
        out_specs=(
            P(),
            P(),
            P("feat"),
            P("dp", "feat"),
            P("dp", "feat"),
            P("dp", "feat"),
            P("feat"),
            P("feat"),
            P("feat"),
            P("feat", "dp"),
            P("feat", "dp"),
            P("feat", "dp"),
            P(),
            P(),
            P(),
        ),
        check_vma=False,
    )
```

profile of v0, /device:TPU:0, one launch (start us, length us, event | category | flops | bytes accessed | tf_op | source)
XLA Modules:
  0.0 869.8 jit_solution(11572026572011455260)
XLA Ops:
  7.3 3.0 convert_element_type.71
  10.4 1.3 convert_reduce_fusion
  11.7 1.5 fusion.24
  13.2 3.3 fusion.19
  16.6 1.4 copy-done.4
  18.0 5.9 collective-permute-start
  23.9 0.1 dynamic_slice.11
  24.0 0.1 dynamic_slice.10
  24.1 1.2 copy.39
  25.2 1.1 and_and_fusion
  26.3 5.1 collective-permute-done
  31.5 2.1 pad_maximum_fusion
  33.6 1.6 copy.40
  35.2 1.3 copy.38
  36.5 10.3 %fusion.50 = (f32[12,512]{1,0:T(8,128)S(1)}, f32[12,512,640]{2,1,0:T(8,128)}) fusion(bf16[512,12,64]{0,2,1:T(8,128)(2,1)} %bitcast.29, bf16[640,12,64]{0,2,1:T(8,128)(2,1)S(1)} %bitcast.28, pred[512,640]{1,0:T(8,128)(4,1)S(1)} %copy-done.7), kind=kOutput, calls=%fused_computation.98 | convolution fusion | flops 519045760 | bytes 17850368 | tf_op jit(solution)/shard_map/sub | solution.py:68
  46.8 7.9 multiply_reduce_fusion.5
  54.7 1.2 convert_element_type.73
  56.0 101.1 %all-gather.5.cloned.1.call-done = bf16[4096,768]{0,1:T(8,128)(2,1)} async-done(((bf16[512,768]{0,1:T(8,128)(2,1)}), bf16[4096,768]{0,1:T(8,128)(2,1)}) %all-gather.5.cloned.1.call-update) | async-done | bytes 6291472 | tf_op jit(solution)/shard_map/all_gather | solution.py:121
  157.2 60.0 %multiply_reduce_fusion = (f32[3072]{0:T(1024)}, f32[3072]{0:T(1024)S(1)}, f32[4096,3072]{1,0:T(8,128)}) fusion(f32[4096]{0:T(1024)S(1)} %convert_element_type.60, f32[3072]{0:T(1024)S(1)} %copy-done.17, bf16[4096,768]{0,1:T(8,128)(2,1)} %all-gather.5.cloned.1.call-done, bf16[768,3072]{1,0:T(8,128)(2,1)} %all-gather.7.cloned.1.call-done), kind=kOutput, calls=%fused_computation.2 | convolution fusion | flops 19465756672 | bytes 61394944 | tf_op jit(solution)/shard_map/dot_general | solution.py:126
  217.2 49.9 %fusion.5 = f32[4096,768]{1,0:T(8,128)} fusion(bf16[3072,768]{0,1:T(8,128)(2,1)} %all-gather.9.cloned.1.call-done, f32[4096,3072]{1,0:T(8,128)} %get-tuple-element.51, f32[3072]{0:T(1024)S(1)} %copy-done.17), kind=kOutput, calls=%fused_computation.12 | convolution fusion | flops 19428016128 | bytes 67645440 | tf_op jit(solution)/shard_map/dot_general | solution.py:138
  267.1 0.7 multiply_reduce_fusion.10
  267.8 42.8 %all-reduce.1 = (f32[]{:T(128)}, f32[]{:T(128)}) all-reduce(f32[]{:T(128)} %get-tuple-element.20, f32[]{:T(128)} %get-tuple-element.19), channel_id=1, replica_groups=mesh['dp'=4,'feat'=8] {'dp','feat'}, use_global_device_ids=true, to_apply=%region_11.12 | all-reduce | flops 2 | bytes 16 | tf_op jit(solution)/shard_map/psum | solution.py:113
  310.5 0.3 copy.41
  312.8 160.9 %reduce-scatter.4.cloned.1.call-done = f32[512,768]{1,0:T(8,128)} async-done(((f32[4096,768]{1,0:T(8,128)}), f32[512,768]{1,0:T(8,128)}) %reduce-scatter.4.cloned.1.call-update) | async-done | bytes 1572880 | tf_op jit(solution)/shard_map/reduce_scatter | solution.py:137
  473.7 3.3 fusion.29
  477.8 3.3 fusion.10
  481.1 0.6 broadcast_multiply_fusion.2
  481.7 93.6 %all-gather.11.cloned.1.call-done = bf16[4096,768]{1,0:T(8,128)(2,1)} async-done(((bf16[512,768]{1,0:T(8,128)(2,1)}), bf16[4096,768]{1,0:T(8,128)(2,1)}) %all-gather.11.cloned.1.call-update) | async-done | bytes 6291472 | tf_op jit(solution)/shard_map/all_gather | solution.py:147
  575.3 48.1 %fusion.12 = f32[3072,768]{0,1:T(8,128)} fusion(bf16[3072,768]{0,1:T(8,128)(2,1)} %all-gather.9.cloned.1.call-done, bf16[4096,768]{1,0:T(8,128)(2,1)} %all-gather.11.cloned.1.call-done, f32[3072]{0:T(1024)S(1)} %get-tuple-element.46, f32[3072]{0:T(1024)S(1)} %get-tuple-element.44, f32[4096,3072]{1,0:T(8,128)} %get-tuple-element.51, f32[3072]{0:T(1024)S(1)} %copy-done.17), kind=kOutput, calls=%fused_computation.20 | convolution fusion | flops 19437453312 | bytes 70815744 | tf_op jit(solution)/shard_map/dot_general | solution.py:162
  623.5 0.6 copy-done.9
  624.1 39.9 %fusion.51 = (f32[3072]{0:T(1024)S(1)}, bf16[4096,3072]{1,0:T(8,128)(2,1)}) fusion(f32[4096,3072]{1,0:T(8,128)} %get-tuple-element.51, f32[3072]{0:T(1024)S(1)} %copy-done.17, f32[3072]{0:T(1024)S(1)} %get-tuple-element.46, f32[4096]{0:T(1024)S(1)} %broadcast_multiply_fusion.1, bf16[4096,768]{1,0:T(8,128)(2,1)} %all-gather.11.cloned.1.call-done, ...), kind=kOutput, calls=%fused_computation.99 | convolution fusion | flops 19440594944 | bytes 86560768 | tf_op jit(solution)/shard_map/dot_general | solution.py:150
  664.1 26.2 %fusion.1 = f32[768,3072]{1,0:T(8,128)} fusion(bf16[4096,768]{0,1:T(8,128)(2,1)} %all-gather.5.cloned.1.call-done, bf16[4096,3072]{1,0:T(8,128)(2,1)} %get-tuple-element.53), kind=kOutput, calls=%fused_computation.5 | convolution fusion | flops 19327352832 | bytes 40894464 | tf_op jit(solution)/shard_map/dot_general | solution.py:156
  691.1 0.6 multiply_reduce_fusion.11
  692.4 37.2 %psum.60 = f32[768]{0:T(1024)S(1)} all-reduce(f32[768]{0:T(1024)S(1)} %copy-done.14), channel_id=1, replica_groups=mesh['dp'=4,'feat'=8] {'dp','feat'}, use_global_device_ids=true, to_apply=%region_24.25 | all-reduce | flops 768 | bytes 6144 | tf_op jit(solution)/shard_map/psum | solution.py:173
  729.6 0.6 multiply_reduce_fusion.9
  730.9 11.6 %psum.59 = f32[3072]{0:T(1024)S(1)} all-reduce(f32[3072]{0:T(1024)S(1)} %get-tuple-element.52), channel_id=1, replica_groups=mesh['dp'=4,'feat'=8] {'dp'}, use_global_device_ids=true, to_apply=%region_21.22 | all-reduce | flops 3072 | bytes 24576 | tf_op jit(solution)/shard_map/psum | solution.py:170
  742.5 0.6 multiply_reduce_fusion.7
  743.8 3.0 multiply_reduce_fusion.3
  746.8 35.2 %reduce-scatter.6.cloned.1.call-done = f32[192,3072]{1,0:T(8,128)} async-done(((f32[768,3072]{1,0:T(8,128)}), f32[192,3072]{1,0:T(8,128)}) %reduce-scatter.6.cloned.1.call-update) | async-done | bytes 2359312 | tf_op jit(solution)/shard_map/reduce_scatter | solution.py:167
  782.1 2.9 multiply_reduce_fusion.4
  786.3 40.4 %all-reduce = (f32[1]{0:T(128)}, f32[]{:T(128)}) all-reduce(f32[1]{0:T(128)} %bitcast.6, f32[]{:T(128)S(6)} %add.216), channel_id=1, replica_groups=mesh['dp'=4,'feat'=8] {'dp','feat'}, use_global_device_ids=true, to_apply=%region_15.16 | all-reduce | flops 2 | bytes 16 | tf_op jit(solution)/shard_map/psum | solution.py:149
  827.4 7.6 multiply_reduce_fusion.2
  835.1 11.7 %all-reduce.2 = (f32[3072]{0:T(1024)}, f32[3072]{0:T(1024)S(1)}) all-reduce(f32[3072]{0:T(1024)S(1)} %copy-done.16, f32[3072]{0:T(1024)S(1)} %get-tuple-element.36), channel_id=1, replica_groups=mesh['dp'=4,'feat'=8] {'dp'}, use_global_device_ids=true, to_apply=%region_28.29 | all-reduce | flops 6144 | bytes 49152 | tf_op jit(solution)/shard_map/psum | solution.py:170
  846.8 0.6 multiply_subtract_fusion.3
  847.5 3.4 broadcast_multiply_fusion
  850.8 0.6 multiply_subtract_fusion.2
  851.4 1.9 pad_maximum_fusion.1
  853.3 8.3 multiply_subtract_fusion.1
  (85 shorter events, 0.7 us)
Async XLA Ops:
  7.2 6.0 copy-start
  7.2 3.1 copy-start.21
  7.2 3.2 copy-start.24
  7.2 3.2 copy-start.25
  7.2 48.8 %all-gather.7.cloned.1.call-start = ((), (), s32[]{:S(2)}) async-start(), calls=%async_computation.4 | async-start | bytes 5898240 | tf_op jit(solution)/shard_map/all_gather | solution.py:123
  10.3 146.9 %all-gather.5.cloned.1.call-start = ((), (), s32[]{:S(2)}) async-start(), calls=%async_computation.3 | async-start | bytes 7077888 | tf_op jit(solution)/shard_map/all_gather | solution.py:121
  13.2 10.6 %copy-start.15 = (s32[4,1024]{1,0:T(4,128)S(1)}, s32[4,1024]{1,0:T(4,128)}, u32[]{:S(2)}) copy-start(s32[4,1024]{1,0:T(4,128)} %param.20) | copy-start | bytes 49156
  16.5 1.4 copy-start.4
  18.0 6.1 slice-start.1
  18.0 13.5 %slice-start = ((bf16[512,2304]{1,0:T(8,128)(2,1)}), bf16[512,1536]{1,0:T(8,128)(2,1)S(1)}, s32[]{:S(2)}) async-start(bf16[512,2304]{1,0:T(8,128)(2,1)} %copy-done.4), calls=%async_computation.10 | async-start | bytes 3145728 | tf_op jit(solution)/shard_map/slice | solution.py:47
  18.0 13.5 %collective-permute-start = (bf16[128,1536]{1,0:T(8,128)(2,1)S(1)}, bf16[128,1536]{1,0:T(8,128)(2,1)}, u32[]{:S(2)}, u32[]{:S(2)}) collective-permute-start(bf16[128,1536]{1,0:T(8,128)(2,1)S(1)} %slice.21), channel_id=1, source_target_pairs={{0,1},{1,2},{2,3},{3,4},{4,5},{5,6},{6,7},{8,9},{9,10},{10,11},{11... | collective-permute-start | bytes 1179656 | tf_op jit(solution)/shard_map/ppermute | solution.py:26
  33.6 2.9 copy-start.7
  36.5 10.3 %copy-start.6 = (bf16[640,768]{0,1:T(8,128)(2,1)S(1)}, bf16[640,768]{0,1:T(8,128)(2,1)}, u32[]{:S(2)}) copy-start(bf16[640,768]{0,1:T(8,128)(2,1)} %copy.38) | copy-start | bytes 2949124
  46.8 7.9 copy-start.2
  54.7 1.3 copy-start.8
  54.7 102.5 %copy-start.17 = (f32[3072]{0:T(1024)S(1)}, f32[3072]{0:T(1024)}, u32[]{:S(2)}) copy-start(f32[3072]{0:T(1024)} %param.27) | copy-start | bytes 36868
  54.7 162.5 %all-gather.9.cloned.1.call-start = ((), (), s32[]{:S(2)}) async-start(), calls=%async_computation.5 | async-start | bytes 5898240 | tf_op jit(solution)/shard_map/all_gather | solution.py:124
  55.9 417.7 %reduce-scatter.4.cloned.1.call-start = ((), (), s32[]{:S(2)}) async-start(), calls=%async_computation.6 | async-start | bytes 14155776 | tf_op jit(solution)/shard_map/reduce_scatter | solution.py:137
  267.0 43.5 %copy-start.5 = (bf16[12,64,512]{2,1,0:T(8,128)(2,1)S(1)}, bf16[12,64,512]{2,1,0:T(8,128)(2,1)}, u32[]{:S(2)}) copy-start(bf16[12,64,512]{2,1,0:T(8,128)(2,1)} %get-tuple-element.50) | copy-start | bytes 2359300
  267.0 206.7 %copy-start.12 = (f32[768]{0:T(1024)S(1)}, f32[768]{0:T(1024)}, u32[]{:S(2)}) copy-start(f32[768]{0:T(1024)} %param.29) | copy-start | bytes 9220
  267.0 308.3 %all-gather.11.cloned.1.call-start = ((), (), s32[]{:S(2)}) async-start(), calls=%async_computation.7 | async-start | bytes 7077888 | tf_op jit(solution)/shard_map/all_gather | solution.py:147
  267.8 213.3 %copy-start.10 = (f32[512]{0:T(512)}, f32[512]{0:T(512)S(1)}, u32[]{:S(2)}) copy-start(f32[512]{0:T(512)S(1)} %get-tuple-element.40) | copy-start | bytes 6148
  477.0 266.7 %reduce-scatter.8.cloned.1.call-start = ((), (), s32[]{:S(2)}) async-start(), calls=%async_computation.9 | async-start | bytes 11796480 | tf_op jit(solution)/shard_map/reduce_scatter | solution.py:168
  623.4 0.7 copy-start.9
  623.4 158.6 %reduce-scatter.6.cloned.1.call-start = ((), (), s32[]{:S(2)}) async-start(), calls=%async_computation.8 | async-start | bytes 11796480 | tf_op jit(solution)/shard_map/reduce_scatter | solution.py:167
  690.3 0.9 copy-start.11
  690.3 0.9 copy-start.20
  690.3 2.1 copy-start.14
  690.3 137.1 %copy-start.3 = (f32[3072,192]{0,1:T(8,128)S(1)}, f32[3072,192]{0,1:T(8,128)}, u32[]{:S(2)}) copy-start(f32[3072,192]{0,1:T(8,128)} %param.28) | copy-start | bytes 7077892
  827.4 7.7 copy-start.16
  827.4 19.4 %copy-start.13 = (f32[768]{0:T(1024)S(1)}, f32[768]{0:T(1024)}, u32[]{:S(2)}) copy-start(f32[768]{0:T(1024)} %param.29) | copy-start | bytes 9220
  827.4 19.4 %copy-start.22 = (f32[768]{0:T(1024)S(1)}, f32[768]{0:T(1024)}, u32[]{:S(2)}) copy-start(f32[768]{0:T(1024)} %param.36) | copy-start | bytes 9220
  827.4 19.4 %copy-start.23 = (f32[768]{0:T(1024)S(1)}, f32[768]{0:T(1024)}, u32[]{:S(2)}) copy-start(f32[768]{0:T(1024)} %param.37) | copy-start | bytes 9220
  835.1 15.8 %copy-start.18 = (f32[3072]{0:T(1024)S(1)}, f32[3072]{0:T(1024)}, u32[]{:S(2)}) copy-start(f32[3072]{0:T(1024)} %param.32) | copy-start | bytes 36868
  835.1 15.8 %copy-start.19 = (f32[3072]{0:T(1024)S(1)}, f32[3072]{0:T(1024)}, u32[]{:S(2)}) copy-start(f32[3072]{0:T(1024)} %param.33) | copy-start | bytes 36868
  853.3 8.3 copy-start.1
Sparse Core Ops, SparseCore 0:
  10.4 40.1 all-gather.6
  54.8 102.2 all-gather.4
  159.3 35.6 all-gather.8
  267.2 206.4 reduce-scatter.3
  477.2 98.1 all-gather.10
  623.6 77.1 reduce-scatter.7
  703.3 78.6 reduce-scatter.5
where the time goes:
time: 877 us; the launch traced here: 870 us
  waiting for transfers between devices  396 us (45%)
  matrix products  246 us (28%)
  blocking collectives  144 us (16%)
  other arithmetic  48.3 us (6%)
  between operations  23.3 us (3%)
    reduce_scatter x1, waiting for transfers between devices, shards(): lax.psum_scatter(jnp.dot(act_low, dec_full, preferred_element_type=jnp.fl...  161 us
    all_gather x1, waiting for transfers between devices, shards(): z_group = lax.all_gather(tokens_z, 'feat', axis=0, tiled=True)  101 us
    all_gather x1, waiting for transfers between devices, shards(): lax.all_gather(grad_out.astype(jnp.bfloat16), 'feat', axis=0, tiled=True)  93.6 us
    dot_general x1, matrix products, shards(): encoded = jnp.dot(z_group, enc_full, preferred_element_type=jnp.float32)  60 us
    dot_general x1, matrix products, shards(): jnp.dot(act_low, dec_full, preferred_element_type=jnp.float32)  49.9 us
    dot_general x1, matrix products, shards(): lax.dot_general(act_low, grad_group, (((0,), (0,)), ((), ())), preferred_...  48.1 us
    psum x1, blocking collectives, shards(): lax.psum((jnp.sum(own_keep), jnp.sum(own_keep * jnp.sum(hidden_code_float...  42.8 us
    psum x1, blocking collectives, shards(): loss_total = lax.psum(loss_part, ('dp', 'feat'))  40.4 us
  transfers between devices with their start and end apart: 8, of which 5 were waited for; matrix products, arithmetic and copies ran while one was open for 19% of the time, Pallas kernels for 0%

commit v1 on v0

v1 whole, which is shorter than its diff:
```python
import functools
import math

import jax
import jax.numpy as jnp
from jax import lax
from jax.experimental import pallas as pl
from jax.experimental.pallas import tpu as pltpu
from jax.sharding import PartitionSpec as P

HEAD = 64
ROW_LEN = 1024
CTX = 128
STEP = 10

LAMBDA = 0.001
CLIP_NORM = 0.004
LEARN = 0.02
BETA_ONE = 0.9
BETA_TWO = 0.999
EPSILON = 1e-08
DECAY = 0.01

FEATURE_BLOCK = 512
ROW_BLOCK = 256
LAST_PARTS = 3
VMEM_BYTES = 56 * 2**20
BF16 = jnp.bfloat16
F32 = jnp.float32


def kernel_params():
    return pltpu.CompilerParams(vmem_limit_bytes=VMEM_BYTES)


def dot_nn(a, b):
    return jnp.dot(a, b, preferred_element_type=F32)


def dot_nt(a, b):
    return lax.dot_general(a, b, (((1,), (1,)), ((), ())), preferred_element_type=F32)


def attend_kernel(own_ref, tail_ref, seg_q_ref, seg_k_ref, gain_ref, bias_ref, w_ref, wb_ref, z_ref, q_s, kv_s):
    rows, width = own_ref.shape

    def normed(block):
        values = block.astype(F32)
        centred = values - jnp.mean(values, axis=1, keepdims=True)
        variance = jnp.mean(centred * centred, axis=1, keepdims=True)
        gain = gain_ref[...].astype(F32)
        return (centred * lax.rsqrt(variance + 1e-05) * gain + bias_ref[...].astype(F32)).astype(BF16)

    own = normed(own_ref[...])
    q_s[...] = (dot_nn(own, w_ref[:, :width]) + wb_ref[:, :width].astype(F32)).astype(BF16)
    kv_s[CTX:, :] = (dot_nn(own, w_ref[:, width:]) + wb_ref[:, width:].astype(F32)).astype(BF16)
    tail = normed(tail_ref[...])
    kv_s[:CTX, :] = (dot_nn(tail, w_ref[:, width:]) + wb_ref[:, width:].astype(F32)).astype(BF16)

    lane = lax.broadcasted_iota(jnp.int32, (CTX, 2 * HEAD), 1)
    first_head = lane < HEAD
    for block in range(rows // CTX):
        base = block * CTX
        place_q = lax.broadcasted_iota(jnp.int32, (CTX, 2 * CTX), 0) + CTX
        place_k = lax.broadcasted_iota(jnp.int32, (CTX, 2 * CTX), 1)
        allowed = (seg_q_ref[base : base + CTX, :] == seg_k_ref[:, base : base + 2 * CTX]) & (place_k <= place_q)
        for pair in range(width // (2 * HEAD)):
            columns = slice(pair * 2 * HEAD, (pair + 1) * 2 * HEAD)
            query = q_s[base : base + CTX, columns]
            keys = kv_s[base : base + 2 * CTX, columns]
            values = kv_s[base : base + 2 * CTX, width + pair * 2 * HEAD : width + (pair + 1) * 2 * HEAD]
            mixed = []
            for half in range(2):
                mine = first_head if half == 0 else ~first_head
                part = jnp.where(mine, query, jnp.zeros_like(query))
                scores = dot_nt(part, keys) * (1.0 / math.sqrt(HEAD))
                scores = jnp.where(allowed, scores, -1e30)
                expo = jnp.exp(scores - jnp.max(scores, axis=1, keepdims=True))
                probs = (expo / jnp.sum(expo, axis=1, keepdims=True)).astype(BF16)
                mixed.append(dot_nn(probs, values))
            z_ref[base : base + CTX, columns] = jnp.where(first_head, mixed[0], mixed[1]).astype(BF16)


def attend(resid, tail, seg_q, seg_k, ln_gain, ln_bias, qkv_weight, qkv_bias):
    rows, width = resid.shape
    return pl.pallas_call(
        attend_kernel,
        out_shape=jax.ShapeDtypeStruct((rows, width), BF16),
        scratch_shapes=[
            pltpu.VMEM((rows, width), BF16),
            pltpu.VMEM((rows + CTX, 2 * width), BF16),
        ],
        compiler_params=kernel_params(),
        cost_estimate=pl.CostEstimate(flops=8 * rows * width * width, bytes_accessed=2 * 3 * width * width, transcendentals=rows * 2 * CTX * 12),
        name="attend",
    )(resid, tail, seg_q, seg_k, ln_gain[None], ln_bias[None], qkv_weight, qkv_bias[None])


def encode_kernel(count, *refs):
    z_refs, (keep_ref, enc_ref, bias_ref, dec_ref), rest = refs[:count], refs[count : count + 4], refs[count + 4 :]
    act_ref, rec_refs, (sum_ref, fire_ref) = rest[0], rest[1 : 1 + count], rest[1 + count : 3 + count]
    totals = rest[3 + count :]
    step, last = pl.program_id(0), pl.num_programs(0) - 1
    features = enc_ref.shape[1]

    @pl.when(step == 0)
    def _():
        for total in totals:
            total[...] = jnp.zeros_like(total)

    sums = jnp.zeros((8, features), F32)
    fires = jnp.zeros((8, features), F32)
    start = 0
    for piece in range(count):
        block = min(ROW_BLOCK, z_refs[piece].shape[0])
        for base in range(0, z_refs[piece].shape[0], block):
            rows = slice(base, base + block)
            spot = slice(start + base, start + base + block)
            preact = dot_nn(z_refs[piece][rows, :], enc_ref[...]) + bias_ref[...]
            tiny = jnp.exp(-jnp.abs(preact))
            log_part = jnp.where(tiny < 2.0**-10, tiny * (1.0 - 0.5 * tiny), jnp.log(1.0 + tiny))
            act = jnp.maximum(preact, 0.0) + log_part
            low = act.astype(BF16)
            act_ref[spot, :] = low
            kept = keep_ref[spot, :]
            sums = sums + jnp.sum((kept * act).reshape(block // 8, 8, features), axis=0)
            fires = fires + jnp.sum((kept * jnp.tanh(act)).reshape(block // 8, 8, features), axis=0)
            part = dot_nt(low, dec_ref[...])
            totals[piece][rows, :] += part
        start += z_refs[piece].shape[0]
    sum_ref[...] = jnp.sum(sums, axis=0, keepdims=True)
    fire_ref[...] = jnp.sum(fires, axis=0, keepdims=True)

    @pl.when(step == last)
    def _():
        for piece in range(count):
            rec_refs[piece][...] = totals[piece][...].astype(rec_refs[piece].dtype)


def encode(pieces, keep_column, enc, bias, dec_t, out_dtype):
    width, features = enc.shape
    sizes = [p.shape[0] for p in pieces]
    tokens = sum(sizes)
    fb = FEATURE_BLOCK
    whole = lambda j: (0, 0)
    across = lambda j: (0, j)
    outs = pl.pallas_call(
        functools.partial(encode_kernel, len(pieces)),
        grid=(features // fb,),
        in_specs=[pl.BlockSpec((s, width), whole) for s in sizes]
        + [
            pl.BlockSpec((tokens, 1), whole),
            pl.BlockSpec((width, fb), across),
            pl.BlockSpec((1, fb), across),
            pl.BlockSpec((width, fb), across),
        ],
        out_specs=[pl.BlockSpec((tokens, fb), across)]
        + [pl.BlockSpec((s, width), whole) for s in sizes]
        + [pl.BlockSpec((1, fb), across)] * 2,
        out_shape=[jax.ShapeDtypeStruct((tokens, features), BF16)]
        + [jax.ShapeDtypeStruct((s, width), out_dtype) for s in sizes]
        + [jax.ShapeDtypeStruct((1, features), F32)] * 2,
        scratch_shapes=[pltpu.VMEM((s, width), F32) for s in sizes],
        compiler_params=kernel_params(),
        cost_estimate=pl.CostEstimate(
            flops=4 * tokens * width * features,
            bytes_accessed=2 * (2 * width * features + tokens * (features + 4 * width)),
            transcendentals=3 * tokens * features,
        ),
        name="encode",
    )(*pieces, keep_column, enc, bias, dec_t)
    return outs[0], outs[1 : 1 + len(pieces)], outs[-2], outs[-1]


def backward_kernel(groups, carried, parted, *refs):
    refs = list(refs)
    slots = refs.pop(0) if parted else None
    acts, zs, gs = [], [], []
    for count in groups:
        acts.append(refs.pop(0))
        zs.append([refs.pop(0) for _ in range(count)])
        gs.append([refs.pop(0) for _ in range(count)])
    keep_ref, norm_ref, dec_ref = refs.pop(0), refs.pop(0), refs.pop(0)
    enc_in, dec_in = (refs.pop(0), refs.pop(0)) if carried else (None, None)
    outs = [refs.pop(0) for _ in range(4 if parted else 2)]
    bias_ref = refs.pop(0)
    z_t, g_t, pre_s = refs

    @pl.when(pl.program_id(0) == 0)
    def _():
        spot = 0
        for z_list, g_list in zip(zs, gs):
            for z_ref, g_ref in zip(z_list, g_list):
                size = z_ref.shape[0]
                z_t[:, spot : spot + size] = z_ref[...].T
                g_t[:, spot : spot + size] = g_ref[...].T
                spot += size

    features = dec_ref.shape[1]
    spot = 0
    sums = jnp.zeros((8, features), F32)
    for act_ref, g_list in zip(acts, gs):
        at = 0
        for g_ref in g_list:
            block = min(ROW_BLOCK, g_ref.shape[0])
            for base in range(0, g_ref.shape[0], block):
                grad_act = dot_nn(g_ref[base : base + block, :], dec_ref[...])
                act = act_ref[at : at + block, :].astype(F32)
                slope = jnp.where(act < 2.0**-10, act * (1.0 - 0.5 * act), 1.0 - jnp.exp(-act))
                pre = (grad_act + keep_ref[spot : spot + block, :] * norm_ref[...]) * slope
                sums = sums + jnp.sum(pre.reshape(block // 8, 8, features), axis=0)
                pre_s[spot : spot + block, :] = pre.astype(BF16)
                at += block
                spot += block
    bias_ref[...] = jnp.sum(sums, axis=0, keepdims=True)
    enc_part = dot_nn(z_t[...], pre_s[...])
    dec_part = None
    spot = 0
    for act_ref in acts:
        size = act_ref.shape[0]
        term = dot_nn(g_t[:, spot : spot + size], act_ref[...])
        dec_part = term if dec_part is None else dec_part + term
        spot += size
    if carried:
        enc_part = enc_part + enc_in[...]
        dec_part = dec_part + dec_in[...]
    if not parted:
        outs[0][...] = enc_part
        outs[1][...] = dec_part
        return
    for value, keep_out, send_out in ((enc_part, outs[0], outs[1]), (dec_part, outs[2], outs[3])):
        rows = value.shape[0] // parted
        me = slots[0]
        for owner in range(parted):
            away = owner ^ me
            half = away // 2
            piece = value[owner * rows : (owner + 1) * rows, :]

            @pl.when(away % 2 == 0)
            def _():
                keep_out[pl.ds(half, 1)] = piece[None].astype(keep_out.dtype)

            @pl.when(away % 2 == 1)
            def _():
                send_out[pl.ds(half, 1)] = piece[None].astype(send_out.dtype)


def backward(groups, keep_column, norm_scaled, dec_t, carried, first, wide, parted, me):
    width = dec_t.shape[0]
    counts = [len(zs) for _, zs, _ in groups]
    tokens = sum(act.shape[0] for act, _, _ in groups)
    fb = FEATURE_BLOCK
    start = first // fb
    whole = lambda j, *_: (0, 0)
    across = lambda j, *_: (0, j + start)
    local = lambda j, *_: (0, j)
    operands, specs = [], []
    for act, zs, gs in groups:
        operands.append(act)
        specs.append(pl.BlockSpec((act.shape[0], fb), across))
        for piece in (*zs, *gs):
            operands.append(piece)
            specs.append(pl.BlockSpec(piece.shape, whole))
    operands += [keep_column, norm_scaled, dec_t]
    specs += [pl.BlockSpec((tokens, 1), whole), pl.BlockSpec((1, fb), across), pl.BlockSpec((width, fb), across)]
    if carried is not None:
        operands += list(carried)
        specs += [pl.BlockSpec((width, fb), across)] * 2
    if parted:
        shape = (parted // 2, width // parted, wide)
        block = pl.BlockSpec((parted // 2, width // parted, fb), lambda j, *_: (0, 0, j))
        out_shape = [jax.ShapeDtypeStruct(shape, F32)] * 4
        out_specs = [block] * 4
    else:
        out_shape = [jax.ShapeDtypeStruct((width, wide), F32)] * 2
        out_specs = [pl.BlockSpec((width, fb), local)] * 2
    out_shape.append(jax.ShapeDtypeStruct((1, wide), F32))
    out_specs.append(pl.BlockSpec((1, fb), local))
    scratch = [pltpu.VMEM((width, tokens), BF16), pltpu.VMEM((width, tokens), BF16), pltpu.VMEM((tokens, fb), BF16)]
    return pl.pallas_call(
        functools.partial(backward_kernel, counts, carried is not None, parted),
        grid_spec=pltpu.PrefetchScalarGridSpec(
            num_scalar_prefetch=1 if parted else 0,
            grid=(wide // fb,),
            in_specs=specs,
            out_specs=out_specs,
            scratch_shapes=scratch,
        ),
        out_shape=out_shape,
        compiler_params=kernel_params(),
        cost_estimate=pl.CostEstimate(
            flops=6 * tokens * width * wide,
            bytes_accessed=2 * tokens * wide + 16 * width * wide,
            transcendentals=tokens * wide,
        ),
        name="backward",
    )(*([me] if parted else []), *operands)


def ring_order(count):
    return list(range(0, count, 2)) + list(range(1, count, 2))[::-1]


def ring_shift(block, direction):
    order = ring_order(lax.axis_size("feat"))
    count = len(order)
    route = [(order[i], order[(i + direction) % count]) for i in range(count)]
    return lax.ppermute(block, "feat", route)


def swapped(block, axis, bit):
    return lax.ppermute(block, axis, [(i, i ^ bit) for i in range(lax.axis_size(axis))])


def summed(block, axes):
    for axis in axes:
        bit = 1
        while bit < lax.axis_size(axis):
            block = block + swapped(block, axis, bit)
            bit *= 2
    return block


def ring_gather(own):
    half = lax.axis_size("feat") // 2
    rows = own.shape[0] // 2
    stages = [[own]]
    right, left = own, own
    for hop in range(1, half + 1):
        if hop == half:
            right, left = right[:rows], left[rows:]
        right, left = ring_shift(right, 1), ring_shift(left, -1)
        stages.append([right, left])
    return stages


def adamw(weight, grad, first, second, decay):
    first = BETA_ONE * first + (1.0 - BETA_ONE) * grad
    second = BETA_TWO * second + (1.0 - BETA_TWO) * grad * grad
    hat_first = first / (1.0 - BETA_ONE**STEP)
    hat_second = second / (1.0 - BETA_TWO**STEP)
    weight = weight - LEARN * (hat_first / (jnp.sqrt(hat_second) + EPSILON) + decay * weight)
    return (weight, first, second)


def shards(
    resid,
    segments,
    keep,
    ln_gain,
    ln_bias,
    qkv_weight,
    qkv_bias,
    enc_weight,
    enc_bias,
    dec_weight,
    dec_bias,
    enc_weight_m,
    enc_weight_v,
    enc_bias_m,
    enc_bias_v,
    dec_weight_m,
    dec_weight_v,
    dec_bias_m,
    dec_bias_v,
):
    own_rows, width = resid.shape
    group = keep.shape[0]
    feat_size, dp_size = lax.axis_size("feat"), lax.axis_size("dp")
    half = feat_size // 2
    features = enc_weight.shape[1]
    feat_at, dp_at = lax.axis_index("feat"), lax.axis_index("dp")
    everywhere = ("dp", "feat")

    tail = lax.ppermute(resid[own_rows - CTX :], "feat", [(i, i + 1) for i in range(feat_size - 1)])
    enc_full = lax.all_gather(enc_weight.astype(BF16), "dp", axis=0, tiled=True)
    dec_full = lax.all_gather(dec_weight.astype(BF16).T, "dp", axis=0, tiled=True)

    offset = feat_at * own_rows
    row_ids = jnp.arange(group, dtype=jnp.int32)
    seg_all = segments.reshape(group) + row_ids // ROW_LEN * ROW_LEN
    own_seg = lax.dynamic_slice_in_dim(seg_all, offset, own_rows)
    tail_seg = lax.dynamic_slice_in_dim(seg_all, jnp.maximum(offset - CTX, 0), CTX)
    tail_seg = jnp.where(feat_at > 0, tail_seg, -1)
    key_seg = jnp.concatenate([tail_seg, own_seg])
    tokens_z = attend(resid, tail, own_seg[:, None], key_seg[None], ln_gain, ln_bias, qkv_weight, qkv_bias)

    order = jnp.asarray(ring_order(feat_size), jnp.int32)
    place = jnp.where(feat_at % 2 == 0, feat_at // 2, feat_size - 1 - feat_at // 2)
    keep_mask = keep.astype(F32)
    keep_rows = keep_mask.reshape(feat_size, own_rows)
    hops = [0]
    for hop in range(1, half):
        hops += [-hop, hop]
    hops.append(half)
    owners = order[(place + jnp.asarray(hops, jnp.int32)) % feat_size]
    keep_ring = keep_rows[owners].reshape(group, 1)
    keep_stage = [keep_ring[:own_rows]]
    for hop in range(1, half):
        keep_stage.append(keep_ring[(2 * hop - 1) * own_rows : (2 * hop + 1) * own_rows])
    keep_stage.append(keep_ring[group - own_rows :])
    own_keep = keep_stage[0]

    z_float = tokens_z.astype(F32)
    counted, squares = summed(
        jnp.stack([jnp.sum(own_keep), jnp.sum(own_keep * z_float * z_float)]), everywhere
    )
    mean_square = squares / (counted * width) + 1e-06
    unit = 2.0 / (width * mean_square * counted)

    z_stages = ring_gather(tokens_z)
    row_norm = jnp.sqrt(jnp.sum(dec_full.astype(F32) ** 2, axis=0, keepdims=True))
    acts, recs, sums, fires = [], [], [], []
    for hop, pieces in enumerate(z_stages):
        act, rec, act_sum, fire = encode(
            pieces, keep_stage[hop], enc_full, enc_bias[None], dec_full, BF16 if hop == half else F32
        )
        acts.append(act)
        recs.append(rec)
        sums.append(act_sum)
        fires.append(fire)
    act_sum, fire_sum = sum(sums), sum(fires)

    rows = own_rows // 2
    right, left = recs[half]
    for hop in range(half - 1, -1, -1):
        right, left = ring_shift(right, 1).astype(F32), ring_shift(left, -1).astype(F32)
        if hop == 0:
            break
        from_left, from_right = recs[hop]
        if hop == half - 1:
            right = jnp.concatenate([from_right[:rows] + right, from_right[rows:]])
            left = jnp.concatenate([from_left[:rows], from_left[rows:] + left])
        else:
            right, left = from_right + right, from_left + left
        right, left = right.astype(BF16), left.astype(BF16)
    residue = recs[0][0] + right + left + dec_bias - z_float
    grad_out = own_keep * residue * unit
    fit_part = jnp.sum(own_keep * residue * residue) / (width * mean_square)
    bias_part = jnp.sum(grad_out, axis=0)
    loss_part = fit_part + LAMBDA * jnp.sum(act_sum * row_norm)

    grad_stages = ring_gather(grad_out.astype(BF16))
    norm_scaled = LAMBDA / counted * row_norm
    me = dp_at.reshape(1).astype(jnp.int32)
    bias_grads = []
    carried = None
    plans = [[0, 1]] + [[hop] for hop in range(2, half - 1)] + [[half - 1, half]]
    for plan in plans[:-1]:
        groups = [(acts[hop], z_stages[hop], grad_stages[hop]) for hop in plan]
        keep_column = jnp.concatenate([keep_stage[hop] for hop in plan])
        *carried, bias_grad = backward(groups, keep_column, norm_scaled, dec_full, carried, 0, features, 0, None)
        bias_grads.append(bias_grad)
    plan = plans[-1]
    groups = [(acts[hop], z_stages[hop], grad_stages[hop]) for hop in plan]
    keep_column = jnp.concatenate([keep_stage[hop] for hop in plan])
    wide = features // LAST_PARTS
    enc_grads, dec_grads, last_bias = [], [], []
    for part in range(LAST_PARTS):
        enc_keep, enc_send, dec_keep, dec_send, bias_grad = backward(
            groups, keep_column, norm_scaled, dec_full, carried, part * wide, wide, dp_size, me
        )
        last_bias.append(bias_grad)
        for kept, sent, into in ((enc_keep, enc_send, enc_grads), (dec_keep, dec_send, dec_grads)):
            total = kept + swapped(sent, "dp", 1)
            own = total[0]
            for other in range(1, dp_size // 2):
                own = own + swapped(total[other].astype(BF16), "dp", 2 * other).astype(F32)
            into.append(own)
    enc_grad = jnp.concatenate(enc_grads, axis=1)
    dec_grad = jnp.concatenate(dec_grads, axis=1)
    bias_share = sum(bias_grads) + jnp.concatenate(last_bias, axis=1)
    enc_bias_grad, fired, act_total = summed(jnp.concatenate([bias_share, fire_sum, act_sum]), ("dp",))
    dec_bias_grad = summed(bias_part, everywhere)
    own_dec = dec_weight.astype(BF16).astype(F32)
    penalty = (LAMBDA / counted) * act_total / row_norm[0]
    dec_grad = dec_grad.T + penalty[:, None] * own_dec

    first_dp = dp_at == 0
    first_both = first_dp & (feat_at == 0)
    own_squares = jnp.sum(enc_grad * enc_grad) + jnp.sum(dec_grad * dec_grad)
    own_squares = own_squares + jnp.where(first_dp, jnp.sum(enc_bias_grad * enc_bias_grad), 0.0)
    own_squares = own_squares + jnp.where(first_both, jnp.sum(dec_bias_grad * dec_bias_grad), 0.0)
    total_squares, loss_total = summed(jnp.stack([own_squares, loss_part]), everywhere)
    overall_derivative_length = jnp.sqrt(total_squares)
    factor = jnp.minimum(1.0, CLIP_NORM / (overall_derivative_length + 1e-06))
    dec_new, dec_m, dec_v = adamw(dec_weight, dec_grad * factor, dec_weight_m, dec_weight_v, DECAY)
    row_squares = summed(jnp.sum(dec_new * dec_new, axis=1), ("dp",))
    enc_new, enc_m, enc_v = adamw(enc_weight, enc_grad * factor, enc_weight_m, enc_weight_v, DECAY)
    bias_new, bias_m, bias_v = adamw(enc_bias, enc_bias_grad * factor, enc_bias_m, enc_bias_v, 0.0)
    out_new, out_m, out_v = adamw(dec_bias, dec_bias_grad * factor, dec_bias_m, dec_bias_v, 0.0)
    dec_new = dec_new * lax.rsqrt(row_squares + 1e-12)[:, None]
    return (
        jnp.stack([loss_total, counted]),
        overall_derivative_length,
        fired,
        enc_new,
        enc_m,
        enc_v,
        bias_new,
        bias_m,
        bias_v,
        dec_new,
        dec_m,
        dec_v,
        out_new,
        out_m,
        out_v,
    )


def solution(mesh):
    return jax.shard_map(
        shards,
        mesh=mesh,
        in_specs=(
            P(("dp", "feat"), None),
            P("dp", None),
            P("dp"),
            P(),
            P(),
            P(),
            P(),
            P("dp", "feat"),
            P("feat"),
            P("feat", "dp"),
            P(),
            P("dp", "feat"),
            P("dp", "feat"),
            P("feat"),
            P("feat"),
            P("feat", "dp"),
            P("feat", "dp"),
            P(),
            P(),
        ),
        out_specs=(
            P(),
            P(),
            P("feat"),
            P("dp", "feat"),
            P("dp", "feat"),
            P("dp", "feat"),
            P("feat"),
            P("feat"),
            P("feat"),
            P("feat", "dp"),
            P("feat", "dp"),
            P("feat", "dp"),
            P(),
            P(),
            P(),
        ),
        check_vma=False,
    )
```

time: 877 us -> 525 us (0.60)
  matrix products: 246 us -> 0 us
  waiting for transfers between devices: 396 us -> 152 us
  Pallas kernels: 0 us -> 205 us
  blocking collectives: 144 us -> 0 us
  starting transfers between devices: 6.14 us -> 57.4 us
  local copies, waits for them, and re-layouts: 6.71 us -> 22.5 us
    dot_general x7 -> x0, matrix products: 235 us -> none  [the longest x1 60 us: shards(): encoded = jnp.dot(z_group, enc_full, preferred_element_type=jnp.float32)]
    pallas_call x0 -> x11, Pallas kernels: none -> 205 us  [the longest x5 102 us: backward(): pl.pallas_call(functools.partial(backward_kernel, counts, carried is not...]
    reduce_scatter x3 -> x0, waiting for transfers between devices: 196 us -> none  [the longest x1 161 us: shards(): lax.psum_scatter(jnp.dot(act_low, dec_full, preferred_element_type=jnp.fl...]
    all_gather x4 -> x2, waiting for transfers between devices: 195 us -> 0.01 us  [the longest x1 0.01 us: shards(): lax.all_gather(dec_weight.astype(BF16).T, 'dp', axis=0, tiled=True)]
    ppermute x1 -> x56, waiting for transfers between devices: 5.15 us -> 151 us  [the longest x31 79.9 us: swapped(): lax.ppermute(block, axis, [(i, i ^ bit) for i in range(lax.axis_size(axis...]
    psum x5 -> x0, blocking collectives: 144 us -> none  [the longest x1 42.8 us: shards(): lax.psum((jnp.sum(own_keep), jnp.sum(own_keep * jnp.sum(hidden_code_float...]
    ppermute x1 -> x56, starting transfers between devices: 5.85 us -> 57.3 us  [the longest x24 27.8 us: ring_shift(): return lax.ppermute(block, 'feat', route)]
    add x2 -> x31, other arithmetic: 0.01 us -> 13.6 us  [the longest x6 9.07 us: shards(): total = kept + swapped(sent, 'dp', 1)]
  transfers between devices with their start and end apart: 8 -> 58, of which waited for: 5 -> 27; matrix products, arithmetic and copies ran while one was open for 19% -> 10% of each run, Pallas kernels for 0% -> 30%
where the time goes in v1:
time: 525 us; the launch traced here: 517 us
  Pallas kernels  205 us (39%)
  waiting for transfers between devices  152 us (29%)
  starting transfers between devices  57.4 us (11%)
  other arithmetic  56 us (11%)
  between operations  24.2 us (5%)
  local copies, waits for them, and re-layouts  22.5 us (4%)
    pallas_call x5, Pallas kernels, backward(): pl.pallas_call(functools.partial(backward_kernel, counts, carried is not...  102 us
    pallas_call x5, Pallas kernels, encode(): pl.pallas_call(functools.partial(encode_kernel, len(pieces)), grid=(featu...  93.7 us
    ppermute x31, waiting for transfers between devices, swapped(): lax.ppermute(block, axis, [(i, i ^ bit) for i in range(lax.axis_size(axis...  79.9 us
    ppermute x24, waiting for transfers between devices, ring_shift(): return lax.ppermute(block, 'feat', route)  70.9 us
    ppermute x24, starting transfers between devices, ring_shift(): return lax.ppermute(block, 'feat', route)  27.8 us
    ppermute x31, starting transfers between devices, swapped(): lax.ppermute(block, axis, [(i, i ^ bit) for i in range(lax.axis_size(axis...  24.7 us
  transfers between devices with their start and end apart: 58, of which 27 were waited for; matrix products, arithmetic and copies ran while one was open for 10% of the time, Pallas kernels for 30%

profile of v1, /device:TPU:0, one launch (start us, length us, event | category | flops | bytes accessed | tf_op | source)
XLA Modules:
  0.0 516.8 jit_solution(880892511658266718)
XLA Ops:
  7.2 3.0 convert_bitcast_fusion
  12.5 4.9 collective-permute-start
  22.2 9.0 %attend.1.refs_0_.refs_1_ = bf16[512,768]{1,0:T(8,128)(2,1)} custom-call(bf16[512,768]{1,0:T(8,128)(2,1)} %own_ref.1, bf16[128,768]{1,0:T(8,128)(2,1)} %copy-done.61, s32[512,1]{1,0:T(8,128)} %copy.47.seg_q_ref, s32[1,640]{1,0:T(1,128)} %broadcast_in_dim.36.seg_k_ref, bf16[1,768]{1,0:T(2,128)(2,1)} %broadcast_in_dim.37.gain_ref, ...), custom_call_target="tpu_custom_call" | custom-call | flops 2415919104 | bytes 3538944 | tf_op jit(solution)/shard_map/attend/pallas_call | solution.py:86
  31.2 3.3 collective-permute-start.1
  34.5 16.6 %collective-permute-done.1.refs_0_.refs_4_ = bf16[512,768]{1,0:T(8,128)(2,1)S(1)} collective-permute-done((bf16[512,768]{1,0:T(8,128)(2,1)}, bf16[512,768]{1,0:T(8,128)(2,1)S(1)}, u32[]{:S(2)}, u32[]{:S(2)}) %collective-permute-start.1) | collective-permute-done | bytes 786464 | tf_op jit(solution)/shard_map/ppermute | solution.py:308
  51.0 2.2 collective-permute-start.2
  54.0 15.5 %collective-permute-done.2.refs_0_.refs_1_ = bf16[512,768]{1,0:T(8,128)(2,1)} collective-permute-done((bf16[512,768]{1,0:T(8,128)(2,1)S(1)}, bf16[512,768]{1,0:T(8,128)(2,1)}, u32[]{:S(2)}, u32[]{:S(2)}) %collective-permute-start.2) | collective-permute-done | bytes 786464 | tf_op jit(solution)/shard_map/ppermute | solution.py:308
  77.5 9.7 %collective-permute-done.3.refs_0_.refs_2_ = bf16[512,768]{1,0:T(8,128)(2,1)S(1)} collective-permute-done((bf16[512,768]{1,0:T(8,128)(2,1)}, bf16[512,768]{1,0:T(8,128)(2,1)S(1)}, u32[]{:S(2)}, u32[]{:S(2)}) %collective-permute-start.3) | collective-permute-done | bytes 786464 | tf_op jit(solution)/shard_map/ppermute | solution.py:308
  97.0 13.1 %encode.9 = (bf16[512,3072]{1,0:T(8,128)(2,1)}, bf16[256,768]{1,0:T(8,128)(2,1)}, bf16[256,768]{1,0:T(8,128)(2,1)}, f32[1,3072]{1,0:T(1,128)}, f32[1,3072]{1,0:T(1,128)}) custom-call(bf16[256,768]{1,0:T(8,128)(2,1)} %copy-done.12, bf16[256,768]{1,0:T(8,128)(2,1)} %copy-done.13, f32[512,1]{1,0:T(8,128)} %copy.52.refs_2_, ...), custom_call_target="tpu_custom_call" | custom-call | flops 4831838208 | bytes 15728640 | tf_op jit(solution)/shard_map/encode/pallas_call | solution.py:147
  110.1 2.1 collective-permute-start.9
  112.3 22.4 %encode.5 = (bf16[1024,3072]{1,0:T(8,128)(2,1)}, f32[512,768]{1,0:T(8,128)}, f32[512,768]{1,0:T(8,128)}, f32[1,3072]{1,0:T(1,128)}, f32[1,3072]{1,0:T(1,128)}) custom-call(bf16[512,768]{1,0:T(8,128)(2,1)} %copy-done.2, bf16[512,768]{1,0:T(8,128)(2,1)} %copy-done.3, f32[1024,1]{1,0:T(8,128)} %copy.48.refs_2_, ...), custom_call_target="tpu_custom_call" | custom-call | flops 9663676416 | bytes 22020096 | tf_op jit(solution)/shard_map/encode/pallas_call | solution.py:147
  138.7 1.9 collective-permute-start.10
  140.6 5.5 %collective-permute-done.13 = bf16[256,768]{1,0:T(8,128)(2,1)S(1)} collective-permute-done((bf16[256,768]{1,0:T(8,128)(2,1)S(1)}, bf16[256,768]{1,0:T(8,128)(2,1)S(1)}, u32[]{:S(2)}, u32[]{:S(2)}) %collective-permute-start.13) | collective-permute-done | bytes 393248 | tf_op jit(solution)/shard_map/ppermute | solution.py:308
  147.0 22.4 %encode.8 = (bf16[1024,3072]{1,0:T(8,128)(2,1)}, f32[512,768]{1,0:T(8,128)}, f32[512,768]{1,0:T(8,128)}, f32[1,3072]{1,0:T(1,128)}, f32[1,3072]{1,0:T(1,128)}) custom-call(bf16[512,768]{1,0:T(8,128)(2,1)} %collective-permute-done.2.refs_0_.refs_1_, bf16[512,768]{1,0:T(8,128)(2,1)} %collective-permute-done.5.refs_1_.refs_2_, f32[1024,1]{1,0:T(8,128)} %bitcast.84, ...), custom_call_target="tpu_custom_call" | custom-call | flops 9663676416 | bytes 22020096 | tf_op jit(solution)/shard_map/encode/pallas_call | solution.py:147
  173.5 22.4 %encode.7 = (bf16[1024,3072]{1,0:T(8,128)(2,1)}, f32[512,768]{1,0:T(8,128)}, f32[512,768]{1,0:T(8,128)}, f32[1,3072]{1,0:T(1,128)}, f32[1,3072]{1,0:T(1,128)}) custom-call(bf16[512,768]{1,0:T(8,128)(2,1)} %copy-done.56, bf16[512,768]{1,0:T(8,128)(2,1)} %copy-done.57, f32[1024,1]{1,0:T(8,128)} %copy.50.refs_2_, ...), custom_call_target="tpu_custom_call" | custom-call | flops 9663676416 | bytes 22020096 | tf_op jit(solution)/shard_map/encode/pallas_call | solution.py:147
  203.0 11.9 %collective-permute-done.19 = f32[2]{0:T(128)S(1)} collective-permute-done((f32[2]{0:T(128)S(1)}, f32[2]{0:T(128)S(1)}, u32[]{:S(2)}, u32[]{:S(2)}) %collective-permute-start.19) | collective-permute-done | bytes 40 | tf_op jit(solution)/shard_map/ppermute | solution.py:312
  214.9 3.5 collective-permute-done.20
  218.5 3.6 collective-permute-start.21
  226.2 13.4 %encode.6 = (bf16[512,3072]{1,0:T(8,128)(2,1)}, f32[512,768]{1,0:T(8,128)}, f32[1,3072]{1,0:T(1,128)}, f32[1,3072]{1,0:T(1,128)}) custom-call(bf16[512,768]{1,0:T(8,128)(2,1)} %attend.1.refs_0_.refs_1_, f32[512,1]{1,0:T(8,128)} %copy.49.refs_1_, bf16[768,3072]{1,0:T(8,128)(2,1)} %all-gather.3.cloned.1.call-done.refs_3_.refs_2_, f32[1,3072]{1,0:T(1,128)} %bitcast.104, ...), custom_call_target="tpu_custom_call" | custom-call | flops 4831838208 | bytes 15728640 | tf_op jit(solution)/shard_map/encode/pallas_call | solution.py:147
  240.5 2.1 fusion.6
  242.7 2.1 collective-permute-start.22
  248.0 3.4 multiply_reduce_fusion
  251.4 8.9 %collective-permute-done.22.refs_6_ = bf16[512,768]{1,0:T(8,128)(2,1)} collective-permute-done((bf16[512,768]{1,0:T(8,128)(2,1)S(1)}, bf16[512,768]{1,0:T(8,128)(2,1)}, u32[]{:S(2)}, u32[]{:S(2)}) %collective-permute-start.22) | collective-permute-done | bytes 786464 | tf_op jit(solution)/shard_map/ppermute | solution.py:308
  260.2 2.0 collective-permute-start.23
  263.6 14.5 %collective-permute-done.23.refs_3_ = bf16[512,768]{1,0:T(8,128)(2,1)S(1)} collective-permute-done((bf16[512,768]{1,0:T(8,128)(2,1)}, bf16[512,768]{1,0:T(8,128)(2,1)S(1)}, u32[]{:S(2)}, u32[]{:S(2)}) %collective-permute-start.23) | collective-permute-done | bytes 786464 | tf_op jit(solution)/shard_map/ppermute | solution.py:308
  278.2 2.0 collective-permute-start.24
  280.2 30.2 %backward.5 = (f32[768,3072]{1,0:T(8,128)}, f32[768,3072]{1,0:T(8,128)}, f32[1,3072]{1,0:T(1,128)}) custom-call(bf16[512,3072]{1,0:T(8,128)(2,1)} %get-tuple-element.72.refs_0_, bf16[512,768]{1,0:T(8,128)(2,1)} %attend.1.refs_0_.refs_1_, bf16[512,768]{1,0:T(8,128)(2,1)} %copy-done.29, bf16[1024,3072]{1,0:T(8,128)(2,1)} %get-tuple-element.73.refs_3_, ...), custom_call_target="tpu_custom_call" | custom-call | flops 21743271936 | bytes 47185920 | tf_op jit(solution)/shard_map/backward/pallas_call | solution.py:280
  310.5 1.8 collective-permute-start.28
  312.8 23.8 %backward.6 = (f32[768,3072]{1,0:T(8,128)}, f32[768,3072]{1,0:T(8,128)}, f32[1,3072]{1,0:T(1,128)}) custom-call(bf16[1024,3072]{1,0:T(8,128)(2,1)} %get-tuple-element.71.refs_0_, bf16[512,768]{1,0:T(8,128)(2,1)} %collective-permute-done.2.refs_0_.refs_1_, bf16[512,768]{1,0:T(8,128)(2,1)} %collective-permute-done.5.refs_1_.refs_2_, ...), custom_call_target="tpu_custom_call" | custom-call | flops 14495514624 | bytes 44040192 | tf_op jit(solution)/shard_map/backward/pallas_call | solution.py:280
  337.6 16.0 %backward.7 = (f32[2,192,1024]{2,1,0:T(8,128)}, f32[2,192,1024]{2,1,0:T(8,128)}, f32[2,192,1024]{2,1,0:T(8,128)}, f32[2,192,1024]{2,1,0:T(8,128)}, f32[1,1024]{1,0:T(1,128)}) custom-call(s32[1]{0:T(128)} %bitcast.refs_0_, bf16[1024,3072]{1,0:T(8,128)(2,1)} %get-tuple-element.60.refs_1_, bf16[512,768]{1,0:T(8,128)(2,1)} %copy-done.2, ...), custom_call_target="tpu_custom_call" | custom-call | flops 7247757312 | bytes 15728640 | tf_op jit(solution)/shard_map/backward/pallas_call | solution.py:280
  353.5 16.2 %backward.8 = (f32[2,192,1024]{2,1,0:T(8,128)}, f32[2,192,1024]{2,1,0:T(8,128)}, f32[2,192,1024]{2,1,0:T(8,128)}, f32[2,192,1024]{2,1,0:T(8,128)}, f32[1,1024]{1,0:T(1,128)}) custom-call(s32[1]{0:T(128)} %bitcast.refs_0_, bf16[1024,3072]{1,0:T(8,128)(2,1)} %get-tuple-element.60.refs_1_, bf16[512,768]{1,0:T(8,128)(2,1)} %copy-done.2, ...), custom_call_target="tpu_custom_call" | custom-call | flops 7247757312 | bytes 15728640 | tf_op jit(solution)/shard_map/backward/pallas_call | solution.py:280
  369.8 16.2 %backward.9 = (f32[2,192,1024]{2,1,0:T(8,128)}, f32[2,192,1024]{2,1,0:T(8,128)}, f32[2,192,1024]{2,1,0:T(8,128)}, f32[2,192,1024]{2,1,0:T(8,128)}, f32[1,1024]{1,0:T(1,128)}) custom-call(s32[1]{0:T(128)} %bitcast.refs_0_, bf16[1024,3072]{1,0:T(8,128)(2,1)} %get-tuple-element.60.refs_1_, bf16[512,768]{1,0:T(8,128)(2,1)} %copy-done.2, ...), custom_call_target="tpu_custom_call" | custom-call | flops 7247757312 | bytes 15728640 | tf_op jit(solution)/shard_map/backward/pallas_call | solution.py:280
  389.6 3.6 collective-permute-done.45
  394.7 2.1 collective-permute-done.46
  400.4 2.9 collective-permute-start.48
  413.8 2.1 collective-permute-start.39
  419.7 2.1 collective-permute-start.31
  426.1 23.1 %collective-permute-done.31 = bf16[192,1024]{1,0:T(8,128)(2,1)S(1)} collective-permute-done((bf16[192,1024]{1,0:T(8,128)(2,1)S(1)}, bf16[192,1024]{1,0:T(8,128)(2,1)S(1)}, u32[]{:S(2)}, u32[]{:S(2)}) %collective-permute-start.31) | collective-permute-done | bytes 393248 | tf_op jit(solution)/shard_map/ppermute | solution.py:312
  449.3 8.3 %collective-permute-done.33 = bf16[192,1024]{1,0:T(8,128)(2,1)S(1)} collective-permute-done((bf16[192,1024]{1,0:T(8,128)(2,1)S(1)}, bf16[192,1024]{1,0:T(8,128)(2,1)S(1)}, u32[]{:S(2)}, u32[]{:S(2)}) %collective-permute-start.33) | collective-permute-done | bytes 393248 | tf_op jit(solution)/shard_map/ppermute | solution.py:312
  457.7 7.4 %collective-permute-done.35 = bf16[192,1024]{1,0:T(8,128)(2,1)S(1)} collective-permute-done((bf16[192,1024]{1,0:T(8,128)(2,1)S(1)}, bf16[192,1024]{1,0:T(8,128)(2,1)S(1)}, u32[]{:S(2)}, u32[]{:S(2)}) %collective-permute-start.35) | collective-permute-done | bytes 393248 | tf_op jit(solution)/shard_map/ppermute | solution.py:312
  468.1 2.6 multiply_reduce_fusion.2
  473.6 3.3 collective-permute-done.50
  477.1 3.3 collective-permute-done.51
  482.2 1.8 collective-permute-done.52
  485.7 2.8 collective-permute-done.53
  490.4 7.4 %multiply_reduce_fusion.1 = (f32[3072]{0:T(1024)S(1)}, f32[3072,192]{0,1:T(8,128)S(1)}, f32[3072,192]{0,1:T(8,128)}, f32[3072,192]{0,1:T(8,128)}) fusion(f32[3072,192]{0,1:T(8,128)S(1)} %copy-done.1, f32[3072,192]{0,1:T(8,128)} %get-tuple-element.123, f32[]{:T(128)S(6)} %min_shard_map.3, f32[3072,192]{0,1:T(8,128)} %param.36, f32[3072,192]{0,1:T(8,128)} %param.37), kind=kLoop, calls=%fused_computation.11 | loop fusion | flops 10613760 | bytes 16527364 | tf_op jit(solution)/shard_map/reduce_sum | solution.py:488
  498.0 3.6 multiply_subtract_fusion.1
  503.2 1.9 pad_maximum_fusion.8
  (316 shorter events, 89.0 us)
Async XLA Ops:
  7.2 89.1 %all-gather.5.cloned.1.call-start = ((), (), s32[]{:S(2)}) async-start(), calls=%async_computation.1 | async-start | bytes 5898240 | tf_op jit(solution)/shard_map/all_gather | solution.py:377
  10.3 86.0 %all-gather.3.cloned.1.call-start = ((), (), s32[]{:S(2)}) async-start(), calls=%async_computation | async-start | bytes 5898240 | tf_op jit(solution)/shard_map/all_gather | solution.py:376
  12.5 9.0 %collective-permute-start = (bf16[128,768]{1,0:T(8,128)(2,1)S(1)}, bf16[128,768]{1,0:T(8,128)(2,1)S(1)}, u32[]{:S(2)}, u32[]{:S(2)}) collective-permute-start(bf16[128,768]{1,0:T(8,128)(2,1)S(1)} %slice.101), channel_id=1, source_target_pairs={{0,1},{1,2},{2,3},{3,4},{4,5},{5,6},{6,7},{8,9},{9,10},{10,11},{11... | collective-permute-start | bytes 589832 | tf_op jit(solution)/shard_map/ppermute | solution.py:375
  31.2 19.8 %collective-permute-start.1 = (bf16[512,768]{1,0:T(8,128)(2,1)}, bf16[512,768]{1,0:T(8,128)(2,1)S(1)}, u32[]{:S(2)}, u32[]{:S(2)}) collective-permute-start(bf16[512,768]{1,0:T(8,128)(2,1)} %attend.1.refs_0_.refs_1_), channel_id=1, source_target_pairs={{0,2},{2,4},{4,6},{6,7},{7,5},{5,3},{3,1},{1,0},{8,10},{10,12},{12... | collective-permute-start | bytes 2359304 | tf_op jit(solution)/shard_map/ppermute | solution.py:308
  34.5 18.7 %collective-permute-start.4 = (bf16[512,768]{1,0:T(8,128)(2,1)}, bf16[512,768]{1,0:T(8,128)(2,1)S(1)}, u32[]{:S(2)}, u32[]{:S(2)}) collective-permute-start(bf16[512,768]{1,0:T(8,128)(2,1)} %attend.1.refs_0_.refs_1_), channel_id=1, source_target_pairs={{0,1},{2,0},{4,2},{6,4},{7,6},{5,7},{3,5},{1,3},{8,9},{10,8},{12,1... | collective-permute-start | bytes 2359304 | tf_op jit(solution)/shard_map/ppermute | solution.py:308
  51.0 18.4 %collective-permute-start.2 = (bf16[512,768]{1,0:T(8,128)(2,1)S(1)}, bf16[512,768]{1,0:T(8,128)(2,1)}, u32[]{:S(2)}, u32[]{:S(2)}) collective-permute-start(bf16[512,768]{1,0:T(8,128)(2,1)S(1)} %collective-permute-done.1.refs_0_.refs_4_), channel_id=1, source_target_pairs={{0,2},{2,4},{4,6},{6,7},{7,5},{5,3},{3,1},{1,0},{8,10},{10,12},{12... | collective-permute-start | bytes 2359304 | tf_op jit(solution)/shard_map/ppermute | solution.py:308
  53.2 17.7 %collective-permute-start.5 = (bf16[512,768]{1,0:T(8,128)(2,1)S(1)}, bf16[512,768]{1,0:T(8,128)(2,1)}, u32[]{:S(2)}, u32[]{:S(2)}) collective-permute-start(bf16[512,768]{1,0:T(8,128)(2,1)S(1)} %collective-permute-done.4.refs_1_.refs_5_), channel_id=1, source_target_pairs={{0,1},{2,0},{4,2},{6,4},{7,6},{5,7},{3,5},{1,3},{8,9},{10,8},{12,1... | collective-permute-start | bytes 2359304 | tf_op jit(solution)/shard_map/ppermute | solution.py:308
  69.5 17.7 %collective-permute-start.3 = (bf16[512,768]{1,0:T(8,128)(2,1)}, bf16[512,768]{1,0:T(8,128)(2,1)S(1)}, u32[]{:S(2)}, u32[]{:S(2)}) collective-permute-start(bf16[512,768]{1,0:T(8,128)(2,1)} %collective-permute-done.2.refs_0_.refs_1_), channel_id=1, source_target_pairs={{0,2},{2,4},{4,6},{6,7},{7,5},{5,3},{3,1},{1,0},{8,10},{10,12},{12... | collective-permute-start | bytes 2359304 | tf_op jit(solution)/shard_map/ppermute | solution.py:308
  70.9 17.5 %collective-permute-start.6 = (bf16[512,768]{1,0:T(8,128)(2,1)}, bf16[512,768]{1,0:T(8,128)(2,1)S(1)}, u32[]{:S(2)}, u32[]{:S(2)}) collective-permute-start(bf16[512,768]{1,0:T(8,128)(2,1)} %collective-permute-done.5.refs_1_.refs_2_), channel_id=1, source_target_pairs={{0,1},{2,0},{4,2},{6,4},{7,6},{5,7},{3,5},{1,3},{8,9},{10,8},{12,1... | collective-permute-start | bytes 2359304 | tf_op jit(solution)/shard_map/ppermute | solution.py:308
  87.2 8.8 %collective-permute-start.7 = (bf16[256,768]{1,0:T(8,128)(2,1)S(1)}, bf16[256,768]{1,0:T(8,128)(2,1)S(1)}, u32[]{:S(2)}, u32[]{:S(2)}) collective-permute-start(bf16[256,768]{1,0:T(8,128)(2,1)S(1)} %slice.141), channel_id=1, source_target_pairs={{0,2},{2,4},{4,6},{6,7},{7,5},{5,3},{3,1},{1,0},{8,10},{10,12},{12... | collective-permute-start | bytes 1179656 | tf_op jit(solution)/shard_map/ppermute | solution.py:308
  88.4 7.8 %collective-permute-start.8 = (bf16[256,768]{1,0:T(8,128)(2,1)S(1)}, bf16[256,768]{1,0:T(8,128)(2,1)S(1)}, u32[]{:S(2)}, u32[]{:S(2)}) collective-permute-start(bf16[256,768]{1,0:T(8,128)(2,1)S(1)} %slice.142), channel_id=1, source_target_pairs={{0,1},{2,0},{4,2},{6,4},{7,6},{5,7},{3,5},{1,3},{8,9},{10,8},{12,1... | collective-permute-start | bytes 1179656 | tf_op jit(solution)/shard_map/ppermute | solution.py:308
  94.5 105.8 %collective-permute-start.18 = (f32[2]{0:T(128)S(1)}, f32[2]{0:T(128)S(1)}, u32[]{:S(2)}, u32[]{:S(2)}) collective-permute-start(f32[2]{0:T(128)S(1)} %fusion.38), channel_id=1, source_target_pairs={{0,16},{8,24},{16,0},{24,8},{1,17},{9,25},{17,1},{25,9},{2,18},{10... | collective-permute-start | bytes 32 | tf_op jit(solution)/shard_map/ppermute | solution.py:312
  110.1 27.3 %collective-permute-start.9 = (bf16[256,768]{1,0:T(8,128)(2,1)}, bf16[256,768]{1,0:T(8,128)(2,1)S(1)}, u32[]{:S(2)}, u32[]{:S(2)}) collective-permute-start(bf16[256,768]{1,0:T(8,128)(2,1)} %get-tuple-element.65), channel_id=1, source_target_pairs={{0,2},{2,4},{4,6},{6,7},{7,5},{5,3},{3,1},{1,0},{8,10},{10,12},{12... | collective-permute-start | bytes 1179656 | tf_op jit(solution)/shard_map/ppermute | solution.py:308
  136.0 10.0 %collective-permute-start.13 = (bf16[256,768]{1,0:T(8,128)(2,1)S(1)}, bf16[256,768]{1,0:T(8,128)(2,1)S(1)}, u32[]{:S(2)}, u32[]{:S(2)}) collective-permute-start(bf16[256,768]{1,0:T(8,128)(2,1)S(1)} %copy-done.60), channel_id=1, source_target_pairs={{0,1},{2,0},{4,2},{6,4},{7,6},{5,7},{3,5},{1,3},{8,9},{10,8},{12,1... | collective-permute-start | bytes 1179656 | tf_op jit(solution)/shard_map/ppermute | solution.py:308
  138.7 30.7 %collective-permute-start.10 = (bf16[512,768]{1,0:T(8,128)(2,1)S(1)}, bf16[512,768]{1,0:T(8,128)(2,1)S(1)}, u32[]{:S(2)}, u32[]{:S(2)}) collective-permute-start(bf16[512,768]{1,0:T(8,128)(2,1)S(1)} %pad_maximum_fusion.1), channel_id=1, source_target_pairs={{0,2},{2,4},{4,6},{6,7},{7,5},{5,3},{3,1},{1,0},{8,10},{10,12},{12... | collective-permute-start | bytes 2359304 | tf_op jit(solution)/shard_map/ppermute | solution.py:308
  146.2 26.2 %collective-permute-start.14 = (bf16[512,768]{1,0:T(8,128)(2,1)S(1)}, bf16[512,768]{1,0:T(8,128)(2,1)S(1)}, u32[]{:S(2)}, u32[]{:S(2)}) collective-permute-start(bf16[512,768]{1,0:T(8,128)(2,1)S(1)} %pad_maximum_fusion.2), channel_id=1, source_target_pairs={{0,1},{2,0},{4,2},{6,4},{7,6},{5,7},{3,5},{1,3},{8,9},{10,8},{12,1... | collective-permute-start | bytes 2359304 | tf_op jit(solution)/shard_map/ppermute | solution.py:308
  171.1 24.8 %collective-permute-start.11 = (bf16[512,768]{1,0:T(8,128)(2,1)S(1)}, bf16[512,768]{1,0:T(8,128)(2,1)S(1)}, u32[]{:S(2)}, u32[]{:S(2)}) collective-permute-start(bf16[512,768]{1,0:T(8,128)(2,1)S(1)} %add_convert_fusion.3), channel_id=1, source_target_pairs={{0,2},{2,4},{4,6},{6,7},{7,5},{5,3},{3,1},{1,0},{8,10},{10,12},{12... | collective-permute-start | bytes 2359304 | tf_op jit(solution)/shard_map/ppermute | solution.py:308
  172.7 26.3 %collective-permute-start.15 = (bf16[512,768]{1,0:T(8,128)(2,1)S(1)}, bf16[512,768]{1,0:T(8,128)(2,1)S(1)}, u32[]{:S(2)}, u32[]{:S(2)}) collective-permute-start(bf16[512,768]{1,0:T(8,128)(2,1)S(1)} %add_convert_fusion.1), channel_id=1, source_target_pairs={{0,1},{2,0},{4,2},{6,4},{7,6},{5,7},{3,5},{1,3},{8,9},{10,8},{12,1... | collective-permute-start | bytes 2359304 | tf_op jit(solution)/shard_map/ppermute | solution.py:308
  197.6 42.0 %collective-permute-start.12 = (bf16[512,768]{1,0:T(8,128)(2,1)S(1)}, bf16[512,768]{1,0:T(8,128)(2,1)S(1)}, u32[]{:S(2)}, u32[]{:S(2)}) collective-permute-start(bf16[512,768]{1,0:T(8,128)(2,1)S(1)} %add_convert_fusion.2), channel_id=1, source_target_pairs={{0,2},{2,4},{4,6},{6,7},{7,5},{5,3},{3,1},{1,0},{8,10},{10,12},{12... | collective-permute-start | bytes 2359304 | tf_op jit(solution)/shard_map/ppermute | solution.py:308
  199.1 40.5 %collective-permute-start.16 = (bf16[512,768]{1,0:T(8,128)(2,1)S(1)}, bf16[512,768]{1,0:T(8,128)(2,1)S(1)}, u32[]{:S(2)}, u32[]{:S(2)}) collective-permute-start(bf16[512,768]{1,0:T(8,128)(2,1)S(1)} %add_convert_fusion), channel_id=1, source_target_pairs={{0,1},{2,0},{4,2},{6,4},{7,6},{5,7},{3,5},{1,3},{8,9},{10,8},{12,1... | collective-permute-start | bytes 2359304 | tf_op jit(solution)/shard_map/ppermute | solution.py:308
  201.7 13.2 %collective-permute-start.19 = (f32[2]{0:T(128)S(1)}, f32[2]{0:T(128)S(1)}, u32[]{:S(2)}, u32[]{:S(2)}) collective-permute-start(f32[2]{0:T(128)S(1)} %fusion.40), channel_id=1, source_target_pairs={{0,1},{1,0},{2,3},{3,2},{4,5},{5,4},{6,7},{7,6},{8,9},{9,8},{10,11... | collective-permute-start | bytes 32 | tf_op jit(solution)/shard_map/ppermute | solution.py:312
  218.5 5.1 collective-permute-start.21
  242.7 17.5 %collective-permute-start.22 = (bf16[512,768]{1,0:T(8,128)(2,1)S(1)}, bf16[512,768]{1,0:T(8,128)(2,1)}, u32[]{:S(2)}, u32[]{:S(2)}) collective-permute-start(bf16[512,768]{1,0:T(8,128)(2,1)S(1)} %get-tuple-element.124.refs_2_), channel_id=1, source_target_pairs={{0,2},{2,4},{4,6},{6,7},{7,5},{5,3},{3,1},{1,0},{8,10},{10,12},{12... | collective-permute-start | bytes 2359304 | tf_op jit(solution)/shard_map/ppermute | solution.py:308
  244.8 17.5 %collective-permute-start.25 = (bf16[512,768]{1,0:T(8,128)(2,1)S(1)}, bf16[512,768]{1,0:T(8,128)(2,1)}, u32[]{:S(2)}, u32[]{:S(2)}) collective-permute-start(bf16[512,768]{1,0:T(8,128)(2,1)S(1)} %get-tuple-element.124.refs_2_), channel_id=1, source_target_pairs={{0,1},{2,0},{4,2},{6,4},{7,6},{5,7},{3,5},{1,3},{8,9},{10,8},{12,1... | collective-permute-start | bytes 2359304 | tf_op jit(solution)/shard_map/ppermute | solution.py:308
  260.2 17.9 %collective-permute-start.23 = (bf16[512,768]{1,0:T(8,128)(2,1)}, bf16[512,768]{1,0:T(8,128)(2,1)S(1)}, u32[]{:S(2)}, u32[]{:S(2)}) collective-permute-start(bf16[512,768]{1,0:T(8,128)(2,1)} %collective-permute-done.22.refs_6_), channel_id=1, source_target_pairs={{0,2},{2,4},{4,6},{6,7},{7,5},{5,3},{3,1},{1,0},{8,10},{10,12},{12... | collective-permute-start | bytes 2359304 | tf_op jit(solution)/shard_map/ppermute | solution.py:308
  262.3 17.9 %collective-permute-start.26 = (bf16[512,768]{1,0:T(8,128)(2,1)}, bf16[512,768]{1,0:T(8,128)(2,1)S(1)}, u32[]{:S(2)}, u32[]{:S(2)}) collective-permute-start(bf16[512,768]{1,0:T(8,128)(2,1)} %collective-permute-done.25.refs_7_), channel_id=1, source_target_pairs={{0,1},{2,0},{4,2},{6,4},{7,6},{5,7},{3,5},{1,3},{8,9},{10,8},{12,1... | collective-permute-start | bytes 2359304 | tf_op jit(solution)/shard_map/ppermute | solution.py:308
  278.2 32.3 %collective-permute-start.24 = (bf16[512,768]{1,0:T(8,128)(2,1)S(1)}, bf16[512,768]{1,0:T(8,128)(2,1)S(1)}, u32[]{:S(2)}, u32[]{:S(2)}) collective-permute-start(bf16[512,768]{1,0:T(8,128)(2,1)S(1)} %collective-permute-done.23.refs_3_), channel_id=1, source_target_pairs={{0,2},{2,4},{4,6},{6,7},{7,5},{5,3},{3,1},{1,0},{8,10},{10,12},{12... | collective-permute-start | bytes 2359304 | tf_op jit(solution)/shard_map/ppermute | solution.py:308
  280.2 32.1 %collective-permute-start.27 = (bf16[512,768]{1,0:T(8,128)(2,1)S(1)}, bf16[512,768]{1,0:T(8,128)(2,1)S(1)}, u32[]{:S(2)}, u32[]{:S(2)}) collective-permute-start(bf16[512,768]{1,0:T(8,128)(2,1)S(1)} %collective-permute-done.26.refs_4_), channel_id=1, source_target_pairs={{0,1},{2,0},{4,2},{6,4},{7,6},{5,7},{3,5},{1,3},{8,9},{10,8},{12,1... | collective-permute-start | bytes 2359304 | tf_op jit(solution)/shard_map/ppermute | solution.py:308
  310.5 26.2 %collective-permute-start.28 = (bf16[256,768]{1,0:T(8,128)(2,1)S(1)}, bf16[256,768]{1,0:T(8,128)(2,1)S(1)}, u32[]{:S(2)}, u32[]{:S(2)}) collective-permute-start(bf16[256,768]{1,0:T(8,128)(2,1)S(1)} %slice.146), channel_id=1, source_target_pairs={{0,2},{2,4},{4,6},{6,7},{7,5},{5,3},{3,1},{1,0},{8,10},{10,12},{12... | collective-permute-start | bytes 1179656 | tf_op jit(solution)/shard_map/ppermute | solution.py:308
  312.3 24.4 %collective-permute-start.29 = (bf16[256,768]{1,0:T(8,128)(2,1)S(1)}, bf16[256,768]{1,0:T(8,128)(2,1)S(1)}, u32[]{:S(2)}, u32[]{:S(2)}) collective-permute-start(bf16[256,768]{1,0:T(8,128)(2,1)S(1)} %slice.147), channel_id=1, source_target_pairs={{0,1},{2,0},{4,2},{6,4},{7,6},{5,7},{3,5},{1,3},{8,9},{10,8},{12,1... | collective-permute-start | bytes 1179656 | tf_op jit(solution)/shard_map/ppermute | solution.py:308
  386.9 16.9 %collective-permute-start.42 = (f32[3,3072]{1,0:T(4,128)S(1)}, f32[3,3072]{1,0:T(4,128)S(1)}, u32[]{:S(2)}, u32[]{:S(2)}) collective-permute-start(f32[3,3072]{1,0:T(4,128)S(1)} %pad_maximum_fusion.3), channel_id=1, source_target_pairs={{0,8},{8,0},{16,24},{24,16},{1,9},{9,1},{17,25},{25,17},{2,10},{10... | collective-permute-start | bytes 110600 | tf_op jit(solution)/shard_map/ppermute | solution.py:312
  400.4 4.5 collective-permute-start.48
  403.3 4.8 collective-permute-start.36
  403.3 8.5 %collective-permute-start.38 = (f32[2,192,1024]{2,1,0:T(8,128)}, f32[2,192,1024]{2,1,0:T(8,128)}, u32[]{:S(2)}, u32[]{:S(2)}) collective-permute-start(f32[2,192,1024]{2,1,0:T(8,128)} %get-tuple-element.87), channel_id=1, source_target_pairs={{0,8},{8,0},{16,24},{24,16},{1,9},{9,1},{17,25},{25,17},{2,10},{10... | collective-permute-start | bytes 4718600 | tf_op jit(solution)/shard_map/ppermute | solution.py:312
  403.9 4.2 collective-permute-start.43
  406.2 7.6 %collective-permute-start.40 = (f32[2,192,1024]{2,1,0:T(8,128)}, f32[2,192,1024]{2,1,0:T(8,128)}, u32[]{:S(2)}, u32[]{:S(2)}) collective-permute-start(f32[2,192,1024]{2,1,0:T(8,128)} %get-tuple-element.89), channel_id=1, source_target_pairs={{0,8},{8,0},{16,24},{24,16},{1,9},{9,1},{17,25},{25,17},{2,10},{10... | collective-permute-start | bytes 4718600 | tf_op jit(solution)/shard_map/ppermute | solution.py:312
  406.3 11.5 %collective-permute-start.30 = (f32[2,192,1024]{2,1,0:T(8,128)}, f32[2,192,1024]{2,1,0:T(8,128)}, u32[]{:S(2)}, u32[]{:S(2)}) collective-permute-start(f32[2,192,1024]{2,1,0:T(8,128)} %get-tuple-element.79), channel_id=1, source_target_pairs={{0,8},{8,0},{16,24},{24,16},{1,9},{9,1},{17,25},{25,17},{2,10},{10... | collective-permute-start | bytes 4718600 | tf_op jit(solution)/shard_map/ppermute | solution.py:312
  408.1 11.6 %collective-permute-start.32 = (f32[2,192,1024]{2,1,0:T(8,128)}, f32[2,192,1024]{2,1,0:T(8,128)S(1)}, u32[]{:S(2)}, u32[]{:S(2)}) collective-permute-start(f32[2,192,1024]{2,1,0:T(8,128)} %get-tuple-element.81), channel_id=1, source_target_pairs={{0,8},{8,0},{16,24},{24,16},{1,9},{9,1},{17,25},{25,17},{2,10},{10... | collective-permute-start | bytes 4718600 | tf_op jit(solution)/shard_map/ppermute | solution.py:312
  408.1 14.0 %collective-permute-start.34 = (f32[2,192,1024]{2,1,0:T(8,128)}, f32[2,192,1024]{2,1,0:T(8,128)}, u32[]{:S(2)}, u32[]{:S(2)}) collective-permute-start(f32[2,192,1024]{2,1,0:T(8,128)} %get-tuple-element.83), channel_id=1, source_target_pairs={{0,8},{8,0},{16,24},{24,16},{1,9},{9,1},{17,25},{25,17},{2,10},{10... | collective-permute-start | bytes 4718600 | tf_op jit(solution)/shard_map/ppermute | solution.py:312
  411.9 13.0 %collective-permute-start.37 = (bf16[192,1024]{1,0:T(8,128)(2,1)S(1)}, bf16[192,1024]{1,0:T(8,128)(2,1)S(1)}, u32[]{:S(2)}, u32[]{:S(2)}) collective-permute-start(bf16[192,1024]{1,0:T(8,128)(2,1)S(1)} %fusion.16), channel_id=1, source_target_pairs={{0,16},{8,24},{16,0},{24,8},{1,17},{9,25},{17,1},{25,9},{2,18},{10... | collective-permute-start | bytes 1179656 | tf_op jit(solution)/shard_map/ppermute | solution.py:312
  413.8 52.6 %collective-permute-start.39 = (bf16[192,1024]{1,0:T(8,128)(2,1)S(1)}, bf16[192,1024]{1,0:T(8,128)(2,1)S(1)}, u32[]{:S(2)}, u32[]{:S(2)}) collective-permute-start(bf16[192,1024]{1,0:T(8,128)(2,1)S(1)} %fusion.17), channel_id=1, source_target_pairs={{0,16},{8,24},{16,0},{24,8},{1,17},{9,25},{17,1},{25,9},{2,18},{10... | collective-permute-start | bytes 1179656 | tf_op jit(solution)/shard_map/ppermute | solution.py:312
  417.7 48.8 %collective-permute-start.41 = (bf16[192,1024]{1,0:T(8,128)(2,1)S(1)}, bf16[192,1024]{1,0:T(8,128)(2,1)S(1)}, u32[]{:S(2)}, u32[]{:S(2)}) collective-permute-start(bf16[192,1024]{1,0:T(8,128)(2,1)S(1)} %fusion.18), channel_id=1, source_target_pairs={{0,16},{8,24},{16,0},{24,8},{1,17},{9,25},{17,1},{25,9},{2,18},{10... | collective-permute-start | bytes 1179656 | tf_op jit(solution)/shard_map/ppermute | solution.py:312
  419.7 29.5 %collective-permute-start.31 = (bf16[192,1024]{1,0:T(8,128)(2,1)S(1)}, bf16[192,1024]{1,0:T(8,128)(2,1)S(1)}, u32[]{:S(2)}, u32[]{:S(2)}) collective-permute-start(bf16[192,1024]{1,0:T(8,128)(2,1)S(1)} %fusion.13), channel_id=1, source_target_pairs={{0,16},{8,24},{16,0},{24,8},{1,17},{9,25},{17,1},{25,9},{2,18},{10... | collective-permute-start | bytes 1179656 | tf_op jit(solution)/shard_map/ppermute | solution.py:312
  422.1 35.5 %collective-permute-start.33 = (bf16[192,1024]{1,0:T(8,128)(2,1)S(1)}, bf16[192,1024]{1,0:T(8,128)(2,1)S(1)}, u32[]{:S(2)}, u32[]{:S(2)}) collective-permute-start(bf16[192,1024]{1,0:T(8,128)(2,1)S(1)} %fusion.14), channel_id=1, source_target_pairs={{0,16},{8,24},{16,0},{24,8},{1,17},{9,25},{17,1},{25,9},{2,18},{10... | collective-permute-start | bytes 1179656 | tf_op jit(solution)/shard_map/ppermute | solution.py:312
  424.9 40.2 %collective-permute-start.35 = (bf16[192,1024]{1,0:T(8,128)(2,1)S(1)}, bf16[192,1024]{1,0:T(8,128)(2,1)S(1)}, u32[]{:S(2)}, u32[]{:S(2)}) collective-permute-start(bf16[192,1024]{1,0:T(8,128)(2,1)S(1)} %fusion.15), channel_id=1, source_target_pairs={{0,16},{8,24},{16,0},{24,8},{1,17},{9,25},{17,1},{25,9},{2,18},{10... | collective-permute-start | bytes 1179656 | tf_op jit(solution)/shard_map/ppermute | solution.py:312
  484.0 4.4 collective-permute-start.53
  497.8 5.0 collective-permute-start.54
  502.8 3.8 collective-permute-start.55
  (73 other events, 808.8 us)
Sparse Core Ops, SparseCore 0:
  10.4 40.1 all-gather.4
  52.7 37.4 all-gather.2

commit v2 on v1

v2 whole, which is shorter than its diff:
```python
import functools
import math

import jax
import jax.numpy as jnp
from jax import lax
from jax.experimental import pallas as pl
from jax.experimental.pallas import tpu as pltpu
from jax.sharding import PartitionSpec as P

HEAD = 64
ROW_LEN = 1024
CTX = 128
STEP = 10

LAMBDA = 0.001
CLIP_NORM = 0.004
LEARN = 0.02
BETA_ONE = 0.9
BETA_TWO = 0.999
EPSILON = 1e-08
DECAY = 0.01

ENCODE_BLOCK = 768
BACKWARD_BLOCK = 512
ROW_BLOCK = 512
LANES = 128
ENCODE_VMEM = 56
BACKWARD_VMEM = 56
LAST_PARTS = 3
PACK_BLOCK = 768
COST_SHARE = 4
BF16 = jnp.bfloat16
F32 = jnp.float32


def kernel_params(mebibytes):
    return pltpu.CompilerParams(vmem_limit_bytes=mebibytes * 2**20)


def dot_nn(a, b):
    return jnp.dot(a, b, preferred_element_type=F32)


def dot_nt(a, b):
    return lax.dot_general(a, b, (((1,), (1,)), ((), ())), preferred_element_type=F32)


def dot_tn(a, b):
    return lax.dot_general(a, b, (((0,), (0,)), ((), ())), preferred_element_type=F32)


def together(*values):
    leaves, tree = jax.tree.flatten(values)
    return jax.tree.unflatten(tree, lax.optimization_barrier(tuple(leaves)))


def attend_kernel(own_ref, tail_ref, seg_q_ref, seg_k_ref, gain_ref, bias_ref, w_ref, wb_ref, z_ref, q_s, kv_s):
    rows, width = own_ref.shape
    gain = gain_ref[...].astype(F32).reshape(1, width)
    shift = bias_ref[...].astype(F32).reshape(1, width)
    offsets = wb_ref[...].astype(F32).reshape(1, 3 * width)

    def normed(block):
        values = block.astype(F32)
        centred = values - jnp.mean(values, axis=1, keepdims=True)
        variance = jnp.mean(centred * centred, axis=1, keepdims=True)
        return (centred * lax.rsqrt(variance + 1e-05) * gain + shift).astype(BF16)

    own = normed(own_ref[...])
    q_s[...] = (dot_nn(own, w_ref[:, :width]) + offsets[:, :width]).astype(BF16)
    kv_s[CTX:, :] = (dot_nn(own, w_ref[:, width:]) + offsets[:, width:]).astype(BF16)
    tail = normed(tail_ref[...])
    kv_s[:CTX, :] = (dot_nn(tail, w_ref[:, width:]) + offsets[:, width:]).astype(BF16)

    lane = lax.broadcasted_iota(jnp.int32, (CTX, 2 * HEAD), 1)
    first_head = lane < HEAD
    place_q = lax.broadcasted_iota(jnp.int32, (CTX, 2 * CTX), 0) + CTX
    place_k = lax.broadcasted_iota(jnp.int32, (CTX, 2 * CTX), 1)
    earlier = place_k <= place_q
    for block in range(rows // CTX):
        base = block * CTX
        seg_q = seg_q_ref[base : base + CTX, :]
        allowed = (jnp.concatenate([seg_q, seg_q], axis=1) == seg_k_ref[:, base : base + 2 * CTX]) & earlier
        for pair in range(width // (2 * HEAD)):
            columns = slice(pair * 2 * HEAD, (pair + 1) * 2 * HEAD)
            query = q_s[base : base + CTX, columns]
            keys = kv_s[base : base + 2 * CTX, columns]
            values = kv_s[base : base + 2 * CTX, width + pair * 2 * HEAD : width + (pair + 1) * 2 * HEAD]
            mixed = []
            for half in range(2):
                mine = first_head if half == 0 else ~first_head
                part = jnp.where(mine, query, jnp.zeros_like(query))
                scores = dot_nt(part, keys) * (1.0 / math.sqrt(HEAD))
                scores = jnp.where(allowed, scores, -1e30)
                expo = jnp.exp(scores - jnp.max(scores, axis=1, keepdims=True))
                probs = (expo / jnp.sum(expo, axis=1, keepdims=True)).astype(BF16)
                mixed.append(dot_nn(probs, values))
            z_ref[base : base + CTX, columns] = jnp.where(first_head, mixed[0], mixed[1]).astype(BF16)


def attend(resid, tail, seg_q, seg_k, ln_gain, ln_bias, qkv_weight, qkv_bias):
    rows, width = resid.shape
    return pl.pallas_call(
        attend_kernel,
        out_shape=jax.ShapeDtypeStruct((rows, width), BF16),
        scratch_shapes=[
            pltpu.VMEM((rows, width), BF16),
            pltpu.VMEM((rows + CTX, 2 * width), BF16),
        ],
        compiler_params=kernel_params(32),
        cost_estimate=pl.CostEstimate(
            flops=8 * rows * width * width, bytes_accessed=6 * width * width, transcendentals=rows * 2 * CTX * 12
        ),
        name="attend",
    )(resid, tail, seg_q, seg_k, ln_gain, ln_bias, qkv_weight, qkv_bias)


def packed_kernel(enc_ref, dec_ref, out_ref):
    out_ref[0] = enc_ref[...].astype(BF16)
    out_ref[1] = dec_ref[...].astype(BF16)


def packed(enc, dec):
    rows, columns = enc.shape
    block = PACK_BLOCK
    across = lambda j: (0, j)
    return pl.pallas_call(
        packed_kernel,
        grid=(columns // block,),
        in_specs=[pl.BlockSpec((rows, block), across)] * 2,
        out_specs=pl.BlockSpec((2, rows, block), lambda j: (0, 0, j)),
        out_shape=jax.ShapeDtypeStruct((2, rows, columns), BF16),
        compiler_params=kernel_params(16),
        cost_estimate=pl.CostEstimate(flops=0, bytes_accessed=12 * rows * columns, transcendentals=0),
        name="packed",
    )(enc, dec)


def encode_kernel(count, rounded, *refs):
    z_refs, (keep_ref, enc_ref, bias_ref, dec_ref), rest = refs[:count], refs[count : count + 4], refs[count + 4 :]
    act_ref, rec_refs, (sum_ref, fire_ref, square_ref) = rest[0], rest[1 : 1 + count], rest[1 + count : 4 + count]
    totals = rest[4 + count :] if rounded else rec_refs
    step, last = pl.program_id(0), pl.num_programs(0) - 1
    features = enc_ref.shape[-1]

    def whole(ref):
        return ref[...].reshape(-1, features)

    @pl.when(step == 0)
    def _():
        spot, squares = 0, 0.0
        for total, z_ref in zip(totals, z_refs):
            total[...] = jnp.zeros_like(total)
            size, width = z_ref.shape
            values = z_ref[...].astype(F32)
            kept = wide(keep_ref[spot : spot + size, :], width) * values * values
            squares = squares + jnp.sum(kept.reshape(-1, 8, width), axis=0)
            spot += size
        square_ref[...] = jnp.sum(squares, axis=0, keepdims=True)

    blocks, spot = [], 0
    for piece in range(count):
        size = z_refs[piece].shape[0]
        block = min(ROW_BLOCK, size)
        for base in range(0, size, block):
            blocks.append((piece, slice(base, base + block), slice(spot + base, spot + base + block)))
        spot += size

    def preact_of(piece, rows):
        return dot_nn(z_refs[piece][rows, :], whole(enc_ref)) + bias_ref[...]

    sums = jnp.zeros((8, features), F32)
    fires = jnp.zeros((8, features), F32)
    coming = preact_of(*blocks[0][:2])
    for at, (piece, rows, place) in enumerate(blocks):
        preact = coming
        if at + 1 < len(blocks):
            coming = preact_of(*blocks[at + 1][:2])
        tiny = jnp.exp(-jnp.abs(preact))
        log_part = jnp.where(tiny < 2.0**-10, tiny * (1.0 - 0.5 * tiny), jnp.log(1.0 + tiny))
        act = jnp.maximum(preact, 0.0) + log_part
        low = act.astype(BF16)
        act_ref[place, :] = low
        kept = wide(keep_ref[place, :], features) * act
        sums = sums + jnp.sum(kept.reshape(-1, 8, features), axis=0)
        fires = fires + jnp.sum(jnp.tanh(kept).reshape(-1, 8, features), axis=0)
        totals[piece][rows, :] += dot_nt(low, whole(dec_ref))
    sum_ref[...] = jnp.sum(sums, axis=0, keepdims=True)
    fire_ref[...] = jnp.sum(fires, axis=0, keepdims=True)

    if rounded:

        @pl.when(step == last)
        def _():
            for piece in range(count):
                rec_refs[piece][...] = totals[piece][...].astype(BF16)


def wide(block, columns):
    return jnp.concatenate([block] * (columns // block.shape[1]), axis=1)


def encode(pieces, keep_wide, keep_at, weights, bias, rounded):
    parts, _, rows, features = weights.shape
    width = parts * rows
    sizes = [p.shape[0] for p in pieces]
    tokens = sum(sizes)
    fb = ENCODE_BLOCK
    whole = lambda j: (0, 0)
    across = lambda j: (0, j)
    keep_block = keep_at // tokens
    outs = pl.pallas_call(
        functools.partial(encode_kernel, len(pieces), rounded),
        grid=(features // fb,),
        in_specs=[pl.BlockSpec((s, width), whole) for s in sizes]
        + [
            pl.BlockSpec((tokens, LANES), lambda j: (keep_block, 0)),
            pl.BlockSpec((parts, None, rows, fb), lambda j: (0, 0, 0, j)),
            pl.BlockSpec((1, fb), across),
            pl.BlockSpec((parts, None, rows, fb), lambda j: (0, 1, 0, j)),
        ],
        out_specs=[pl.BlockSpec((tokens, fb), across)]
        + [pl.BlockSpec((s, width), whole) for s in sizes]
        + [pl.BlockSpec((1, fb), across)] * 2
        + [pl.BlockSpec((1, width), whole)],
        out_shape=[jax.ShapeDtypeStruct((tokens, features), BF16)]
        + [jax.ShapeDtypeStruct((s, width), BF16 if rounded else F32) for s in sizes]
        + [jax.ShapeDtypeStruct((1, features), F32)] * 2
        + [jax.ShapeDtypeStruct((1, width), F32)],
        scratch_shapes=[pltpu.VMEM((s, width), F32) for s in sizes] if rounded else [],
        compiler_params=kernel_params(ENCODE_VMEM),
        cost_estimate=pl.CostEstimate(
            flops=4 * tokens * width * features // COST_SHARE,
            bytes_accessed=2 * (2 * width * features + tokens * (features + 4 * width)) // COST_SHARE,
            transcendentals=3 * tokens * features // COST_SHARE,
        ),
        name="encode",
    )(*pieces, keep_wide, weights, bias, weights)
    return outs[0], outs[1 : 1 + len(pieces)], outs[-3:]


def backward_kernel(groups, carried, parted, *refs):
    refs = list(refs)
    slots = refs.pop(0) if parted else None
    acts, zs, gs, keeps = [], [], [], []
    for count in groups:
        acts.append(refs.pop(0))
        zs.append([refs.pop(0) for _ in range(count)])
        gs.append([refs.pop(0) for _ in range(count)])
        keeps.append(refs.pop(0))
    norm_ref, dec_ref = refs.pop(0), refs.pop(0)
    enc_in, dec_in = (refs.pop(0), refs.pop(0)) if carried else (None, None)
    outs = [refs.pop(0) for _ in range(2)]
    bias_ref, out_bias_ref, pre_s = refs
    features = dec_ref.shape[-1]

    @pl.when(pl.program_id(0) == 0)
    def _():
        total = 0.0
        for g_list in gs:
            for g_ref in g_list:
                total = total + jnp.sum(g_ref[...].astype(F32).reshape(-1, 8, g_ref.shape[1]), axis=0)
        out_bias_ref[...] = jnp.sum(total, axis=0, keepdims=True)


    blocks, pieces, spot = [], [], 0
    for act_ref, z_list, g_list, keep_ref in zip(acts, zs, gs, keeps):
        at = 0
        for z_ref, g_ref in zip(z_list, g_list):
            size = g_ref.shape[0]
            block = min(ROW_BLOCK, size)
            for base in range(0, size, block):
                blocks.append((g_ref, slice(base, base + block), act_ref, keep_ref, slice(at + base, at + base + block), slice(spot + base, spot + base + block)))
            pieces.append((z_ref, g_ref, act_ref, slice(at, at + size), slice(spot, spot + size)))
            at += size
            spot += size

    def grad_of(g_ref, rows):
        return dot_nn(g_ref[rows, :], dec_ref[...].reshape(-1, features))

    sums = jnp.zeros((8, features), F32)
    coming = grad_of(*blocks[0][:2])
    for at, (_, _, act_ref, keep_ref, local, place) in enumerate(blocks):
        grad_act = coming
        if at + 1 < len(blocks):
            coming = grad_of(*blocks[at + 1][:2])
        act = act_ref[local, :].astype(F32)
        slope = jnp.where(act < 2.0**-10, act * (1.0 - 0.5 * act), 1.0 - jnp.exp(-act))
        pre = (grad_act + wide(keep_ref[local, :], features) * norm_ref[...]) * slope
        sums = sums + jnp.sum(pre.reshape(-1, 8, features), axis=0)
        pre_s[place, :] = pre.astype(BF16)
    bias_ref[...] = jnp.sum(sums, axis=0, keepdims=True)
    dec_part = dec_in[...] if carried else None
    for _, g_ref, act_ref, local, _ in pieces:
        term = dot_tn(g_ref[...], act_ref[local, :])
        dec_part = term if dec_part is None else dec_part + term
    enc_part = enc_in[...] if carried else None
    for z_ref, _, _, _, place in pieces:
        term = dot_tn(z_ref[...], pre_s[place, :])
        enc_part = term if enc_part is None else enc_part + term
    if not parted:
        outs[0][...] = enc_part
        outs[1][...] = dec_part
        return
    keep_out, send_out = outs
    me = slots[0]
    for matrix, value in enumerate((enc_part, dec_part)):
        rows = value.shape[0] // parted
        for owner in range(parted):
            away = owner ^ me
            half = away // 2
            piece = value[owner * rows : (owner + 1) * rows, :]

            @pl.when(away % 2 == 0)
            def _():
                keep_out[pl.ds(half, 1), matrix] = piece[None]

            @pl.when(away % 2 == 1)
            def _():
                send_out[pl.ds(half, 1), matrix] = piece[None]


def backward(groups, keep_wide, norm_scaled, weights, carried, first, wide_by, parted, me):
    blocks, _, rows, _ = weights.shape
    width = blocks * rows
    counts = [len(zs) for _, zs, _, _ in groups]
    tokens = sum(act.shape[0] for act, _, _, _ in groups)
    fb = BACKWARD_BLOCK
    start = first // fb
    whole = lambda j, *_: (0, 0)
    across = lambda j, *_: (0, j + start)
    local = lambda j, *_: (0, j)
    operands, specs = [], []
    for act, zs, gs, keep_at in groups:
        size = act.shape[0]
        operands.append(act)
        specs.append(pl.BlockSpec((size, fb), across))
        for piece in (*zs, *gs):
            operands.append(piece)
            specs.append(pl.BlockSpec(piece.shape, whole, pipeline_mode=pl.Buffered(1)))
        operands.append(keep_wide)
        specs.append(pl.BlockSpec((size, LANES), lambda j, *_, at=keep_at // size: (at, 0)))
    operands += [norm_scaled, weights]
    specs += [pl.BlockSpec((1, fb), across), pl.BlockSpec((blocks, None, rows, fb), lambda j, *_: (0, 1, 0, j + start))]
    if carried is not None:
        operands += list(carried)
        specs += [pl.BlockSpec((width, fb), across)] * 2
    if parted:
        shape = (parted // 2, 2, width // parted, wide_by)
        block = pl.BlockSpec((parted // 2, 2, width // parted, fb), lambda j, *_: (0, 0, 0, j))
        out_shape = [jax.ShapeDtypeStruct(shape, F32)] * 2
        out_specs = [block] * 2
    else:
        out_shape = [jax.ShapeDtypeStruct((width, wide_by), F32)] * 2
        out_specs = [pl.BlockSpec((width, fb), local)] * 2
    out_shape += [jax.ShapeDtypeStruct((1, wide_by), F32), jax.ShapeDtypeStruct((1, width), F32)]
    out_specs += [pl.BlockSpec((1, fb), local), pl.BlockSpec((1, width), whole)]
    return pl.pallas_call(
        functools.partial(backward_kernel, counts, carried is not None, parted),
        grid_spec=pltpu.PrefetchScalarGridSpec(
            num_scalar_prefetch=1 if parted else 0,
            grid=(wide_by // fb,),
            in_specs=specs,
            out_specs=out_specs,
            scratch_shapes=[pltpu.VMEM((tokens, fb), BF16)],
        ),
        out_shape=out_shape,
        compiler_params=kernel_params(BACKWARD_VMEM),
        cost_estimate=pl.CostEstimate(
            flops=6 * tokens * width * wide_by // COST_SHARE,
            bytes_accessed=(2 * tokens * wide_by + 16 * width * wide_by) // COST_SHARE,
            transcendentals=tokens * wide_by // COST_SHARE,
        ),
        name="backward",
    )(*([me] if parted else []), *operands)


def ring_order(count):
    return list(range(0, count, 2)) + list(range(1, count, 2))[::-1]


def ring_shift(block, direction):
    order = ring_order(lax.axis_size("feat"))
    count = len(order)
    route = [(order[i], order[(i + direction) % count]) for i in range(count)]
    return lax.ppermute(block, "feat", route)


def swapped(block, axis, bit):
    return lax.ppermute(block, axis, [(i, i ^ bit) for i in range(lax.axis_size(axis))])


def summed(block, axes):
    for axis in axes:
        bit = 1
        while bit < lax.axis_size(axis):
            block = block + swapped(block, axis, bit)
            bit *= 2
    return block


def adamw(weight, grad, first, second, decay):
    first = BETA_ONE * first + (1.0 - BETA_ONE) * grad
    second = BETA_TWO * second + (1.0 - BETA_TWO) * grad * grad
    hat_first = first / (1.0 - BETA_ONE**STEP)
    hat_second = second / (1.0 - BETA_TWO**STEP)
    weight = weight - LEARN * (hat_first / (jnp.sqrt(hat_second) + EPSILON) + decay * weight)
    return (weight, first, second)


def shards(
    resid,
    segments,
    keep,
    ln_gain,
    ln_bias,
    qkv_weight,
    qkv_bias,
    enc_weight,
    enc_bias,
    dec_weight,
    dec_bias,
    enc_weight_m,
    enc_weight_v,
    enc_bias_m,
    enc_bias_v,
    dec_weight_m,
    dec_weight_v,
    dec_bias_m,
    dec_bias_v,
):
    own_rows, width = resid.shape
    group = keep.shape[0]
    feat_size, dp_size = lax.axis_size("feat"), lax.axis_size("dp")
    half = feat_size // 2
    features = enc_weight.shape[1]
    feat_at, dp_at = lax.axis_index("feat"), lax.axis_index("dp")
    everywhere = ("dp", "feat")

    me = dp_at.reshape(1).astype(jnp.int32)

    offset = feat_at * own_rows
    row_ids = jnp.arange(group, dtype=jnp.int32)
    seg_all = segments.reshape(group) + row_ids // ROW_LEN * ROW_LEN
    own_seg = lax.dynamic_slice_in_dim(seg_all, offset, own_rows)
    tail_seg = lax.dynamic_slice_in_dim(seg_all, jnp.maximum(offset - CTX, 0), CTX)
    tail_seg = jnp.where(feat_at > 0, tail_seg, -1)
    key_seg = jnp.concatenate([tail_seg, own_seg])[None]
    seg_wide = jnp.broadcast_to(own_seg[:, None], (own_rows, LANES))
    both = packed(enc_weight, dec_weight.T)
    weights = lax.all_gather(both, "dp")
    tail = lax.ppermute(resid[own_rows - CTX :], "feat", [(i, i + 1) for i in range(feat_size - 1)])
    tail, key_seg, seg_wide, both = together(tail, key_seg, seg_wide, both)
    tokens_z = attend(resid, tail, seg_wide, key_seg, ln_gain, ln_bias, qkv_weight, qkv_bias)

    tokens_z, keep = together(tokens_z, keep)
    z_stages = [[tokens_z]]
    right, left = tokens_z, tokens_z
    rows = own_rows // 2
    for hop in range(1, half):
        right, left = ring_shift(right, 1), ring_shift(left, -1)
        if hop == 1:
            order = jnp.asarray(ring_order(feat_size), jnp.int32)
            place = jnp.where(feat_at % 2 == 0, feat_at // 2, feat_size - 1 - feat_at // 2)
            keep_mask = keep.astype(F32)
            hops = []
            for away in range(1, half):
                hops += [-away, away]
            hops += [0, half]
            owners = order[(place + jnp.asarray(hops, jnp.int32)) % feat_size]
            keep_ring = keep_mask.reshape(feat_size, own_rows)[owners].reshape(group)
            keep_wide = jnp.broadcast_to(keep_ring[:, None], (group, LANES))
            own_keep = keep_ring[group - 2 * own_rows : group - own_rows][:, None]
            keep_total = jnp.sum(keep_mask)
            right, left, keep_wide, own_keep, keep_total = together(right, left, keep_wide, own_keep, keep_total)
        elif hop < half - 1:
            right, left = together(right, left)
        z_stages.append([right, left])
    right, left, weights = together(right, left, weights)
    z_stages[half - 1] = [right, left]
    keep_at = [group - 2 * own_rows] + [2 * (hop - 1) * own_rows for hop in range(1, half)] + [group - own_rows]
    z_float = tokens_z.astype(F32)
    acts, recs, stats = [None] * (half + 1), [None] * (half + 1), [None] * (half + 1)
    bias_row = enc_bias[None]

    def encoded(hop):
        acts[hop], recs[hop], stats[hop] = encode(
            z_stages[hop], keep_wide, keep_at[hop], weights, bias_row, hop == half
        )

    z_stages.append([ring_shift(right[:rows], 1), ring_shift(left[rows:], -1)])
    encoded(half - 1)
    z_stages[half], recs[half - 1], acts[half - 1] = together(z_stages[half], recs[half - 1], acts[half - 1])
    encoded(half)

    recs[half], weights = together(recs[half], weights)
    right, left = recs[half]
    for step in range(1, half + 1):
        right, left = ring_shift(right, 1), ring_shift(left, -1)
        if step == 1:
            dec_float = weights[:, 1].astype(F32)
            row_norm = jnp.sqrt(jnp.sum(dec_float * dec_float, axis=(0, 1)))[None]
            right, left, row_norm, z_stages[half - 2] = together(right, left, row_norm, z_stages[half - 2])
        elif step < half:
            hop = half - step
            encoded(hop)
            right, left, recs[hop], acts[hop], z_stages[hop - 1] = together(
                right, left, recs[hop], acts[hop], z_stages[hop - 1]
            )
        else:
            encoded(0)
            act_sum, fire_sum, square_sum = (sum(parts) for parts in zip(*stats))
            totals = jnp.stack([keep_total, jnp.sum(square_sum)])
            totals = jnp.pad(totals, (0, fire_sum.shape[1] - 2))[None]
            fired, act_total, totals = summed(jnp.concatenate([fire_sum, act_sum, totals]), ("dp",))
            counted, squares = totals[0], totals[1]
            mean_square = squares / (counted * width) + 1e-06
            unit = 2.0 / (width * mean_square * counted)
            norm_scaled = LAMBDA / counted * row_norm
            loss_part = LAMBDA * jnp.sum(act_sum * row_norm)
            penalty = (LAMBDA / counted) * act_total / row_norm[0]
            right, left, recs[0], acts[0], unit, norm_scaled, loss_part, penalty, fired = together(
                right, left, recs[0], acts[0], unit, norm_scaled, loss_part, penalty, fired
            )
            break
        from_left, from_right = recs[half - step]
        right, left = right.astype(F32), left.astype(F32)
        if step == 1:
            right = jnp.concatenate([from_right[:rows] + right, from_right[rows:]])
            left = jnp.concatenate([from_left[:rows], from_left[rows:] + left])
        else:
            right, left = from_right + right, from_left + left
        right, left = right.astype(BF16), left.astype(BF16)
    residue = recs[0][0] + right.astype(F32) + left.astype(F32) + dec_bias - z_float
    grad_out = own_keep * residue * unit
    fit_part = jnp.sum(own_keep * residue * residue) / (width * mean_square)
    loss_part = fit_part + loss_part
    own_grad = grad_out.astype(BF16)
    own_grad, loss_part = together(own_grad, loss_part)

    bias_share = out_bias_share = 0.0
    carried = None
    grad_stages = [[own_grad]]
    right, left = own_grad, own_grad

    def group_of(plan):
        return [(acts[hop], z_stages[hop], grad_stages[hop], keep_at[hop]) for hop in plan]

    for hop in range(1, half + 1):
        if hop == half:
            right, left = right[:rows], left[rows:]
        right, left = ring_shift(right, 1), ring_shift(left, -1)
        if hop < half:
            *carried, bias_grad, out_bias_grad = backward(
                group_of([hop - 1]), keep_wide, norm_scaled, weights, carried, 0, features, 0, None
            )
            bias_share, out_bias_share = bias_share + bias_grad, out_bias_share + out_bias_grad
        right, left, carried, bias_share, out_bias_share = together(right, left, carried, bias_share, out_bias_share)
        grad_stages.append([right, left])

    wide_by = features // LAST_PARTS
    kept, sent, aways, owns, last_bias = [], [], [], [], []
    scaled = norm_scaled
    for turn in range(LAST_PARTS + 2):
        coming = []
        if turn >= 2:
            away = aways[turn - 2]
            coming.append([swapped(block, "dp", 2 * other + 2) for other, block in enumerate(away)])
        else:
            coming.append([])
        coming.append(swapped(sent[turn - 1], "dp", 1) if 1 <= turn <= LAST_PARTS else None)
        if turn < LAST_PARTS:
            keep_part, send_part, bias_grad, out_bias_grad = backward(
                group_of([half - 1, half]), keep_wide, scaled, weights, carried, turn * wide_by, wide_by, dp_size, me
            )
            kept.append(keep_part)
            sent.append(send_part)
            last_bias.append(bias_grad)
        if turn == LAST_PARTS:
            bias_share = jnp.concatenate(
                [bias_share + jnp.concatenate(last_bias, axis=1), out_bias_share + out_bias_grad], axis=1
            )
            bias_share = summed(bias_share, ("dp",))[0]
        coming, scaled, sent, kept, bias_share = together(coming, scaled, sent, kept, bias_share)
        arrived, paired = coming
        if turn >= 2:
            owns[turn - 2] = owns[turn - 2] + sum(block.astype(F32) for block in arrived)
        if paired is not None:
            total = kept[turn - 1] + paired
            owns.append(total[0])
            aways.append([total[other].astype(BF16) for other in range(1, dp_size // 2)])
    enc_bias_grad, dec_bias_grad = bias_share[:features], bias_share[features:]
    own_dec = dec_weight.astype(BF16).astype(F32)
    own_squares = 0.0
    enc_grads, dec_grads = [], []
    for part in range(LAST_PARTS):
        span = slice(part * wide_by, (part + 1) * wide_by)
        enc_grads.append(owns[part][0])
        dec_grads.append(owns[part][1].T + penalty[span, None] * own_dec[span])
        own_squares = own_squares + jnp.sum(enc_grads[part] ** 2) + jnp.sum(dec_grads[part] ** 2)
    enc_grad = jnp.concatenate(enc_grads, axis=1)
    dec_grad = jnp.concatenate(dec_grads, axis=0)

    first_dp = dp_at == 0
    first_both = first_dp & (feat_at == 0)
    own_squares = own_squares + jnp.where(first_dp, jnp.sum(enc_bias_grad * enc_bias_grad), 0.0)
    own_squares = own_squares + jnp.where(first_both, jnp.sum(dec_bias_grad * dec_bias_grad), 0.0)
    total_squares, loss_total = summed(jnp.stack([own_squares, loss_part]), everywhere)
    overall_derivative_length = jnp.sqrt(total_squares)
    factor = jnp.minimum(1.0, CLIP_NORM / (overall_derivative_length + 1e-06))
    dec_new, dec_m, dec_v = adamw(dec_weight, dec_grad * factor, dec_weight_m, dec_weight_v, DECAY)
    row_squares = summed(jnp.sum(dec_new * dec_new, axis=1), ("dp",))
    enc_new, enc_m, enc_v = adamw(enc_weight, enc_grad * factor, enc_weight_m, enc_weight_v, DECAY)
    bias_new, bias_m, bias_v = adamw(enc_bias, enc_bias_grad * factor, enc_bias_m, enc_bias_v, 0.0)
    out_new, out_m, out_v = adamw(dec_bias, dec_bias_grad * factor, dec_bias_m, dec_bias_v, 0.0)
    dec_new = dec_new * lax.rsqrt(row_squares + 1e-12)[:, None]
    return (
        jnp.stack([loss_total, counted]),
        overall_derivative_length,
        fired,
        enc_new,
        enc_m,
        enc_v,
        bias_new,
        bias_m,
        bias_v,
        dec_new,
        dec_m,
        dec_v,
        out_new,
        out_m,
        out_v,
    )


def solution(mesh):
    return jax.shard_map(
        shards,
        mesh=mesh,
        in_specs=(
            P(("dp", "feat"), None),
            P("dp", None),
            P("dp"),
            P(),
            P(),
            P(),
            P(),
            P("dp", "feat"),
            P("feat"),
            P("feat", "dp"),
            P(),
            P("dp", "feat"),
            P("dp", "feat"),
            P("feat"),
            P("feat"),
            P("feat", "dp"),
            P("feat", "dp"),
            P(),
            P(),
        ),
        out_specs=(
            P(),
            P(),
            P("feat"),
            P("dp", "feat"),
            P("dp", "feat"),
            P("dp", "feat"),
            P("feat"),
            P("feat"),
            P("feat"),
            P("feat", "dp"),
            P("feat", "dp"),
            P("feat", "dp"),
            P(),
            P(),
            P(),
        ),
        check_vma=False,
    )
```

time: 525 us -> 466 us (0.89)
  Pallas kernels: 205 us -> 187 us
  waiting for transfers between devices: 152 us -> 135 us
  starting transfers between devices: 57.4 us -> 40.8 us
    ppermute x31 -> x17, waiting for transfers between devices: 79.9 us -> 50.6 us  [swapped(): lax.ppermute(block, axis, [(i, i ^ bit) for i in range(lax.axis_size(axis...]
    ppermute x31 -> x17, starting transfers between devices: 24.7 us -> 8.83 us  [swapped(): lax.ppermute(block, axis, [(i, i ^ bit) for i in range(lax.axis_size(axis...]
    pallas_call x5 -> x6, Pallas kernels: 93.7 us -> 78.2 us  [the longest x5 76 us: encode(): pl.pallas_call(functools.partial(encode_kernel, len(pieces), rounded), gr...]
    ppermute x24, waiting for transfers between devices: 70.9 us -> 80.6 us  [ring_shift(): return lax.ppermute(block, 'feat', route)]
    unnamed x131 -> x135, local copies, waits for them, and re-layouts: 6.89 us -> 10.9 us
    reduce_sum x6 -> x9, other arithmetic: 10.9 us -> 14.3 us  [the longest x1 3.31 us: shards(): row_norm = jnp.sqrt(jnp.sum(dec_float * dec_float, axis=(0, 1)))[None]]
    add x14 -> x12, other arithmetic: 10.6 us -> 13.7 us  [the longest x3 8.7 us: shards(): total = kept[turn - 1] + paired]
    pallas_call x5 -> x6, Pallas kernels: 102 us -> 103 us  [backward(): pl.pallas_call(functools.partial(backward_kernel, counts, carried is not...]
  transfers between devices with their start and end apart: 58 -> 43, of which waited for: 27 -> 23; matrix products, arithmetic and copies ran while one was open for 10% -> 8% of each run, Pallas kernels for 30% -> 32%
where the time goes in v2:
time: 466 us; the launch traced here: 459 us
  Pallas kernels  187 us (40%)
  waiting for transfers between devices  135 us (29%)
  other arithmetic  51.6 us (11%)
  starting transfers between devices  40.8 us (9%)
  between operations  26.7 us (6%)
  local copies, waits for them, and re-layouts  18 us (4%)
    pallas_call x6, Pallas kernels, backward(): pl.pallas_call(functools.partial(backward_kernel, counts, carried is not...  103 us
    ppermute x24, waiting for transfers between devices, ring_shift(): return lax.ppermute(block, 'feat', route)  80.6 us
    pallas_call x5, Pallas kernels, encode(): pl.pallas_call(functools.partial(encode_kernel, len(pieces), rounded), gr...  76 us
    ppermute x17, waiting for transfers between devices, swapped(): lax.ppermute(block, axis, [(i, i ^ bit) for i in range(lax.axis_size(axis...  50.6 us
    ppermute x24, starting transfers between devices, ring_shift(): return lax.ppermute(block, 'feat', route)  27.1 us
    unnamed x135, local copies, waits for them, and re-layouts  10.9 us
  transfers between devices with their start and end apart: 43, of which 23 were waited for; matrix products, arithmetic and copies ran while one was open for 8% of the time, Pallas kernels for 32%

profile of v2, /device:TPU:0, one launch (start us, length us, event | category | flops | bytes accessed | tf_op | source)
XLA Modules:
  0.0 459.3 jit_solution(7374429003907238523)
XLA Ops:
  10.6 2.2 packed.1
  13.9 4.9 %collective-permute-start = (bf16[128,768]{1,0:T(8,128)(2,1)S(1)}, bf16[128,768]{1,0:T(8,128)(2,1)S(1)}, u32[]{:S(2)}, u32[]{:S(2)}) collective-permute-start(bf16[128,768]{1,0:T(8,128)(2,1)S(1)} %slice.111), channel_id=1, source_target_pairs={{0,1},{1,2},{2,3},{3,4},{4,5},{5,6},{6,7},{8,9},{9,10},{10,11},{11... | collective-permute-start | bytes 589832 | tf_op jit(solution)/shard_map/ppermute | solution.py:453
  19.0 3.9 collective-permute-done.tail_ref
  23.1 2.5 copy-done.7
  25.6 5.9 %attend.1.refs_0_.refs_1_ = bf16[512,768]{1,0:T(8,128)(2,1)S(1)} custom-call(bf16[512,768]{1,0:T(8,128)(2,1)S(1)} %copy-done.6, bf16[128,768]{1,0:T(8,128)(2,1)S(1)} %collective-permute-done.tail_ref, s32[512,128]{1,0:T(8,128)S(1)} %broadcast_in_dim.41.seg_q_ref, s32[1,640]{1,0:T(1,128)S(1)} %broadcast_in_dim.40.seg_k_ref, bf16[768]{0:T(1024)(128)(2,1)S(1)} %copy-done.9, ...), custom_call_target="tpu_custom_call" | custom-call | flops 2415919104 | bytes 3538944 | tf_op jit(solution)/shard_map/attend/pallas_call | solution.py:104
  31.6 3.4 collective-permute-start.1
  36.9 14.1 %collective-permute-done.1.refs_0_.refs_1_ = bf16[512,768]{1,0:T(8,128)(2,1)S(1)} collective-permute-done((bf16[512,768]{1,0:T(8,128)(2,1)S(1)}, bf16[512,768]{1,0:T(8,128)(2,1)S(1)}, u32[]{:S(2)}, u32[]{:S(2)}) %collective-permute-start.1) | collective-permute-done | bytes 786464 | tf_op jit(solution)/shard_map/ppermute | solution.py:387
  51.0 2.2 collective-permute-done.2.refs_1_.refs_2_
  53.2 1.9 broadcast_in_dim.44.refs_2_.refs_1_.refs_3_.refs_5_.refs_6_.refs_12_
  57.2 15.4 %collective-permute-done.3.refs_0_.refs_1_ = bf16[512,768]{1,0:T(8,128)(2,1)S(1)} collective-permute-done((bf16[512,768]{1,0:T(8,128)(2,1)S(1)}, bf16[512,768]{1,0:T(8,128)(2,1)S(1)}, u32[]{:S(2)}, u32[]{:S(2)}) %collective-permute-start.3) | collective-permute-done | bytes 786464 | tf_op jit(solution)/shard_map/ppermute | solution.py:387
  75.9 14.8 %collective-permute-done.5.refs_0_.refs_2_ = bf16[512,768]{1,0:T(8,128)(2,1)S(1)} collective-permute-done((bf16[512,768]{1,0:T(8,128)(2,1)S(1)}, bf16[512,768]{1,0:T(8,128)(2,1)S(1)}, u32[]{:S(2)}, u32[]{:S(2)}) %collective-permute-start.5) | collective-permute-done | bytes 786464 | tf_op jit(solution)/shard_map/ppermute | solution.py:387
  94.5 17.5 %encode.5 = (bf16[1024,3072]{1,0:T(8,128)(2,1)}, f32[512,768]{1,0:T(8,128)}, f32[512,768]{1,0:T(8,128)}, f32[1,3072]{1,0:T(1,128)}, f32[1,3072]{1,0:T(1,128)}, /*index=5*/f32[1,768]{1,0:T(1,128)}) custom-call(bf16[512,768]{1,0:T(8,128)(2,1)} %copy-done.12, bf16[512,768]{1,0:T(8,128)(2,1)} %copy-done.13, ...), custom_call_target="tpu_custom_call" | custom-call | flops 2415919104 | bytes 5505024 | tf_op jit(solution)/shard_map/encode/pallas_call | solution.py:213
  112.9 11.4 %encode.6 = (bf16[512,3072]{1,0:T(8,128)(2,1)}, bf16[256,768]{1,0:T(8,128)(2,1)}, bf16[256,768]{1,0:T(8,128)(2,1)}, f32[1,3072]{1,0:T(1,128)}, f32[1,3072]{1,0:T(1,128)}, /*index=5*/f32[1,768]{1,0:T(1,128)}) custom-call(bf16[256,768]{1,0:T(8,128)(2,1)} %copy-done.17, bf16[256,768]{1,0:T(8,128)(2,1)} %copy-done.18, ...), custom_call_target="tpu_custom_call" | custom-call | flops 1207959552 | bytes 3932160 | tf_op jit(solution)/shard_map/encode/pallas_call | solution.py:213
  124.5 1.9 collective-permute-start.9
  126.4 3.3 multiply_reduce_fusion
  129.8 6.3 %collective-permute-done.10 = bf16[256,768]{1,0:T(8,128)(2,1)S(1)} collective-permute-done((bf16[256,768]{1,0:T(8,128)(2,1)}, bf16[256,768]{1,0:T(8,128)(2,1)S(1)}, u32[]{:S(2)}, u32[]{:S(2)}) %collective-permute-start.10) | collective-permute-done | bytes 393248 | tf_op jit(solution)/shard_map/ppermute | solution.py:387
  136.4 2.5 collective-permute-start.11
  138.9 17.4 %encode.7 = (bf16[1024,3072]{1,0:T(8,128)(2,1)}, f32[512,768]{1,0:T(8,128)}, f32[512,768]{1,0:T(8,128)}, f32[1,3072]{1,0:T(1,128)}, f32[1,3072]{1,0:T(1,128)}, /*index=5*/f32[1,768]{1,0:T(1,128)}) custom-call(bf16[512,768]{1,0:T(8,128)(2,1)} %copy-done.26, bf16[512,768]{1,0:T(8,128)(2,1)} %copy-done.27, ...), custom_call_target="tpu_custom_call" | custom-call | flops 2415919104 | bytes 5505024 | tf_op jit(solution)/shard_map/encode/pallas_call | solution.py:213
  158.4 2.0 collective-permute-start.13
  160.4 17.4 %encode.8 = (bf16[1024,3072]{1,0:T(8,128)(2,1)}, f32[512,768]{1,0:T(8,128)}, f32[512,768]{1,0:T(8,128)}, f32[1,3072]{1,0:T(1,128)}, f32[1,3072]{1,0:T(1,128)}, /*index=5*/f32[1,768]{1,0:T(1,128)}) custom-call(bf16[512,768]{1,0:T(8,128)(2,1)} %copy-done.24, bf16[512,768]{1,0:T(8,128)(2,1)} %copy-done.25, ...), custom_call_target="tpu_custom_call" | custom-call | flops 2415919104 | bytes 5505024 | tf_op jit(solution)/shard_map/encode/pallas_call | solution.py:213
  178.0 12.3 %encode.9 = (bf16[512,3072]{1,0:T(8,128)(2,1)}, f32[512,768]{1,0:T(8,128)}, f32[1,3072]{1,0:T(1,128)}, f32[1,3072]{1,0:T(1,128)}, f32[1,768]{1,0:T(1,128)}) custom-call(bf16[512,768]{1,0:T(8,128)(2,1)} %copy-done.4, f32[4096,128]{1,0:T(8,128)} %broadcast_in_dim.44.refs_2_.refs_1_.refs_3_.refs_5_.refs_6_.refs_12_, bf16[4,2,192,3072]{3,2,1,0:T(8,128)(2,1)} %bitcast.89, ...), custom_call_target="tpu_custom_call" | custom-call | flops 1207959552 | bytes 3932160 | tf_op jit(solution)/shard_map/encode/pallas_call | solution.py:213
  198.6 2.0 collective-permute-start.15
  205.3 10.7 %collective-permute-done.16 = bf16[512,768]{1,0:T(8,128)(2,1)} collective-permute-done((bf16[512,768]{1,0:T(8,128)(2,1)}, bf16[512,768]{1,0:T(8,128)(2,1)}, u32[]{:S(2)}, u32[]{:S(2)}) %collective-permute-start.16) | collective-permute-done | bytes 786464 | tf_op jit(solution)/shard_map/ppermute | solution.py:387
  216.0 2.5 collective-permute-done.15
  219.4 2.9 fusion.3
  222.9 1.8 collective-permute-start.19
  225.0 13.4 %backward.6 = (f32[768,3072]{1,0:T(8,128)}, f32[768,3072]{1,0:T(8,128)}, f32[1,3072]{1,0:T(1,128)}, f32[1,768]{1,0:T(1,128)}) custom-call(bf16[512,3072]{1,0:T(8,128)(2,1)} %get-tuple-element.238.refs_0_, bf16[512,768]{1,0:T(8,128)(2,1)} %copy-done.4, bf16[512,768]{1,0:T(8,128)(2,1)} %copy-done.23, ...), custom_call_target="tpu_custom_call" | custom-call | flops 1811939328 | bytes 10223616 | tf_op jit(solution)/shard_map/backward/pallas_call | solution.py:359
  238.4 3.2 collective-permute-done.19.refs_3_
  245.0 22.7 %backward.7 = (f32[768,3072]{1,0:T(8,128)}, f32[768,3072]{1,0:T(8,128)}, f32[1,3072]{1,0:T(1,128)}, f32[1,768]{1,0:T(1,128)}) custom-call(bf16[1024,3072]{1,0:T(8,128)(2,1)} %get-tuple-element.245.refs_0_, bf16[512,768]{1,0:T(8,128)(2,1)} %copy-done.24, bf16[512,768]{1,0:T(8,128)(2,1)} %copy-done.25, bf16[512,768]{1,0:T(8,128)(2,1)} %copy-done.40, ...), custom_call_target="tpu_custom_call" | custom-call | flops 3623878656 | bytes 11010048 | tf_op jit(solution)/shard_map/backward/pallas_call | solution.py:359
  271.3 22.8 %backward.8 = (f32[768,3072]{1,0:T(8,128)}, f32[768,3072]{1,0:T(8,128)}, f32[1,3072]{1,0:T(1,128)}, f32[1,768]{1,0:T(1,128)}) custom-call(bf16[1024,3072]{1,0:T(8,128)(2,1)} %get-tuple-element.256.refs_0_, bf16[512,768]{1,0:T(8,128)(2,1)} %copy-done.26, bf16[512,768]{1,0:T(8,128)(2,1)} %copy-done.27, bf16[512,768]{1,0:T(8,128)(2,1)} %copy-done.38, ...), custom_call_target="tpu_custom_call" | custom-call | flops 3623878656 | bytes 11010048 | tf_op jit(solution)/shard_map/backward/pallas_call | solution.py:359
  297.9 5.5 %collective-permute-done.25.refs_10_ = bf16[256,768]{1,0:T(8,128)(2,1)S(1)} collective-permute-done((bf16[256,768]{1,0:T(8,128)(2,1)S(1)}, bf16[256,768]{1,0:T(8,128)(2,1)S(1)}, u32[]{:S(2)}, u32[]{:S(2)}) %collective-permute-start.25) | collective-permute-done | bytes 393248 | tf_op jit(solution)/shard_map/ppermute | solution.py:387
  303.4 2.0 collective-permute-done.26.refs_11_
  306.1 14.5 %backward.9 = (f32[2,2,192,1024]{3,2,1,0:T(8,128)}, f32[2,2,192,1024]{3,2,1,0:T(8,128)}, f32[1,1024]{1,0:T(1,128)}, f32[1,768]{1,0:T(1,128)}) custom-call(s32[1]{0:T(128)} %bitcast.14.refs_0_, bf16[1024,3072]{1,0:T(8,128)(2,1)} %get-tuple-element.230.refs_1_, bf16[512,768]{1,0:T(8,128)(2,1)} %copy-done.12, bf16[512,768]{1,0:T(8,128)(2,1)} %copy-done.13, ...), custom_call_target="tpu_custom_call" | custom-call | flops 1811939328 | bytes 3932160 | tf_op jit(solution)/shard_map/backward/pallas_call | solution.py:359
  320.7 14.7 %backward.10 = (f32[2,2,192,1024]{3,2,1,0:T(8,128)}, f32[2,2,192,1024]{3,2,1,0:T(8,128)}, f32[1,1024]{1,0:T(1,128)}, f32[1,768]{1,0:T(1,128)}) custom-call(s32[1]{0:T(128)} %bitcast.14.refs_0_, bf16[1024,3072]{1,0:T(8,128)(2,1)} %get-tuple-element.230.refs_1_, bf16[512,768]{1,0:T(8,128)(2,1)} %copy-done.12, bf16[512,768]{1,0:T(8,128)(2,1)} %copy-done.13, ...), custom_call_target="tpu_custom_call" | custom-call | flops 1811939328 | bytes 3932160 | tf_op jit(solution)/shard_map/backward/pallas_call | solution.py:359
  336.0 3.9 add.321
  342.2 14.8 %backward.11 = (f32[2,2,192,1024]{3,2,1,0:T(8,128)}, f32[2,2,192,1024]{3,2,1,0:T(8,128)}, f32[1,1024]{1,0:T(1,128)}, f32[1,768]{1,0:T(1,128)}) custom-call(s32[1]{0:T(128)} %bitcast.14.refs_0_, bf16[1024,3072]{1,0:T(8,128)(2,1)} %get-tuple-element.230.refs_1_, bf16[512,768]{1,0:T(8,128)(2,1)} %copy-done.12, bf16[512,768]{1,0:T(8,128)(2,1)} %copy-done.13, ...), custom_call_target="tpu_custom_call" | custom-call | flops 1811939328 | bytes 3932160 | tf_op jit(solution)/shard_map/backward/pallas_call | solution.py:359
  357.0 2.6 collective-permute-done.28
  361.6 3.8 add.325
  368.2 17.3 %collective-permute-done.33 = f32[1,3840]{1,0:T(1,128)S(1)} collective-permute-done((f32[1,3840]{1,0:T(1,128)S(1)}, f32[1,3840]{1,0:T(1,128)S(1)}, u32[]{:S(2)}, u32[]{:S(2)}) %collective-permute-start.33) | collective-permute-done | bytes 15392 | tf_op jit(solution)/shard_map/ppermute | solution.py:391
  390.0 15.3 %collective-permute-done.34 = bf16[2,192,1024]{2,1,0:T(8,128)(2,1)S(1)} collective-permute-done((bf16[2,192,1024]{2,1,0:T(8,128)(2,1)S(1)}, bf16[2,192,1024]{2,1,0:T(8,128)(2,1)S(1)}, u32[]{:S(2)}, u32[]{:S(2)}) %collective-permute-start.34) | collective-permute-done | bytes 786464 | tf_op jit(solution)/shard_map/ppermute | solution.py:391
  408.5 2.3 multiply_reduce_fusion.2
  417.8 3.0 collective-permute-done.36
  421.2 3.2 collective-permute-done.37
  425.1 2.9 collective-permute-done.38
  428.6 3.8 collective-permute-done.39
  433.9 5.6 %multiply_reduce_fusion.1 = (f32[3072]{0:T(1024)S(1)}, f32[3072,192]{0,1:T(8,128)S(1)}, f32[3072,192]{0,1:T(8,128)}, f32[3072,192]{0,1:T(8,128)}) fusion(f32[3072,192]{0,1:T(8,128)S(1)} %copy-done.1, f32[]{:T(128)S(6)} %min_shard_map.3, f32[1024,192]{0,1:T(8,128)} %get-tuple-element.327, f32[1024,192]{0,1:T(8,128)} %get-tuple-element.337, ...), kind=kLoop, calls=%fused_computation.9 | loop fusion | flops 11793408 | bytes 16527364 | tf_op jit(solution)/shard_map/reduce_sum | solution.py:613
  441.2 3.6 multiply_subtract_fusion.1
  446.0 1.9 pad_maximum_fusion.5
  (274 shorter events, 66.7 us)
Async XLA Ops:
  7.2 84.9 %all-gather.3.cloned.1.call-start = ((), (), s32[]{:S(2)}) async-start(), calls=%async_computation | async-start | bytes 11796480 | tf_op jit(solution)/shard_map/all_gather | solution.py:452
  13.9 9.0 %collective-permute-start = (bf16[128,768]{1,0:T(8,128)(2,1)S(1)}, bf16[128,768]{1,0:T(8,128)(2,1)S(1)}, u32[]{:S(2)}, u32[]{:S(2)}) collective-permute-start(bf16[128,768]{1,0:T(8,128)(2,1)S(1)} %slice.111), channel_id=1, source_target_pairs={{0,1},{1,2},{2,3},{3,4},{4,5},{5,6},{6,7},{8,9},{9,10},{10,11},{11... | collective-permute-start | bytes 589832 | tf_op jit(solution)/shard_map/ppermute | solution.py:453
  31.6 80.4 %copy-start.4 = (bf16[512,768]{1,0:T(8,128)(2,1)}, bf16[512,768]{1,0:T(8,128)(2,1)S(1)}, u32[]{:S(2)}) copy-start(bf16[512,768]{1,0:T(8,128)(2,1)S(1)} %attend.1.refs_0_.refs_1_) | copy-start | bytes 2359300
  31.6 19.5 %collective-permute-start.1 = (bf16[512,768]{1,0:T(8,128)(2,1)S(1)}, bf16[512,768]{1,0:T(8,128)(2,1)S(1)}, u32[]{:S(2)}, u32[]{:S(2)}) collective-permute-start(bf16[512,768]{1,0:T(8,128)(2,1)S(1)} %attend.1.refs_0_.refs_1_), channel_id=1, source_target_pairs={{0,2},{2,4},{4,6},{6,7},{7,5},{5,3},{3,1},{1,0},{8,10},{10,12},{12... | collective-permute-start | bytes 2359304 | tf_op jit(solution)/shard_map/ppermute | solution.py:387
  35.0 18.2 %collective-permute-start.2 = (bf16[512,768]{1,0:T(8,128)(2,1)S(1)}, bf16[512,768]{1,0:T(8,128)(2,1)S(1)}, u32[]{:S(2)}, u32[]{:S(2)}) collective-permute-start(bf16[512,768]{1,0:T(8,128)(2,1)S(1)} %attend.1.refs_0_.refs_1_), channel_id=1, source_target_pairs={{0,1},{2,0},{4,2},{6,4},{7,6},{5,7},{3,5},{1,3},{8,9},{10,8},{12,1... | collective-permute-start | bytes 2359304 | tf_op jit(solution)/shard_map/ppermute | solution.py:387
  51.0 61.0 %copy-start.24 = (bf16[512,768]{1,0:T(8,128)(2,1)}, bf16[512,768]{1,0:T(8,128)(2,1)S(1)}, u32[]{:S(2)}) copy-start(bf16[512,768]{1,0:T(8,128)(2,1)S(1)} %collective-permute-done.1.refs_0_.refs_1_) | copy-start | bytes 2359300
  55.2 17.4 %collective-permute-start.3 = (bf16[512,768]{1,0:T(8,128)(2,1)S(1)}, bf16[512,768]{1,0:T(8,128)(2,1)S(1)}, u32[]{:S(2)}, u32[]{:S(2)}) collective-permute-start(bf16[512,768]{1,0:T(8,128)(2,1)S(1)} %collective-permute-done.1.refs_0_.refs_1_), channel_id=1, source_target_pairs={{0,2},{2,4},{4,6},{6,7},{7,5},{5,3},{3,1},{1,0},{8,10},{10,12},{12... | collective-permute-start | bytes 2359304 | tf_op jit(solution)/shard_map/ppermute | solution.py:387
  56.8 17.1 %collective-permute-start.4 = (bf16[512,768]{1,0:T(8,128)(2,1)S(1)}, bf16[512,768]{1,0:T(8,128)(2,1)S(1)}, u32[]{:S(2)}, u32[]{:S(2)}) collective-permute-start(bf16[512,768]{1,0:T(8,128)(2,1)S(1)} %collective-permute-done.2.refs_1_.refs_2_), channel_id=1, source_target_pairs={{0,1},{2,0},{4,2},{6,4},{7,6},{5,7},{3,5},{1,3},{8,9},{10,8},{12,1... | collective-permute-start | bytes 2359304 | tf_op jit(solution)/shard_map/ppermute | solution.py:387
  73.9 16.8 %collective-permute-start.5 = (bf16[512,768]{1,0:T(8,128)(2,1)S(1)}, bf16[512,768]{1,0:T(8,128)(2,1)S(1)}, u32[]{:S(2)}, u32[]{:S(2)}) collective-permute-start(bf16[512,768]{1,0:T(8,128)(2,1)S(1)} %collective-permute-done.3.refs_0_.refs_1_), channel_id=1, source_target_pairs={{0,2},{2,4},{4,6},{6,7},{7,5},{5,3},{3,1},{1,0},{8,10},{10,12},{12... | collective-permute-start | bytes 2359304 | tf_op jit(solution)/shard_map/ppermute | solution.py:387
  75.6 16.5 %collective-permute-start.6 = (bf16[512,768]{1,0:T(8,128)(2,1)S(1)}, bf16[512,768]{1,0:T(8,128)(2,1)S(1)}, u32[]{:S(2)}, u32[]{:S(2)}) collective-permute-start(bf16[512,768]{1,0:T(8,128)(2,1)S(1)} %collective-permute-done.4.refs_1_.refs_2_), channel_id=1, source_target_pairs={{0,1},{2,0},{4,2},{6,4},{7,6},{5,7},{3,5},{1,3},{8,9},{10,8},{12,1... | collective-permute-start | bytes 2359304 | tf_op jit(solution)/shard_map/ppermute | solution.py:387
  92.1 19.9 %collective-permute-start.7 = (bf16[256,768]{1,0:T(8,128)(2,1)S(1)}, bf16[256,768]{1,0:T(8,128)(2,1)S(1)}, u32[]{:S(2)}, u32[]{:S(2)}) collective-permute-start(bf16[256,768]{1,0:T(8,128)(2,1)S(1)} %slice.113), channel_id=1, source_target_pairs={{0,2},{2,4},{4,6},{6,7},{7,5},{5,3},{3,1},{1,0},{8,10},{10,12},{12... | collective-permute-start | bytes 1179656 | tf_op jit(solution)/shard_map/ppermute | solution.py:387
  93.2 18.8 %collective-permute-start.8 = (bf16[256,768]{1,0:T(8,128)(2,1)S(1)}, bf16[256,768]{1,0:T(8,128)(2,1)S(1)}, u32[]{:S(2)}, u32[]{:S(2)}) collective-permute-start(bf16[256,768]{1,0:T(8,128)(2,1)S(1)} %slice.114), channel_id=1, source_target_pairs={{0,1},{2,0},{4,2},{6,4},{7,6},{5,7},{3,5},{1,3},{8,9},{10,8},{12,1... | collective-permute-start | bytes 1179656 | tf_op jit(solution)/shard_map/ppermute | solution.py:387
  124.3 11.8 %collective-permute-start.10 = (bf16[256,768]{1,0:T(8,128)(2,1)}, bf16[256,768]{1,0:T(8,128)(2,1)S(1)}, u32[]{:S(2)}, u32[]{:S(2)}) collective-permute-start(bf16[256,768]{1,0:T(8,128)(2,1)} %get-tuple-element.186), channel_id=1, source_target_pairs={{0,1},{2,0},{4,2},{6,4},{7,6},{5,7},{3,5},{1,3},{8,9},{10,8},{12,1... | collective-permute-start | bytes 1179656 | tf_op jit(solution)/shard_map/ppermute | solution.py:387
  124.5 11.6 %collective-permute-start.9 = (bf16[256,768]{1,0:T(8,128)(2,1)}, bf16[256,768]{1,0:T(8,128)(2,1)S(1)}, u32[]{:S(2)}, u32[]{:S(2)}) collective-permute-start(bf16[256,768]{1,0:T(8,128)(2,1)} %get-tuple-element.185), channel_id=1, source_target_pairs={{0,2},{2,4},{4,6},{6,7},{7,5},{5,3},{3,1},{1,0},{8,10},{10,12},{12... | collective-permute-start | bytes 1179656 | tf_op jit(solution)/shard_map/ppermute | solution.py:387
  136.2 20.1 %collective-permute-start.12 = (bf16[512,768]{1,0:T(8,128)(2,1)S(1)}, bf16[512,768]{1,0:T(8,128)(2,1)S(1)}, u32[]{:S(2)}, u32[]{:S(2)}) collective-permute-start(bf16[512,768]{1,0:T(8,128)(2,1)S(1)} %pad_maximum_fusion.1), channel_id=1, source_target_pairs={{0,1},{2,0},{4,2},{6,4},{7,6},{5,7},{3,5},{1,3},{8,9},{10,8},{12,1... | collective-permute-start | bytes 2359304 | tf_op jit(solution)/shard_map/ppermute | solution.py:387
  136.4 19.9 %collective-permute-start.11 = (bf16[512,768]{1,0:T(8,128)(2,1)S(1)}, bf16[512,768]{1,0:T(8,128)(2,1)S(1)}, u32[]{:S(2)}, u32[]{:S(2)}) collective-permute-start(bf16[512,768]{1,0:T(8,128)(2,1)S(1)} %pad_maximum_fusion), channel_id=1, source_target_pairs={{0,2},{2,4},{4,6},{6,7},{7,5},{5,3},{3,1},{1,0},{8,10},{10,12},{12... | collective-permute-start | bytes 2359304 | tf_op jit(solution)/shard_map/ppermute | solution.py:387
  158.1 19.8 %collective-permute-start.14 = (bf16[512,768]{1,0:T(8,128)(2,1)S(1)}, bf16[512,768]{1,0:T(8,128)(2,1)S(1)}, u32[]{:S(2)}, u32[]{:S(2)}) collective-permute-start(bf16[512,768]{1,0:T(8,128)(2,1)S(1)} %add_convert_fusion.2), channel_id=1, source_target_pairs={{0,1},{2,0},{4,2},{6,4},{7,6},{5,7},{3,5},{1,3},{8,9},{10,8},{12,1... | collective-permute-start | bytes 2359304 | tf_op jit(solution)/shard_map/ppermute | solution.py:387
  158.4 19.4 %collective-permute-start.13 = (bf16[512,768]{1,0:T(8,128)(2,1)S(1)}, bf16[512,768]{1,0:T(8,128)(2,1)S(1)}, u32[]{:S(2)}, u32[]{:S(2)}) collective-permute-start(bf16[512,768]{1,0:T(8,128)(2,1)S(1)} %add_convert_fusion.3), channel_id=1, source_target_pairs={{0,2},{2,4},{4,6},{6,7},{7,5},{5,3},{3,1},{1,0},{8,10},{10,12},{12... | collective-permute-start | bytes 2359304 | tf_op jit(solution)/shard_map/ppermute | solution.py:387
  194.6 1.3 collective-permute-start.17
  195.8 23.6 %copy-start.45 = (f32[768]{0:T(1024)S(1)}, f32[768]{0:T(1024)}, u32[]{:S(2)}) copy-start(f32[768]{0:T(1024)} %param.31) | copy-start | bytes 9220
  195.8 20.3 %collective-permute-start.16 = (bf16[512,768]{1,0:T(8,128)(2,1)}, bf16[512,768]{1,0:T(8,128)(2,1)}, u32[]{:S(2)}, u32[]{:S(2)}) collective-permute-start(bf16[512,768]{1,0:T(8,128)(2,1)} %add_convert_fusion), channel_id=1, source_target_pairs={{0,1},{2,0},{4,2},{6,4},{7,6},{5,7},{3,5},{1,3},{8,9},{10,8},{12,1... | collective-permute-start | bytes 2359304 | tf_op jit(solution)/shard_map/ppermute | solution.py:387
  196.0 5.3 %collective-permute-start.18 = (f32[3,3072]{1,0:T(4,128)S(1)}, f32[3,3072]{1,0:T(4,128)S(1)}, u32[]{:S(2)}, u32[]{:S(2)}) collective-permute-start(f32[3,3072]{1,0:T(4,128)S(1)} %fusion.24), channel_id=1, source_target_pairs={{0,16},{8,24},{16,0},{24,8},{1,17},{9,25},{17,1},{25,9},{2,18},{10... | collective-permute-start | bytes 110600 | tf_op jit(solution)/shard_map/ppermute | solution.py:391
  198.6 19.9 %collective-permute-start.15 = (bf16[512,768]{1,0:T(8,128)(2,1)}, bf16[512,768]{1,0:T(8,128)(2,1)S(1)}, u32[]{:S(2)}, u32[]{:S(2)}) collective-permute-start(bf16[512,768]{1,0:T(8,128)(2,1)} %add_convert_fusion.1), channel_id=1, source_target_pairs={{0,2},{2,4},{4,6},{6,7},{7,5},{5,3},{3,1},{1,0},{8,10},{10,12},{12... | collective-permute-start | bytes 2359304 | tf_op jit(solution)/shard_map/ppermute | solution.py:387
  222.9 18.7 %collective-permute-start.19 = (bf16[512,768]{1,0:T(8,128)(2,1)S(1)}, bf16[512,768]{1,0:T(8,128)(2,1)S(1)}, u32[]{:S(2)}, u32[]{:S(2)}) collective-permute-start(bf16[512,768]{1,0:T(8,128)(2,1)S(1)} %get-tuple-element.237.refs_2_), channel_id=1, source_target_pairs={{0,2},{2,4},{4,6},{6,7},{7,5},{5,3},{3,1},{1,0},{8,10},{10,12},{12... | collective-permute-start | bytes 2359304 | tf_op jit(solution)/shard_map/ppermute | solution.py:387
  224.7 18.2 %collective-permute-start.20 = (bf16[512,768]{1,0:T(8,128)(2,1)S(1)}, bf16[512,768]{1,0:T(8,128)(2,1)S(1)}, u32[]{:S(2)}, u32[]{:S(2)}) collective-permute-start(bf16[512,768]{1,0:T(8,128)(2,1)S(1)} %get-tuple-element.237.refs_2_), channel_id=1, source_target_pairs={{0,1},{2,0},{4,2},{6,4},{7,6},{5,7},{3,5},{1,3},{8,9},{10,8},{12,1... | collective-permute-start | bytes 2359304 | tf_op jit(solution)/shard_map/ppermute | solution.py:387
  242.9 24.8 %copy-start.61 = (f32[1,768]{1,0:T(1,128)S(1)}, f32[1,768]{1,0:T(1,128)}, u32[]{:S(2)}) copy-start(f32[1,768]{1,0:T(1,128)} %get-tuple-element.252) | copy-start | bytes 9220
  242.9 25.5 %copy-start.54 = (f32[1,3072]{1,0:T(1,128)S(1)}, f32[1,3072]{1,0:T(1,128)}, u32[]{:S(2)}) copy-start(f32[1,3072]{1,0:T(1,128)} %get-tuple-element.250) | copy-start | bytes 36868
  242.9 26.2 %collective-permute-start.21 = (bf16[512,768]{1,0:T(8,128)(2,1)S(1)}, bf16[512,768]{1,0:T(8,128)(2,1)S(1)}, u32[]{:S(2)}, u32[]{:S(2)}) collective-permute-start(bf16[512,768]{1,0:T(8,128)(2,1)S(1)} %collective-permute-done.19.refs_3_), channel_id=1, source_target_pairs={{0,2},{2,4},{4,6},{6,7},{7,5},{5,3},{3,1},{1,0},{8,10},{10,12},{12... | collective-permute-start | bytes 2359304 | tf_op jit(solution)/shard_map/ppermute | solution.py:387
  244.6 24.5 %collective-permute-start.22 = (bf16[512,768]{1,0:T(8,128)(2,1)S(1)}, bf16[512,768]{1,0:T(8,128)(2,1)S(1)}, u32[]{:S(2)}, u32[]{:S(2)}) collective-permute-start(bf16[512,768]{1,0:T(8,128)(2,1)S(1)} %collective-permute-done.20.refs_4_), channel_id=1, source_target_pairs={{0,1},{2,0},{4,2},{6,4},{7,6},{5,7},{3,5},{1,3},{8,9},{10,8},{12,1... | collective-permute-start | bytes 2359304 | tf_op jit(solution)/shard_map/ppermute | solution.py:387
  269.2 26.3 %collective-permute-start.23 = (bf16[512,768]{1,0:T(8,128)(2,1)S(1)}, bf16[512,768]{1,0:T(8,128)(2,1)S(1)}, u32[]{:S(2)}, u32[]{:S(2)}) collective-permute-start(bf16[512,768]{1,0:T(8,128)(2,1)S(1)} %collective-permute-done.21.refs_3_), channel_id=1, source_target_pairs={{0,2},{2,4},{4,6},{6,7},{7,5},{5,3},{3,1},{1,0},{8,10},{10,12},{12... | collective-permute-start | bytes 2359304 | tf_op jit(solution)/shard_map/ppermute | solution.py:387
  270.9 24.6 %collective-permute-start.24 = (bf16[512,768]{1,0:T(8,128)(2,1)S(1)}, bf16[512,768]{1,0:T(8,128)(2,1)S(1)}, u32[]{:S(2)}, u32[]{:S(2)}) collective-permute-start(bf16[512,768]{1,0:T(8,128)(2,1)S(1)} %collective-permute-done.22.refs_4_), channel_id=1, source_target_pairs={{0,1},{2,0},{4,2},{6,4},{7,6},{5,7},{3,5},{1,3},{8,9},{10,8},{12,1... | collective-permute-start | bytes 2359304 | tf_op jit(solution)/shard_map/ppermute | solution.py:387
  295.5 7.8 %collective-permute-start.25 = (bf16[256,768]{1,0:T(8,128)(2,1)S(1)}, bf16[256,768]{1,0:T(8,128)(2,1)S(1)}, u32[]{:S(2)}, u32[]{:S(2)}) collective-permute-start(bf16[256,768]{1,0:T(8,128)(2,1)S(1)} %slice.122), channel_id=1, source_target_pairs={{0,2},{2,4},{4,6},{6,7},{7,5},{5,3},{3,1},{1,0},{8,10},{10,12},{12... | collective-permute-start | bytes 1179656 | tf_op jit(solution)/shard_map/ppermute | solution.py:387
  297.3 8.0 %collective-permute-start.26 = (bf16[256,768]{1,0:T(8,128)(2,1)S(1)}, bf16[256,768]{1,0:T(8,128)(2,1)S(1)}, u32[]{:S(2)}, u32[]{:S(2)}) collective-permute-start(bf16[256,768]{1,0:T(8,128)(2,1)S(1)} %slice.123), channel_id=1, source_target_pairs={{0,1},{2,0},{4,2},{6,4},{7,6},{5,7},{3,5},{1,3},{8,9},{10,8},{12,1... | collective-permute-start | bytes 1179656 | tf_op jit(solution)/shard_map/ppermute | solution.py:387
  320.7 14.8 %collective-permute-start.27 = (f32[2,2,192,1024]{3,2,1,0:T(8,128)}, f32[2,2,192,1024]{3,2,1,0:T(8,128)}, u32[]{:S(2)}, u32[]{:S(2)}) collective-permute-start(f32[2,2,192,1024]{3,2,1,0:T(8,128)} %get-tuple-element.279), channel_id=1, source_target_pairs={{0,8},{8,0},{16,24},{24,16},{1,9},{9,1},{17,25},{25,17},{2,10},{10... | collective-permute-start | bytes 9437192 | tf_op jit(solution)/shard_map/ppermute | solution.py:391
  335.4 24.2 %collective-permute-start.29 = (f32[2,2,192,1024]{3,2,1,0:T(8,128)}, f32[2,2,192,1024]{3,2,1,0:T(8,128)}, u32[]{:S(2)}, u32[]{:S(2)}) collective-permute-start(f32[2,2,192,1024]{3,2,1,0:T(8,128)} %get-tuple-element.287), channel_id=1, source_target_pairs={{0,8},{8,0},{16,24},{24,16},{1,9},{9,1},{17,25},{25,17},{2,10},{10... | collective-permute-start | bytes 9437192 | tf_op jit(solution)/shard_map/ppermute | solution.py:391
  340.1 19.6 %collective-permute-start.28 = (bf16[2,192,1024]{2,1,0:T(8,128)(2,1)S(1)}, bf16[2,192,1024]{2,1,0:T(8,128)(2,1)S(1)}, u32[]{:S(2)}, u32[]{:S(2)}) collective-permute-start(bf16[2,192,1024]{2,1,0:T(8,128)(2,1)S(1)} %fusion.7), channel_id=1, source_target_pairs={{0,16},{8,24},{16,0},{24,8},{1,17},{9,25},{17,1},{25,9},{2,18},{10... | collective-permute-start | bytes 2359304 | tf_op jit(solution)/shard_map/ppermute | solution.py:391
  359.6 25.9 %collective-permute-start.31 = (f32[2,2,192,1024]{3,2,1,0:T(8,128)}, f32[2,2,192,1024]{3,2,1,0:T(8,128)S(1)}, u32[]{:S(2)}, u32[]{:S(2)}) collective-permute-start(f32[2,2,192,1024]{3,2,1,0:T(8,128)} %get-tuple-element.297), channel_id=1, source_target_pairs={{0,8},{8,0},{16,24},{24,16},{1,9},{9,1},{17,25},{25,17},{2,10},{10... | collective-permute-start | bytes 9437192 | tf_op jit(solution)/shard_map/ppermute | solution.py:391
  361.1 5.4 %collective-permute-start.32 = (f32[1,3840]{1,0:T(1,128)S(1)}, f32[1,3840]{1,0:T(1,128)S(1)}, u32[]{:S(2)}, u32[]{:S(2)}) collective-permute-start(f32[1,3840]{1,0:T(1,128)S(1)} %pad_maximum_fusion.3), channel_id=1, source_target_pairs={{0,8},{8,0},{16,24},{24,16},{1,9},{9,1},{17,25},{25,17},{2,10},{10... | collective-permute-start | bytes 46088 | tf_op jit(solution)/shard_map/ppermute | solution.py:391
  365.6 19.9 %collective-permute-start.30 = (bf16[2,192,1024]{2,1,0:T(8,128)(2,1)S(1)}, bf16[2,192,1024]{2,1,0:T(8,128)(2,1)S(1)}, u32[]{:S(2)}, u32[]{:S(2)}) collective-permute-start(bf16[2,192,1024]{2,1,0:T(8,128)(2,1)S(1)} %fusion.8), channel_id=1, source_target_pairs={{0,16},{8,24},{16,0},{24,8},{1,17},{9,25},{17,1},{25,9},{2,18},{10... | collective-permute-start | bytes 2359304 | tf_op jit(solution)/shard_map/ppermute | solution.py:391
  366.5 18.9 %collective-permute-start.33 = (f32[1,3840]{1,0:T(1,128)S(1)}, f32[1,3840]{1,0:T(1,128)S(1)}, u32[]{:S(2)}, u32[]{:S(2)}) collective-permute-start(f32[1,3840]{1,0:T(1,128)S(1)} %fusion.23), channel_id=1, source_target_pairs={{0,16},{8,24},{16,0},{24,8},{1,17},{9,25},{17,1},{25,9},{2,18},{10... | collective-permute-start | bytes 46088 | tf_op jit(solution)/shard_map/ppermute | solution.py:391
  386.6 18.7 %collective-permute-start.34 = (bf16[2,192,1024]{2,1,0:T(8,128)(2,1)S(1)}, bf16[2,192,1024]{2,1,0:T(8,128)(2,1)S(1)}, u32[]{:S(2)}, u32[]{:S(2)}) collective-permute-start(bf16[2,192,1024]{2,1,0:T(8,128)(2,1)S(1)} %fusion.9), channel_id=1, source_target_pairs={{0,16},{8,24},{16,0},{24,8},{1,17},{9,25},{17,1},{25,9},{2,18},{10... | collective-permute-start | bytes 2359304 | tf_op jit(solution)/shard_map/ppermute | solution.py:391
  416.1 1.1 collective-permute-start.35
  417.3 3.5 collective-permute-start.36
  420.9 3.5 collective-permute-start.37
  424.4 3.5 collective-permute-start.38
  428.0 4.4 collective-permute-start.39
  439.5 6.0 %collective-permute-start.40 = (f32[3072]{0:T(1024)S(1)}, f32[3072]{0:T(1024)S(1)}, u32[]{:S(2)}, u32[]{:S(2)}) collective-permute-start(f32[3072]{0:T(1024)S(1)} %get-tuple-element.316), channel_id=1, source_target_pairs={{0,8},{8,0},{16,24},{24,16},{1,9},{9,1},{17,25},{25,17},{2,10},{10... | collective-permute-start | bytes 36872 | tf_op jit(solution)/shard_map/ppermute | solution.py:391
  445.5 3.8 collective-permute-start.41
  (62 other events, 546.1 us)
Sparse Core Ops, SparseCore 0:
  12.9 66.9 all-gather.2

commit v3 on v2

--- a/solution.py
+++ b/solution.py
@@ -25,17 +25,16 @@
 BACKWARD_BLOCK = 512
 ROW_BLOCK = 512
 LANES = 128
-ENCODE_VMEM = 56
-BACKWARD_VMEM = 56
+VMEM_BYTES = 60 * 2**20
 LAST_PARTS = 3
-PACK_BLOCK = 768
+PACK_BLOCK = 1536
 COST_SHARE = 4
 BF16 = jnp.bfloat16
 F32 = jnp.float32
 
 
-def kernel_params(mebibytes):
-    return pltpu.CompilerParams(vmem_limit_bytes=mebibytes * 2**20)
+def kernel_params():
+    return pltpu.CompilerParams(vmem_limit_bytes=VMEM_BYTES)
 
 
 def dot_nn(a, b):
@@ -55,65 +54,115 @@
     return jax.tree.unflatten(tree, lax.optimization_barrier(tuple(leaves)))
 
 
-def attend_kernel(own_ref, tail_ref, seg_q_ref, seg_k_ref, gain_ref, bias_ref, w_ref, wb_ref, z_ref, q_s, kv_s):
-    rows, width = own_ref.shape
-    gain = gain_ref[...].astype(F32).reshape(1, width)
-    shift = bias_ref[...].astype(F32).reshape(1, width)
-    offsets = wb_ref[...].astype(F32).reshape(1, 3 * width)
-
-    def normed(block):
-        values = block.astype(F32)
-        centred = values - jnp.mean(values, axis=1, keepdims=True)
-        variance = jnp.mean(centred * centred, axis=1, keepdims=True)
-        return (centred * lax.rsqrt(variance + 1e-05) * gain + shift).astype(BF16)
-
-    own = normed(own_ref[...])
-    q_s[...] = (dot_nn(own, w_ref[:, :width]) + offsets[:, :width]).astype(BF16)
-    kv_s[CTX:, :] = (dot_nn(own, w_ref[:, width:]) + offsets[:, width:]).astype(BF16)
-    tail = normed(tail_ref[...])
-    kv_s[:CTX, :] = (dot_nn(tail, w_ref[:, width:]) + offsets[:, width:]).astype(BF16)
-
+def normed(block, gain, shift):
+    values = block.astype(F32)
+    centred = values - jnp.mean(values, axis=1, keepdims=True)
+    variance = jnp.mean(centred * centred, axis=1, keepdims=True)
+    return (centred * lax.rsqrt(variance + 1e-05) * gain + shift).astype(BF16)
+
+
+def project_kernel(rows_ref, gain_ref, bias_ref, w_ref, wb_ref, out_ref, normed_s):
+    width = rows_ref.shape[1]
+
+    @pl.when(pl.program_id(0) == 0)
+    def _():
+        gain = gain_ref[...].astype(F32).reshape(1, width)
+        shift = bias_ref[...].astype(F32).reshape(1, width)
+        normed_s[...] = normed(rows_ref[...], gain, shift)
+
+    out_ref[...] = (dot_nn(normed_s[...], w_ref[...]) + wb_ref[...].astype(F32)).astype(BF16)
+
+
+def project(resid, ln_gain, ln_bias, qkv_weight, qkv_bias):
+    rows, width = resid.shape
+    whole = lambda j: (0, 0)
+    across = lambda j: (0, j)
+    return pl.pallas_call(
+        project_kernel,
+        grid=(3,),
+        in_specs=[
+            pl.BlockSpec((rows, width), whole),
+            pl.BlockSpec((width,), lambda j: (0,)),
+            pl.BlockSpec((width,), lambda j: (0,)),
+            pl.BlockSpec((width, width), across),
+            pl.BlockSpec((1, width), across),
+        ],
+        out_specs=pl.BlockSpec((rows, width), across),
+        out_shape=jax.ShapeDtypeStruct((rows, 3 * width), BF16),
+        scratch_shapes=[pltpu.VMEM((rows, width), BF16)],
+        compiler_params=kernel_params(),
+        cost_estimate=pl.CostEstimate(flops=6 * rows * width * width, bytes_accessed=6 * width * width, transcendentals=0),
+        name="project",
+    )(resid, ln_gain, ln_bias, qkv_weight, qkv_bias[None])
+
+
+def attend_kernel(own_ref, tail_ref, seg_q_ref, seg_k_ref, gain_ref, bias_ref, w_ref, wb_ref, z_ref, w_s, kv_s, sem):
+    rows, width = z_ref.shape
+    load = pltpu.make_async_copy(w_ref.at[:, pl.ds(width, 2 * width)], w_s, sem)
+    load.start()
     lane = lax.broadcasted_iota(jnp.int32, (CTX, 2 * HEAD), 1)
     first_head = lane < HEAD
     place_q = lax.broadcasted_iota(jnp.int32, (CTX, 2 * CTX), 0) + CTX
     place_k = lax.broadcasted_iota(jnp.int32, (CTX, 2 * CTX), 1)
     earlier = place_k <= place_q
-    for block in range(rows // CTX):
+
+    def pairs_of(block, columns):
+        if block > 0:
+            return own_ref[(block - 1) * CTX : (block + 1) * CTX, columns]
+        return jnp.concatenate([kv_s[:, columns.start - width : columns.stop - width], own_ref[:CTX, columns]], axis=0)
+
+    for block in (*range(1, rows // CTX), 0):
+        if block == 0:
+            load.wait()
+            gain = gain_ref[...].astype(F32).reshape(1, width)
+            shift = bias_ref[...].astype(F32).reshape(1, width)
+            offsets = wb_ref[...].astype(F32).reshape(1, 3 * width)
+            tail = normed(tail_ref[...], gain, shift)
+            kv_s[...] = (dot_nn(tail, w_s[...]) + offsets[:, width:]).astype(BF16)
         base = block * CTX
         seg_q = seg_q_ref[base : base + CTX, :]
         allowed = (jnp.concatenate([seg_q, seg_q], axis=1) == seg_k_ref[:, base : base + 2 * CTX]) & earlier
-        for pair in range(width // (2 * HEAD)):
-            columns = slice(pair * 2 * HEAD, (pair + 1) * 2 * HEAD)
-            query = q_s[base : base + CTX, columns]
-            keys = kv_s[base : base + 2 * CTX, columns]
-            values = kv_s[base : base + 2 * CTX, width + pair * 2 * HEAD : width + (pair + 1) * 2 * HEAD]
-            mixed = []
-            for half in range(2):
-                mine = first_head if half == 0 else ~first_head
-                part = jnp.where(mine, query, jnp.zeros_like(query))
-                scores = dot_nt(part, keys) * (1.0 / math.sqrt(HEAD))
-                scores = jnp.where(allowed, scores, -1e30)
-                expo = jnp.exp(scores - jnp.max(scores, axis=1, keepdims=True))
-                probs = (expo / jnp.sum(expo, axis=1, keepdims=True)).astype(BF16)
-                mixed.append(dot_nn(probs, values))
-            z_ref[base : base + CTX, columns] = jnp.where(first_head, mixed[0], mixed[1]).astype(BF16)
-
-
-def attend(resid, tail, seg_q, seg_k, ln_gain, ln_bias, qkv_weight, qkv_bias):
-    rows, width = resid.shape
+        allowed = jnp.concatenate([allowed, allowed], axis=0)
+        starts = range(0, width, 2 * HEAD)
+        scores = []
+        for start in starts:
+            query = own_ref[base : base + CTX, start : start + 2 * HEAD]
+            keys = pairs_of(block, slice(width + start, width + start + 2 * HEAD))
+            none = jnp.zeros_like(query)
+            query = query * jnp.asarray(1.0 / math.sqrt(HEAD), BF16)
+            query = jnp.concatenate([jnp.where(first_head, query, none), jnp.where(first_head, none, query)], axis=0)
+            scores.append(dot_nt(query, keys))
+        probs = []
+        for part in scores:
+            part = jnp.where(allowed, part, -1e30)
+            expo = jnp.exp(part - jnp.max(part, axis=1, keepdims=True))
+            probs.append((expo * (1.0 / jnp.sum(expo, axis=1, keepdims=True))).astype(BF16))
+        for start, part in zip(starts, probs):
+            values = pairs_of(block, slice(2 * width + start, 2 * width + start + 2 * HEAD))
+            mixed = dot_nn(part, values)
+            z_ref[base : base + CTX, start : start + 2 * HEAD] = jnp.where(first_head, mixed[:CTX], mixed[CTX:]).astype(BF16)
+
+
+def attend(projected, tail, seg_q, seg_k, ln_gain, ln_bias, qkv_weight, qkv_bias):
+    rows = projected.shape[0]
+    width = tail.shape[1]
+    vmem = pl.BlockSpec(memory_space=pltpu.VMEM)
     return pl.pallas_call(
         attend_kernel,
+        in_specs=[vmem] * 6 + [pl.BlockSpec(memory_space=pl.ANY), vmem],
+        out_specs=vmem,
         out_shape=jax.ShapeDtypeStruct((rows, width), BF16),
         scratch_shapes=[
-            pltpu.VMEM((rows, width), BF16),
-            pltpu.VMEM((rows + CTX, 2 * width), BF16),
+            pltpu.VMEM((width, 2 * width), BF16),
+            pltpu.VMEM((CTX, 2 * width), BF16),
+            pltpu.SemaphoreType.DMA,
         ],
-        compiler_params=kernel_params(32),
+        compiler_params=kernel_params(),
         cost_estimate=pl.CostEstimate(
-            flops=8 * rows * width * width, bytes_accessed=6 * width * width, transcendentals=rows * 2 * CTX * 12
+            flops=4 * rows * width * width, bytes_accessed=8 * width * width, transcendentals=rows * 2 * CTX * 12
         ),
         name="attend",
-    )(resid, tail, seg_q, seg_k, ln_gain, ln_bias, qkv_weight, qkv_bias)
+    )(projected, tail, seg_q, seg_k, ln_gain, ln_bias, qkv_weight, qkv_bias)
 
 
 def packed_kernel(enc_ref, dec_ref, out_ref):
@@ -131,7 +180,7 @@
         in_specs=[pl.BlockSpec((rows, block), across)] * 2,
         out_specs=pl.BlockSpec((2, rows, block), lambda j: (0, 0, j)),
         out_shape=jax.ShapeDtypeStruct((2, rows, columns), BF16),
-        compiler_params=kernel_params(16),
+        compiler_params=kernel_params(),
         cost_estimate=pl.CostEstimate(flops=0, bytes_accessed=12 * rows * columns, transcendentals=0),
         name="packed",
     )(enc, dec)
@@ -229,7 +278,7 @@
         + [jax.ShapeDtypeStruct((1, features), F32)] * 2
         + [jax.ShapeDtypeStruct((1, width), F32)],
         scratch_shapes=[pltpu.VMEM((s, width), F32) for s in sizes] if rounded else [],
-        compiler_params=kernel_params(ENCODE_VMEM),
+        compiler_params=kernel_params(),
         cost_estimate=pl.CostEstimate(
             flops=4 * tokens * width * features // COST_SHARE,
             bytes_accessed=2 * (2 * width * features + tokens * (features + 4 * width)) // COST_SHARE,
@@ -238,6 +287,69 @@
         name="encode",
     )(*pieces, keep_wide, weights, bias, weights)
     return outs[0], outs[1 : 1 + len(pieces)], outs[-3:]
+
+
+def joined_kernel(right_ref, left_ref, from_right_ref, from_left_ref, right_out, left_out):
+    rows = right_ref.shape[0]
+    right_out[:rows, :] = (from_right_ref[:rows, :] + right_ref[...].astype(F32)).astype(BF16)
+    right_out[rows:, :] = from_right_ref[rows:, :].astype(BF16)
+    left_out[:rows, :] = from_left_ref[:rows, :].astype(BF16)
+    left_out[rows:, :] = (from_left_ref[rows:, :] + left_ref[...].astype(F32)).astype(BF16)
+
+
+def joined(right, left, from_right, from_left):
+    shape = jax.ShapeDtypeStruct(from_right.shape, BF16)
+    return pl.pallas_call(
+        joined_kernel, out_shape=[shape, shape], compiler_params=kernel_params(), name="joined"
+    )(right, left, from_right, from_left)
+
+
+def compared_kernel(rec_ref, right_ref, left_ref, z_ref, bias_ref, keep_ref, totals_ref, norm_ref, grad_ref, fit_ref, scaled_ref, penalty_ref, counted_ref):
+    rows, width = z_ref.shape
+    squares = jnp.sum(totals_ref[0:1, :], keepdims=True)
+    counted = jnp.sum(totals_ref[1:2, :], keepdims=True)
+    mean_square = squares / (counted * width) + 1e-06
+    unit = 2.0 / (width * mean_square * counted)
+    share = LAMBDA / counted
+    norms = norm_ref[...]
+    scaled_ref[...] = share * norms
+    penalty_ref[...] = share / norms
+    counted_ref[...] = counted + jnp.zeros(counted_ref.shape, F32)
+    residue = rec_ref[...] + right_ref[...].astype(F32) + left_ref[...].astype(F32) + bias_ref[...] - z_ref[...].astype(F32)
+    kept = wide(keep_ref[...], width) * residue
+    grad_ref[...] = (kept * unit).astype(BF16)
+    fit = jnp.sum((kept * residue).reshape(rows // 8, 8, width), axis=0)
+    fit_ref[...] = sum(fit[:, at : at + LANES] for at in range(0, width, LANES)) / (width * mean_square)
+
+
+def compared(rec, right, left, tokens_z, dec_bias, keep_wide, keep_at, totals, row_norm):
+    rows, width = tokens_z.shape
+    features = row_norm.shape[1]
+    whole = lambda j: (0, 0)
+    own = pl.BlockSpec((rows, width), whole)
+    line = pl.BlockSpec((1, features), whole)
+    tile = pl.BlockSpec((8, LANES), whole)
+    return pl.pallas_call(
+        compared_kernel,
+        grid=(1,),
+        in_specs=[own] * 4
+        + [
+            pl.BlockSpec((1, width), whole),
+            pl.BlockSpec((rows, LANES), lambda j: (keep_at // rows, 0)),
+            pl.BlockSpec(totals.shape, whole),
+            line,
+        ],
+        out_specs=[own, tile, line, line, tile],
+        out_shape=[
+            jax.ShapeDtypeStruct((rows, width), BF16),
+            jax.ShapeDtypeStruct((8, LANES), F32),
+            jax.ShapeDtypeStruct((1, features), F32),
+            jax.ShapeDtypeStruct((1, features), F32),
+            jax.ShapeDtypeStruct((8, LANES), F32),
+        ],
+        compiler_params=kernel_params(),
+        name="compared",
+    )(rec, right, left, tokens_z, dec_bias, keep_wide, totals, row_norm)
 
 
 def backward_kernel(groups, carried, parted, *refs):
@@ -318,7 +430,7 @@
 
             @pl.when(away % 2 == 1)
             def _():
-                send_out[pl.ds(half, 1), matrix] = piece[None]
+                send_out[pl.ds(half, 1), matrix] = piece[None].astype(send_out.dtype)
 
 
 def backward(groups, keep_wide, norm_scaled, weights, carried, first, wide_by, parted, me):
@@ -349,7 +461,7 @@
     if parted:
         shape = (parted // 2, 2, width // parted, wide_by)
         block = pl.BlockSpec((parted // 2, 2, width // parted, fb), lambda j, *_: (0, 0, 0, j))
-        out_shape = [jax.ShapeDtypeStruct(shape, F32)] * 2
+        out_shape = [jax.ShapeDtypeStruct(shape, F32), jax.ShapeDtypeStruct(shape, BF16)]
         out_specs = [block] * 2
     else:
         out_shape = [jax.ShapeDtypeStruct((width, wide_by), F32)] * 2
@@ -366,7 +478,7 @@
             scratch_shapes=[pltpu.VMEM((tokens, fb), BF16)],
         ),
         out_shape=out_shape,
-        compiler_params=kernel_params(BACKWARD_VMEM),
+        compiler_params=kernel_params(),
         cost_estimate=pl.CostEstimate(
             flops=6 * tokens * width * wide_by // COST_SHARE,
             bytes_accessed=(2 * tokens * wide_by + 16 * width * wide_by) // COST_SHARE,
@@ -376,6 +488,53 @@
     )(*([me] if parted else []), *operands)
 
 
+def finished_kernel(arrived_count, first, kept_ref, paired_ref, *refs):
+    arrived, (penalty_ref, low_ref), rest = refs[:arrived_count], refs[arrived_count : arrived_count + 2], refs[arrived_count + 2 :]
+    enc_ref, dec_ref, norm_ref = rest if first else rest[2:]
+    grad = kept_ref[...] + paired_ref[...].astype(F32)
+    for block in arrived:
+        grad = grad + block[...].astype(F32)
+    enc, dec = grad[0], grad[1] + penalty_ref[...] * low_ref[...].astype(F32)
+    enc_ref[...] = enc
+    dec_ref[...] = dec
+    squares = enc * enc + dec * dec
+    total = jnp.sum(squares.reshape(-1, 8, squares.shape[1]), axis=0)
+    lanes = sum(total[:, at : at + LANES] for at in range(0, total.shape[1], LANES))
+
+    @pl.when(pl.program_id(0) == 0)
+    def _():
+        norm_ref[...] = jnp.zeros_like(norm_ref)
+
+    norm_ref[:8, :] += lanes
+
+
+def finished(kept, paired, arrived, penalty, both, grads, part):
+    _, _, rows, wide_by = kept.shape
+    features = both.shape[2]
+    fb = BACKWARD_BLOCK
+    start = part * wide_by // fb
+    own = pl.BlockSpec((None, 2, rows, fb), lambda j: (0, 0, 0, j))
+    along = pl.BlockSpec((2, rows, fb), lambda j: (0, 0, j))
+    first = grads is None
+    return pl.pallas_call(
+        functools.partial(finished_kernel, len(arrived), first),
+        grid=(wide_by // fb,),
+        in_specs=[own, own]
+        + [along] * len(arrived)
+        + [
+            pl.BlockSpec((1, fb), lambda j: (0, j + start)),
+            pl.BlockSpec((None, rows, fb), lambda j: (1, 0, j + start)),
+        ]
+        + ([] if first else [pl.BlockSpec(memory_space=pl.ANY)] * 2),
+        out_specs=[pl.BlockSpec((rows, fb), lambda j: (0, j + start))] * 2 + [pl.BlockSpec((16, LANES), lambda j: (0, 0))],
+        out_shape=[jax.ShapeDtypeStruct((rows, features), F32)] * 2 + [jax.ShapeDtypeStruct((16, LANES), F32)],
+        input_output_aliases={} if first else {4 + len(arrived): 0, 5 + len(arrived): 1},
+        compiler_params=kernel_params(),
+        cost_estimate=pl.CostEstimate(flops=0, bytes_accessed=24 * rows * wide_by, transcendentals=0),
+        name="finished",
+    )(kept, paired, *arrived, penalty, both, *([] if first else grads))
+
+
 def ring_order(count):
     return list(range(0, count, 2)) + list(range(1, count, 2))[::-1]
 
@@ -393,9 +552,14 @@
 
 def summed(block, axes):
     for axis in axes:
-        bit = 1
-        while bit < lax.axis_size(axis):
-            block = block + swapped(block, axis, bit)
+        size, bit = lax.axis_size(axis), 1
+        while bit < size:
+            if axis == "feat" and 4 * bit == size:
+                first, second, third = (swapped(block, axis, bit * i) for i in (1, 2, 3))
+                block = (block + first) + (second + third)
+                bit *= 2
+            else:
+                block = block + swapped(block, axis, bit)
             bit *= 2
     return block
 
@@ -450,11 +614,12 @@
     seg_wide = jnp.broadcast_to(own_seg[:, None], (own_rows, LANES))
     both = packed(enc_weight, dec_weight.T)
     weights = lax.all_gather(both, "dp")
-    tail = lax.ppermute(resid[own_rows - CTX :], "feat", [(i, i + 1) for i in range(feat_size - 1)])
-    tail, key_seg, seg_wide, both = together(tail, key_seg, seg_wide, both)
-    tokens_z = attend(resid, tail, seg_wide, key_seg, ln_gain, ln_bias, qkv_weight, qkv_bias)
-
+    tail = lax.ppermute(resid[own_rows - CTX :], "feat", [(i, (i + 1) % feat_size) for i in range(feat_size)])
+    projected = project(resid, ln_gain, ln_bias, qkv_weight, qkv_bias)
+    tail, key_seg, seg_wide, both, projected = together(tail, key_seg, seg_wide, both, projected)
+    tokens_z = attend(projected, tail, seg_wide, key_seg, ln_gain, ln_bias, qkv_weight, qkv_bias)
     tokens_z, keep = together(tokens_z, keep)
+
     z_stages = [[tokens_z]]
     right, left = tokens_z, tokens_z
     rows = own_rows // 2
@@ -471,81 +636,88 @@
             owners = order[(place + jnp.asarray(hops, jnp.int32)) % feat_size]
             keep_ring = keep_mask.reshape(feat_size, own_rows)[owners].reshape(group)
             keep_wide = jnp.broadcast_to(keep_ring[:, None], (group, LANES))
-            own_keep = keep_ring[group - 2 * own_rows : group - own_rows][:, None]
-            keep_total = jnp.sum(keep_mask)
-            right, left, keep_wide, own_keep, keep_total = together(right, left, keep_wide, own_keep, keep_total)
+            keep_total = jnp.pad(jnp.sum(keep_mask.reshape(-1, LANES), axis=0), (0, width - LANES))[None]
+            right, left, keep_wide, keep_total = together(right, left, keep_wide, keep_total)
         elif hop < half - 1:
             right, left = together(right, left)
         z_stages.append([right, left])
-    right, left, weights = together(right, left, weights)
+    dec_float = weights[:, 1].astype(F32)
+    row_norm = jnp.sqrt(jnp.sum(dec_float * dec_float, axis=(0, 1)))[None]
+    near_squares = 0.0
+    for hop in range(half - 1):
+        for at, piece in enumerate(z_stages[hop]):
+            first = group - 2 * own_rows if hop == 0 else (2 * (hop - 1) + at) * own_rows
+            kept = keep_wide[first : first + own_rows, :1] * piece.astype(F32) ** 2
+            near_squares = near_squares + jnp.sum(kept, axis=0, keepdims=True)
+    right, left, weights, row_norm, near_squares = together(right, left, weights, row_norm, near_squares)
     z_stages[half - 1] = [right, left]
     keep_at = [group - 2 * own_rows] + [2 * (hop - 1) * own_rows for hop in range(1, half)] + [group - own_rows]
-    z_float = tokens_z.astype(F32)
     acts, recs, stats = [None] * (half + 1), [None] * (half + 1), [None] * (half + 1)
     bias_row = enc_bias[None]
 
-    def encoded(hop):
-        acts[hop], recs[hop], stats[hop] = encode(
-            z_stages[hop], keep_wide, keep_at[hop], weights, bias_row, hop == half
-        )
+    def encoded(hop, pieces=slice(None)):
+        chosen = z_stages[hop][pieces]
+        at = keep_at[hop] + (own_rows if pieces == slice(1, 2) else 0)
+        act, rec, stat = encode(chosen, keep_wide, at, weights, bias_row, hop == half)
+        if pieces == slice(1, 2):
+            act, rec, stat = [*acts[hop], act], [*recs[hop], *rec], [a + b for a, b in zip(stats[hop], stat)]
+        elif pieces == slice(0, 1):
+            act = [act]
+        acts[hop], recs[hop], stats[hop] = act, list(rec), stat
 
     z_stages.append([ring_shift(right[:rows], 1), ring_shift(left[rows:], -1)])
-    encoded(half - 1)
+    encoded(half - 1, slice(0, 1))
     z_stages[half], recs[half - 1], acts[half - 1] = together(z_stages[half], recs[half - 1], acts[half - 1])
     encoded(half)
 
-    recs[half], weights = together(recs[half], weights)
+    recs[half], weights, z_stages[half - 1] = together(recs[half], weights, z_stages[half - 1])
     right, left = recs[half]
     for step in range(1, half + 1):
         right, left = ring_shift(right, 1), ring_shift(left, -1)
         if step == 1:
-            dec_float = weights[:, 1].astype(F32)
-            row_norm = jnp.sqrt(jnp.sum(dec_float * dec_float, axis=(0, 1)))[None]
-            right, left, row_norm, z_stages[half - 2] = together(right, left, row_norm, z_stages[half - 2])
+            encoded(half - 1, slice(1, 2))
+            far_squares = [stats[half - 1][2], stats[half][2]]
+            right, left, recs[half - 1], acts[half - 1], far_squares = together(
+                right, left, recs[half - 1], acts[half - 1], far_squares
+            )
         elif step < half:
             hop = half - step
             encoded(hop)
-            right, left, recs[hop], acts[hop], z_stages[hop - 1] = together(
-                right, left, recs[hop], acts[hop], z_stages[hop - 1]
-            )
+            if step == 2:
+                totals = jnp.concatenate([near_squares + far_squares[0] + far_squares[1], keep_total])
+                totals = summed(totals, ("dp",))
+            right, left, recs[hop], acts[hop], totals = together(right, left, recs[hop], acts[hop], totals)
         else:
             encoded(0)
-            act_sum, fire_sum, square_sum = (sum(parts) for parts in zip(*stats))
-            totals = jnp.stack([keep_total, jnp.sum(square_sum)])
-            totals = jnp.pad(totals, (0, fire_sum.shape[1] - 2))[None]
-            fired, act_total, totals = summed(jnp.concatenate([fire_sum, act_sum, totals]), ("dp",))
-            counted, squares = totals[0], totals[1]
-            mean_square = squares / (counted * width) + 1e-06
-            unit = 2.0 / (width * mean_square * counted)
-            norm_scaled = LAMBDA / counted * row_norm
-            loss_part = LAMBDA * jnp.sum(act_sum * row_norm)
-            penalty = (LAMBDA / counted) * act_total / row_norm[0]
-            right, left, recs[0], acts[0], unit, norm_scaled, loss_part, penalty, fired = together(
-                right, left, recs[0], acts[0], unit, norm_scaled, loss_part, penalty, fired
-            )
+            right, left, recs[0], acts[0], stats = together(right, left, recs[0], acts[0], stats)
             break
         from_left, from_right = recs[half - step]
-        right, left = right.astype(F32), left.astype(F32)
         if step == 1:
-            right = jnp.concatenate([from_right[:rows] + right, from_right[rows:]])
-            left = jnp.concatenate([from_left[:rows], from_left[rows:] + left])
+            right, left = joined(right, left, from_right, from_left)
         else:
-            right, left = from_right + right, from_left + left
-        right, left = right.astype(BF16), left.astype(BF16)
-    residue = recs[0][0] + right.astype(F32) + left.astype(F32) + dec_bias - z_float
-    grad_out = own_keep * residue * unit
-    fit_part = jnp.sum(own_keep * residue * residue) / (width * mean_square)
-    loss_part = fit_part + loss_part
-    own_grad = grad_out.astype(BF16)
-    own_grad, loss_part = together(own_grad, loss_part)
-
-    bias_share = out_bias_share = 0.0
+            right = (from_right + right.astype(F32)).astype(BF16)
+            left = (from_left + left.astype(F32)).astype(BF16)
+        following = half - step - 1
+        right, left, z_stages[following] = together(right, left, z_stages[following])
+    own_grad, fit_part, norm_scaled, penalty_scale, counted = compared(
+        recs[0][0], right, left, tokens_z, dec_bias[None], keep_wide, keep_at[0], totals, row_norm
+    )
+    own_grad, fit_part, norm_scaled = together(own_grad, fit_part, norm_scaled)
+
+    bias_shares, out_bias_shares = [], []
     carried = None
     grad_stages = [[own_grad]]
     right, left = own_grad, own_grad
 
     def group_of(plan):
-        return [(acts[hop], z_stages[hop], grad_stages[hop], keep_at[hop]) for hop in plan]
+        groups = []
+        for hop in plan:
+            zs, gs, at = z_stages[hop], grad_stages[hop], keep_at[hop]
+            if isinstance(acts[hop], list):
+                groups += [(act, [z], [g], at + i * own_rows) for i, (act, z, g) in enumerate(zip(acts[hop], zs, gs))]
+            else:
+                groups.append((acts[hop], zs, gs, at))
+        return groups
 
     for hop in range(1, half + 1):
         if hop == half:
@@ -555,68 +727,84 @@
             *carried, bias_grad, out_bias_grad = backward(
                 group_of([hop - 1]), keep_wide, norm_scaled, weights, carried, 0, features, 0, None
             )
-            bias_share, out_bias_share = bias_share + bias_grad, out_bias_share + out_bias_grad
-        right, left, carried, bias_share, out_bias_share = together(right, left, carried, bias_share, out_bias_share)
+            bias_shares.append(bias_grad)
+            out_bias_shares.append(out_bias_grad)
+        right, left, carried = together(right, left, carried)
         grad_stages.append([right, left])
 
     wide_by = features // LAST_PARTS
-    kept, sent, aways, owns, last_bias = [], [], [], [], []
-    scaled = norm_scaled
-    for turn in range(LAST_PARTS + 2):
-        coming = []
+    kept, paired, arrived, last_bias = [], [], [], []
+    grads = None
+
+    def crossed(part):
+        away = [kept[part][i] + paired[part][i].astype(F32) for i in range(1, dp_size // 2)]
+        return [swapped(block.astype(BF16), "dp", 2 * i + 2) for i, block in enumerate(away)]
+
+    def rest_of(block):
+        for bit in range(2, dp_size, 2):
+            if bit & (bit - 1) == 0:
+                block = block + swapped(block, "dp", bit)
+        return block
+
+    act_sum, fire_sum, _ = (sum(parts) for parts in zip(*stats))
+    counts = jnp.concatenate([fire_sum, act_sum])
+    loss_share = LAMBDA * jnp.sum(act_sum * row_norm)
+    sent = []
+    for turn in range(LAST_PARTS):
         if turn >= 2:
-            away = aways[turn - 2]
-            coming.append([swapped(block, "dp", 2 * other + 2) for other, block in enumerate(away)])
-        else:
-            coming.append([])
-        coming.append(swapped(sent[turn - 1], "dp", 1) if 1 <= turn <= LAST_PARTS else None)
-        if turn < LAST_PARTS:
-            keep_part, send_part, bias_grad, out_bias_grad = backward(
-                group_of([half - 1, half]), keep_wide, scaled, weights, carried, turn * wide_by, wide_by, dp_size, me
-            )
-            kept.append(keep_part)
-            sent.append(send_part)
-            last_bias.append(bias_grad)
-        if turn == LAST_PARTS:
-            bias_share = jnp.concatenate(
-                [bias_share + jnp.concatenate(last_bias, axis=1), out_bias_share + out_bias_grad], axis=1
-            )
-            bias_share = summed(bias_share, ("dp",))[0]
-        coming, scaled, sent, kept, bias_share = together(coming, scaled, sent, kept, bias_share)
-        arrived, paired = coming
-        if turn >= 2:
-            owns[turn - 2] = owns[turn - 2] + sum(block.astype(F32) for block in arrived)
-        if paired is not None:
-            total = kept[turn - 1] + paired
-            owns.append(total[0])
-            aways.append([total[other].astype(BF16) for other in range(1, dp_size // 2)])
-    enc_bias_grad, dec_bias_grad = bias_share[:features], bias_share[features:]
-    own_dec = dec_weight.astype(BF16).astype(F32)
-    own_squares = 0.0
-    enc_grads, dec_grads = [], []
-    for part in range(LAST_PARTS):
-        span = slice(part * wide_by, (part + 1) * wide_by)
-        enc_grads.append(owns[part][0])
-        dec_grads.append(owns[part][1].T + penalty[span, None] * own_dec[span])
-        own_squares = own_squares + jnp.sum(enc_grads[part] ** 2) + jnp.sum(dec_grads[part] ** 2)
-    enc_grad = jnp.concatenate(enc_grads, axis=1)
-    dec_grad = jnp.concatenate(dec_grads, axis=0)
-
+            arrived.append(crossed(turn - 2))
+        if turn == 2:
+            counts = rest_of(counts)
+        if turn >= 1:
+            paired.append(swapped(sent[turn - 1], "dp", 1))
+        if turn == 1:
+            counts = counts + swapped(counts, "dp", 1)
+        keep_part, send_part, bias_grad, out_bias_grad = backward(
+            group_of([half - 1, half]), keep_wide, norm_scaled, weights, carried, turn * wide_by, wide_by, dp_size, me
+        )
+        kept.append(keep_part)
+        sent.append(send_part)
+        last_bias.append(bias_grad)
+        arrived, paired, norm_scaled, sent, kept, last_bias, counts, loss_share = together(
+            arrived, paired, norm_scaled, sent, kept, last_bias, counts, loss_share
+        )
+    fired, act_total = counts[0], counts[1:]
+    penalty = penalty_scale * act_total
+    arrived.append(crossed(LAST_PARTS - 2))
+    paired.append(swapped(sent[-1], "dp", 1))
+    arrived.append(crossed(LAST_PARTS - 1))
+    bias_share = sum(bias_shares) + jnp.concatenate(last_bias, axis=1)
+    out_bias_share = jnp.pad(sum(out_bias_shares) + out_bias_grad, ((0, 0), (0, features - width)))
+    shares = jnp.concatenate([bias_share, out_bias_share])
+    shares = rest_of(shares + swapped(shares, "dp", 1))
+    enc_bias_grad, dec_bias_grad = shares[0], shares[1, :width]
     first_dp = dp_at == 0
     first_both = first_dp & (feat_at == 0)
-    own_squares = own_squares + jnp.where(first_dp, jnp.sum(enc_bias_grad * enc_bias_grad), 0.0)
-    own_squares = own_squares + jnp.where(first_both, jnp.sum(dec_bias_grad * dec_bias_grad), 0.0)
-    total_squares, loss_total = summed(jnp.stack([own_squares, loss_part]), everywhere)
-    overall_derivative_length = jnp.sqrt(total_squares)
+    bias_squares = jnp.where(first_dp, jnp.sum(enc_bias_grad * enc_bias_grad), 0.0)
+    bias_squares = bias_squares + jnp.where(first_both, jnp.sum(dec_bias_grad * dec_bias_grad), 0.0)
+    row = lax.broadcasted_iota(jnp.int32, (16, LANES), 0)
+    column = lax.broadcasted_iota(jnp.int32, (16, LANES), 1)
+    norms = jnp.where((row == 0) & (column == 0), bias_squares, 0.0)
+    norms = norms + jnp.where((row == 8) & (column == 0), loss_share, 0.0)
+    norms = norms + jnp.pad(fit_part, ((8, 0), (0, 0)))
+    for part in range(LAST_PARTS):
+        *grads, part_norms = finished(kept[part], paired[part], arrived[part], penalty, both, grads, part)
+        norms = norms + part_norms
+
+    norms = summed(norms, everywhere)
+    loss_total = jnp.sum(norms[8:])
+    overall_derivative_length = jnp.sqrt(jnp.sum(norms[:8]))
     factor = jnp.minimum(1.0, CLIP_NORM / (overall_derivative_length + 1e-06))
-    dec_new, dec_m, dec_v = adamw(dec_weight, dec_grad * factor, dec_weight_m, dec_weight_v, DECAY)
-    row_squares = summed(jnp.sum(dec_new * dec_new, axis=1), ("dp",))
-    enc_new, enc_m, enc_v = adamw(enc_weight, enc_grad * factor, enc_weight_m, enc_weight_v, DECAY)
+    dec_new, dec_m, dec_v = adamw(dec_weight.T, grads[1] * factor, dec_weight_m.T, dec_weight_v.T, DECAY)
+    row_squares = jnp.sum(dec_new * dec_new, axis=0, keepdims=True)
+    row_squares = summed(row_squares, ("dp",))
+    enc_new, enc_m, enc_v = adamw(enc_weight, grads[0] * factor, enc_weight_m, enc_weight_v, DECAY)
     bias_new, bias_m, bias_v = adamw(enc_bias, enc_bias_grad * factor, enc_bias_m, enc_bias_v, 0.0)
     out_new, out_m, out_v = adamw(dec_bias, dec_bias_grad * factor, dec_bias_m, dec_bias_v, 0.0)
-    dec_new = dec_new * lax.rsqrt(row_squares + 1e-12)[:, None]
+    dec_new = (dec_new * lax.rsqrt(row_squares + 1e-12)).T
+    dec_m, dec_v = dec_m.T, dec_v.T
     return (
-        jnp.stack([loss_total, counted]),
+        jnp.stack([loss_total, counted[0, 0]]),
         overall_derivative_length,
         fired,
         enc_new,

time: 466 us -> 435 us (0.933)
  waiting for transfers between devices: 135 us -> 93.6 us
  Pallas kernels: 187 us -> 219 us
  other arithmetic: 51.6 us -> 39.9 us
  between operations: 26.7 us -> 19.4 us
  local copies, waits for them, and re-layouts: 18 us -> 12.4 us
    ppermute x24, waiting for transfers between devices: 80.6 us -> 51.6 us  [ring_shift(): return lax.ppermute(block, 'feat', route)]
    pallas_call x1 -> x7, Pallas kernels: 5.94 us -> 30.3 us  [the longest x3 9.48 us: finished(): pl.pallas_call(functools.partial(finished_kernel, len(arrived), first), g...]
    ppermute x17 -> x20, waiting for transfers between devices: 50.6 us -> 37.2 us  [swapped(): lax.ppermute(block, axis, [(i, i ^ bit) for i in range(lax.axis_size(axis...]
    add x12 -> x14, other arithmetic: 13.7 us -> 3.07 us  [the longest x1 0.78 us: shards(): norms = norms + part_norms]
    pallas_call x5 -> x6, Pallas kernels: 76 us -> 83.3 us  [encode(): pl.pallas_call(functools.partial(encode_kernel, len(pieces), rounded), gr...]
    unnamed x135 -> x143, local copies, waits for them, and re-layouts: 10.9 us -> 4.59 us
    ppermute x17 -> x20, starting transfers between devices: 8.83 us -> 14.2 us  [swapped(): lax.ppermute(block, axis, [(i, i ^ bit) for i in range(lax.axis_size(axis...]
    reduce_sum x9 -> x7, other arithmetic: 16.6 us -> 11.2 us  [the longest x1 7.41 us: shards(): row_squares = jnp.sum(dec_new * dec_new, axis=0, keepdims=True)]
  transfers between devices with their start and end apart: 43 -> 46, of which waited for: 23 -> 24; matrix products, arithmetic and copies ran while one was open for 8% -> 8% of each run, Pallas kernels for 32% -> 42%
where the time goes in v3:
time: 435 us; the launch traced here: 428 us
  Pallas kernels  219 us (50%)
  waiting for transfers between devices  93.6 us (22%)
  starting transfers between devices  42.9 us (10%)
  other arithmetic  39.9 us (9%)
  between operations  19.4 us (4%)
  local copies, waits for them, and re-layouts  12.4 us (3%)
    pallas_call x6, Pallas kernels, backward(): pl.pallas_call(functools.partial(backward_kernel, counts, carried is not...  102 us
    pallas_call x6, Pallas kernels, encode(): pl.pallas_call(functools.partial(encode_kernel, len(pieces), rounded), gr...  83.3 us
    ppermute x24, waiting for transfers between devices, ring_shift(): return lax.ppermute(block, 'feat', route)  51.6 us
    ppermute x20, waiting for transfers between devices, swapped(): lax.ppermute(block, axis, [(i, i ^ bit) for i in range(lax.axis_size(axis...  37.2 us
    ppermute x24, starting transfers between devices, ring_shift(): return lax.ppermute(block, 'feat', route)  25.6 us
    ppermute x20, starting transfers between devices, swapped(): lax.ppermute(block, axis, [(i, i ^ bit) for i in range(lax.axis_size(axis...  14.2 us
    pallas_call x3, Pallas kernels, finished(): pl.pallas_call(functools.partial(finished_kernel, len(arrived), first), g...  9.48 us
  transfers between devices with their start and end apart: 46, of which 24 were waited for; matrix products, arithmetic and copies ran while one was open for 8% of the time, Pallas kernels for 42%

profile of v3, /device:TPU:0, one launch (start us, length us, event | category | flops | bytes accessed | tf_op | source)
XLA Modules:
  0.0 427.5 jit_solution(8409246273981881900)
XLA Ops:
  7.2 3.5 packed.1.refs_2_
  11.7 3.0 collective-permute-start
  16.0 6.2 %project.1.own_ref = bf16[512,2304]{1,0:T(8,128)(2,1)} custom-call(bf16[512,768]{1,0:T(8,128)(2,1)} %rows_ref.1, bf16[768]{0:T(1024)(128)(2,1)} %gain_ref.3, bf16[768]{0:T(1024)(128)(2,1)} %bias_ref.3, bf16[768,2304]{1,0:T(8,128)(2,1)} %w_ref.3, bf16[1,2304]{1,0:T(2,128)(2,1)} %broadcast_in_dim.60.wb_ref), custom_call_target="tpu_custom_call" | custom-call | flops 1811939328 | bytes 3538944 | tf_op jit(solution)/shard_map/project/pallas_call | solution.py:80
  23.5 6.8 %attend.1.refs_0_.z_ref.refs_1_ = bf16[512,768]{1,0:T(8,128)(2,1)} custom-call(bf16[512,2304]{1,0:T(8,128)(2,1)} %project.1.own_ref, bf16[128,768]{1,0:T(8,128)(2,1)} %copy-done.34, s32[512,128]{1,0:T(8,128)} %broadcast_in_dim.59.seg_q_ref, s32[1,640]{1,0:T(1,128)} %broadcast_in_dim.58.seg_k_ref, bf16[768]{0:T(1024)(128)(2,1)} %gain_ref.3, ...), custom_call_target="tpu_custom_call" | custom-call | flops 1207959552 | bytes 4718592 | tf_op jit(solution)/shard_map/attend/pallas_call | solution.py:150
  33.8 15.4 %collective-permute-done.2.refs_1_.refs_2_ = bf16[512,768]{1,0:T(8,128)(2,1)S(1)} collective-permute-done((bf16[512,768]{1,0:T(8,128)(2,1)}, bf16[512,768]{1,0:T(8,128)(2,1)S(1)}, u32[]{:S(2)}, u32[]{:S(2)}) %collective-permute-start.2) | collective-permute-done | bytes 786464 | tf_op jit(solution)/shard_map/ppermute | solution.py:546
  54.3 14.9 %collective-permute-done.3.refs_0_.refs_1_ = bf16[512,768]{1,0:T(8,128)(2,1)} collective-permute-done((bf16[512,768]{1,0:T(8,128)(2,1)S(1)}, bf16[512,768]{1,0:T(8,128)(2,1)}, u32[]{:S(2)}, u32[]{:S(2)}) %collective-permute-start.3) | collective-permute-done | bytes 786464 | tf_op jit(solution)/shard_map/ppermute | solution.py:546
  71.5 1.8 multiply_reduce_fusion.2
  73.4 4.4 %all-gather.3.cloned.1.call-done = bf16[8,192,3072]{2,1,0:T(8,128)(2,1)} async-done(((bf16[2,192,3072]{2,1,0:T(8,128)(2,1)}), bf16[8,192,3072]{2,1,0:T(8,128)(2,1)}) %all-gather.3.cloned.1.call-update) | async-done | bytes 9437200 | tf_op jit(solution)/shard_map/all_gather | solution.py:616
  77.8 3.3 multiply_reduce_fusion
  81.8 5.0 %collective-permute-done.5.refs_0_.refs_2_ = bf16[512,768]{1,0:T(8,128)(2,1)S(1)} collective-permute-done((bf16[512,768]{1,0:T(8,128)(2,1)}, bf16[512,768]{1,0:T(8,128)(2,1)S(1)}, u32[]{:S(2)}, u32[]{:S(2)}) %collective-permute-start.5) | collective-permute-done | bytes 786464 | tf_op jit(solution)/shard_map/ppermute | solution.py:546
  87.7 1.7 collective-permute-start.7
  90.0 12.3 %encode.6 = (bf16[512,3072]{1,0:T(8,128)(2,1)}, f32[512,768]{1,0:T(8,128)}, f32[1,3072]{1,0:T(1,128)}, f32[1,3072]{1,0:T(1,128)}, f32[1,768]{1,0:T(1,128)}) custom-call(bf16[512,768]{1,0:T(8,128)(2,1)} %copy-done.4, f32[4096,128]{1,0:T(8,128)} %copy-done, bf16[4,2,192,3072]{3,2,1,0:T(8,128)(2,1)} %bitcast.51, f32[1,3072]{1,0:T(1,128)} %bitcast.70, ...), custom_call_target="tpu_custom_call" | custom-call | flops 1207959552 | bytes 3932160 | tf_op jit(solution)/shard_map/encode/pallas_call | solution.py:262
  103.2 11.6 %encode.7 = (bf16[512,3072]{1,0:T(8,128)(2,1)}, bf16[256,768]{1,0:T(8,128)(2,1)}, bf16[256,768]{1,0:T(8,128)(2,1)}, f32[1,3072]{1,0:T(1,128)}, f32[1,3072]{1,0:T(1,128)}, /*index=5*/f32[1,768]{1,0:T(1,128)}) custom-call(bf16[256,768]{1,0:T(8,128)(2,1)} %copy-done.15, bf16[256,768]{1,0:T(8,128)(2,1)} %copy-done.16, f32[4096,128]{1,0:T(8,128)} %copy-done, ...), custom_call_target="tpu_custom_call" | custom-call | flops 1207959552 | bytes 3932160 | tf_op jit(solution)/shard_map/encode/pallas_call | solution.py:262
  116.9 12.1 %encode.8 = (bf16[512,3072]{1,0:T(8,128)(2,1)}, f32[512,768]{1,0:T(8,128)}, f32[1,3072]{1,0:T(1,128)}, f32[1,3072]{1,0:T(1,128)}, f32[1,768]{1,0:T(1,128)}) custom-call(bf16[512,768]{1,0:T(8,128)(2,1)} %copy-done.5, f32[4096,128]{1,0:T(8,128)} %copy-done, bf16[4,2,192,3072]{3,2,1,0:T(8,128)(2,1)} %bitcast.55, f32[1,3072]{1,0:T(1,128)} %bitcast.72, ...), custom_call_target="tpu_custom_call" | custom-call | flops 1207959552 | bytes 3932160 | tf_op jit(solution)/shard_map/encode/pallas_call | solution.py:262
  130.7 3.4 joined.1
  139.3 17.6 %encode.9 = (bf16[1024,3072]{1,0:T(8,128)(2,1)}, f32[512,768]{1,0:T(8,128)}, f32[512,768]{1,0:T(8,128)}, f32[1,3072]{1,0:T(1,128)}, f32[1,3072]{1,0:T(1,128)}, /*index=5*/f32[1,768]{1,0:T(1,128)}) custom-call(bf16[512,768]{1,0:T(8,128)(2,1)} %collective-permute-done.3.refs_0_.refs_1_, bf16[512,768]{1,0:T(8,128)(2,1)} %collective-permute-done.4.refs_1_.refs_2_, ...), custom_call_target="tpu_custom_call" | custom-call | flops 2415919104 | bytes 5505024 | tf_op jit(solution)/shard_map/encode/pallas_call | solution.py:262
  161.4 17.5 %encode.10 = (bf16[1024,3072]{1,0:T(8,128)(2,1)}, f32[512,768]{1,0:T(8,128)}, f32[512,768]{1,0:T(8,128)}, f32[1,3072]{1,0:T(1,128)}, f32[1,3072]{1,0:T(1,128)}, /*index=5*/f32[1,768]{1,0:T(1,128)}) custom-call(bf16[512,768]{1,0:T(8,128)(2,1)} %copy-done.11, bf16[512,768]{1,0:T(8,128)(2,1)} %copy-done.10, f32[4096,128]{1,0:T(8,128)} %copy-done, ...), custom_call_target="tpu_custom_call" | custom-call | flops 2415919104 | bytes 5505024 | tf_op jit(solution)/shard_map/encode/pallas_call | solution.py:262
  184.7 12.3 %encode.11 = (bf16[512,3072]{1,0:T(8,128)(2,1)}, f32[512,768]{1,0:T(8,128)}, f32[1,3072]{1,0:T(1,128)}, f32[1,3072]{1,0:T(1,128)}, f32[1,768]{1,0:T(1,128)}) custom-call(bf16[512,768]{1,0:T(8,128)(2,1)} %attend.1.refs_0_.z_ref.refs_1_, f32[4096,128]{1,0:T(8,128)} %copy-done, bf16[4,2,192,3072]{3,2,1,0:T(8,128)(2,1)} %bitcast.61, f32[1,3072]{1,0:T(1,128)} %bitcast.75, ...), custom_call_target="tpu_custom_call" | custom-call | flops 1207959552 | bytes 3932160 | tf_op jit(solution)/shard_map/encode/pallas_call | solution.py:262
  197.0 3.0 collective-permute-done.17.right_ref
  202.4 4.3 %compared.1 = (bf16[512,768]{1,0:T(8,128)(2,1)}, f32[8,128]{1,0:T(8,128)}, f32[1,3072]{1,0:T(1,128)}, f32[1,3072]{1,0:T(1,128)}, f32[8,128]{1,0:T(8,128)}) custom-call(f32[512,768]{1,0:T(8,128)} %get-tuple-element.283.rec_ref, bf16[512,768]{1,0:T(8,128)(2,1)} %copy-done.25, bf16[512,768]{1,0:T(8,128)(2,1)} %copy-done.26, ...), custom_call_target="tpu_custom_call" | custom-call | tf_op jit(solution)/shard_map/compared/pallas_call | solution.py:332
  208.7 13.3 %backward.6 = (f32[768,3072]{1,0:T(8,128)}, f32[768,3072]{1,0:T(8,128)}, f32[1,3072]{1,0:T(1,128)}, f32[1,768]{1,0:T(1,128)}) custom-call(bf16[512,3072]{1,0:T(8,128)(2,1)} %get-tuple-element.282.refs_0_, bf16[512,768]{1,0:T(8,128)(2,1)} %attend.1.refs_0_.z_ref.refs_1_, bf16[512,768]{1,0:T(8,128)(2,1)} %get-tuple-element.291.refs_2_, f32[4096,128]{1,0:T(8,128)} %copy-done, ...), custom_call_target="tpu_custom_call" | custom-call | flops 1811939328 | bytes 10223616 | tf_op jit(solution)/shard_map/backward/pallas_call | solution.py:471
  222.0 2.0 collective-permute-done.20.refs_4_
  226.4 22.7 %backward.7 = (f32[768,3072]{1,0:T(8,128)}, f32[768,3072]{1,0:T(8,128)}, f32[1,3072]{1,0:T(1,128)}, f32[1,768]{1,0:T(1,128)}) custom-call(bf16[1024,3072]{1,0:T(8,128)(2,1)} %get-tuple-element.294.refs_0_, bf16[512,768]{1,0:T(8,128)(2,1)} %copy-done.11, bf16[512,768]{1,0:T(8,128)(2,1)} %copy-done.10, bf16[512,768]{1,0:T(8,128)(2,1)} %copy-done.30, ...), custom_call_target="tpu_custom_call" | custom-call | flops 3623878656 | bytes 11010048 | tf_op jit(solution)/shard_map/backward/pallas_call | solution.py:471
  249.2 1.7 collective-permute-start.23
  251.4 22.8 %backward.8 = (f32[768,3072]{1,0:T(8,128)}, f32[768,3072]{1,0:T(8,128)}, f32[1,3072]{1,0:T(1,128)}, f32[1,768]{1,0:T(1,128)}) custom-call(bf16[1024,3072]{1,0:T(8,128)(2,1)} %get-tuple-element.302.refs_0_, bf16[512,768]{1,0:T(8,128)(2,1)} %collective-permute-done.3.refs_0_.refs_1_, bf16[512,768]{1,0:T(8,128)(2,1)} %collective-permute-done.4.refs_1_.refs_2_, ...), custom_call_target="tpu_custom_call" | custom-call | flops 3623878656 | bytes 11010048 | tf_op jit(solution)/shard_map/backward/pallas_call | solution.py:471
  277.9 4.2 collective-permute-done.26.refs_13_
  284.6 14.2 %backward.9 = (f32[2,2,192,1024]{3,2,1,0:T(8,128)}, bf16[2,2,192,1024]{3,2,1,0:T(8,128)(2,1)}, f32[1,1024]{1,0:T(1,128)}, f32[1,768]{1,0:T(1,128)}) custom-call(s32[1]{0:T(128)} %bitcast.7.refs_0_, bf16[512,3072]{1,0:T(8,128)(2,1)} %get-tuple-element.310.refs_1_, bf16[512,768]{1,0:T(8,128)(2,1)} %copy-done.4, bf16[512,768]{1,0:T(8,128)(2,1)} %copy-done.6, ...), custom_call_target="tpu_custom_call" | custom-call | flops 1811939328 | bytes 3932160 | tf_op jit(solution)/shard_map/backward/pallas_call | solution.py:471
  299.4 14.6 %backward.10 = (f32[2,2,192,1024]{3,2,1,0:T(8,128)}, bf16[2,2,192,1024]{3,2,1,0:T(8,128)(2,1)}, f32[1,1024]{1,0:T(1,128)}, f32[1,768]{1,0:T(1,128)}) custom-call(s32[1]{0:T(128)} %bitcast.7.refs_0_, bf16[512,3072]{1,0:T(8,128)(2,1)} %get-tuple-element.310.refs_1_, bf16[512,768]{1,0:T(8,128)(2,1)} %copy-done.4, bf16[512,768]{1,0:T(8,128)(2,1)} %copy-done.6, ...), custom_call_target="tpu_custom_call" | custom-call | flops 1811939328 | bytes 3932160 | tf_op jit(solution)/shard_map/backward/pallas_call | solution.py:471
  314.1 2.3 fusion.2
  316.8 1.7 collective-permute-start.31
  318.6 14.5 %backward.11 = (f32[2,2,192,1024]{3,2,1,0:T(8,128)}, bf16[2,2,192,1024]{3,2,1,0:T(8,128)(2,1)}, f32[1,1024]{1,0:T(1,128)}, f32[1,768]{1,0:T(1,128)}) custom-call(s32[1]{0:T(128)} %bitcast.7.refs_0_, bf16[512,3072]{1,0:T(8,128)(2,1)} %get-tuple-element.310.refs_1_, bf16[512,768]{1,0:T(8,128)(2,1)} %copy-done.4, bf16[512,768]{1,0:T(8,128)(2,1)} %copy-done.6, ...), custom_call_target="tpu_custom_call" | custom-call | flops 1811939328 | bytes 3932160 | tf_op jit(solution)/shard_map/backward/pallas_call | solution.py:471
  333.8 3.2 collective-permute-done.31
  338.5 2.3 fusion.3
  341.7 3.2 finished.3
  345.0 1.7 collective-permute-start.33
  346.7 2.3 fusion.4
  349.3 12.5 %collective-permute-done.33 = f32[2,3072]{1,0:T(2,128)S(1)} collective-permute-done((f32[2,3072]{1,0:T(2,128)S(1)}, f32[2,3072]{1,0:T(2,128)S(1)}, u32[]{:S(2)}, u32[]{:S(2)}) %collective-permute-start.33) | collective-permute-done | bytes 24608 | tf_op jit(solution)/shard_map/ppermute | solution.py:550
  364.5 3.1 finished.4
  367.5 10.3 %collective-permute-done.36.refs_0_ = bf16[2,192,1024]{2,1,0:T(8,128)(2,1)S(1)} collective-permute-done((bf16[2,192,1024]{2,1,0:T(8,128)(2,1)}, bf16[2,192,1024]{2,1,0:T(8,128)(2,1)S(1)}, u32[]{:S(2)}, u32[]{:S(2)}) %collective-permute-start.36) | collective-permute-done | bytes 786464 | tf_op jit(solution)/shard_map/ppermute | solution.py:550
  378.8 3.2 finished.5
  384.3 3.3 collective-permute-done.38
  389.2 2.1 collective-permute-done.39
  391.3 3.1 collective-permute-start.42
  396.9 2.0 collective-permute-done.41
  400.4 7.4 %multiply_reduce_fusion.1 = (f32[3072]{0:T(1024)S(1)}, f32[192,3072]{1,0:T(8,128)S(1)}, f32[3072,192]{0,1:T(8,128)}, f32[3072,192]{0,1:T(8,128)}) fusion(f32[3072,192]{0,1:T(8,128)} %param.37, f32[192,3072]{1,0:T(8,128)} %get-tuple-element.386, f32[]{:T(128)S(6)} %min_shard_map.3, f32[3072,192]{0,1:T(8,128)} %param.36, f32[3072,192]{0,1:T(8,128)S(1)} %copy-done.8), kind=kLoop, calls=%fused_computation.9 | loop fusion | flops 10613760 | bytes 16527364 | tf_op jit(solution)/shard_map/reduce_sum | solution.py:799
  408.5 4.4 %multiply_subtract_fusion.1 = (f32[192,3072]{1,0:T(8,128)}, f32[192,3072]{1,0:T(8,128)}, f32[192,3072]{1,0:T(8,128)}) fusion(f32[192,3072]{1,0:T(8,128)S(1)} %copy-done.9, f32[192,3072]{1,0:T(8,128)S(1)} %copy-done.2, f32[]{:T(128)S(6)} %min_shard_map.3, f32[192,3072]{1,0:T(8,128)S(1)} %copy-done.19, f32[192,3072]{1,0:T(8,128)S(1)} %copy-done.20), kind=kLoop, calls=%fused_computation.11 | loop fusion | flops 9437184 | bytes 16515076 | tf_op jit(solution)/shard_map/sub | solution.py:572
  414.1 1.8 pad_maximum_fusion.2
  417.4 1.8 multiply_bitcast_fusion
  (287 shorter events, 66.2 us)
Async XLA Ops:
  7.2 70.7 %all-gather.3.cloned.1.call-start = ((), (), s32[]{:S(2)}) async-start(), calls=%async_computation | async-start | bytes 11796480 | tf_op jit(solution)/shard_map/all_gather | solution.py:616
  11.7 10.9 %collective-permute-start = (bf16[128,768]{1,0:T(8,128)(2,1)S(1)}, bf16[128,768]{1,0:T(8,128)(2,1)S(1)}, u32[]{:S(2)}, u32[]{:S(2)}) collective-permute-start(bf16[128,768]{1,0:T(8,128)(2,1)S(1)} %slice.72), channel_id=1, source_target_pairs={{0,1},{1,2},{2,3},{3,4},{4,5},{5,6},{6,7},{7,0},{8,9},{9,10},{10,1... | collective-permute-start | bytes 589832 | tf_op jit(solution)/shard_map/ppermute | solution.py:617
  30.3 18.8 %collective-permute-start.2 = (bf16[512,768]{1,0:T(8,128)(2,1)}, bf16[512,768]{1,0:T(8,128)(2,1)S(1)}, u32[]{:S(2)}, u32[]{:S(2)}) collective-permute-start(bf16[512,768]{1,0:T(8,128)(2,1)} %attend.1.refs_0_.z_ref.refs_1_), channel_id=1, source_target_pairs={{0,1},{2,0},{4,2},{6,4},{7,6},{5,7},{3,5},{1,3},{8,9},{10,8},{12,1... | collective-permute-start | bytes 2359304 | tf_op jit(solution)/shard_map/ppermute | solution.py:546
  31.5 19.0 %collective-permute-start.1 = (bf16[512,768]{1,0:T(8,128)(2,1)}, bf16[512,768]{1,0:T(8,128)(2,1)S(1)}, u32[]{:S(2)}, u32[]{:S(2)}) collective-permute-start(bf16[512,768]{1,0:T(8,128)(2,1)} %attend.1.refs_0_.z_ref.refs_1_), channel_id=1, source_target_pairs={{0,2},{2,4},{4,6},{6,7},{7,5},{5,3},{3,1},{1,0},{8,10},{10,12},{12... | collective-permute-start | bytes 2359304 | tf_op jit(solution)/shard_map/ppermute | solution.py:546
  51.1 18.1 %collective-permute-start.3 = (bf16[512,768]{1,0:T(8,128)(2,1)S(1)}, bf16[512,768]{1,0:T(8,128)(2,1)}, u32[]{:S(2)}, u32[]{:S(2)}) collective-permute-start(bf16[512,768]{1,0:T(8,128)(2,1)S(1)} %collective-permute-done.1.refs_0_.refs_1_), channel_id=1, source_target_pairs={{0,2},{2,4},{4,6},{6,7},{7,5},{5,3},{3,1},{1,0},{8,10},{10,12},{12... | collective-permute-start | bytes 2359304 | tf_op jit(solution)/shard_map/ppermute | solution.py:546
  51.6 17.9 %collective-permute-start.4 = (bf16[512,768]{1,0:T(8,128)(2,1)S(1)}, bf16[512,768]{1,0:T(8,128)(2,1)}, u32[]{:S(2)}, u32[]{:S(2)}) collective-permute-start(bf16[512,768]{1,0:T(8,128)(2,1)S(1)} %collective-permute-done.2.refs_1_.refs_2_), channel_id=1, source_target_pairs={{0,1},{2,0},{4,2},{6,4},{7,6},{5,7},{3,5},{1,3},{8,9},{10,8},{12,1... | collective-permute-start | bytes 2359304 | tf_op jit(solution)/shard_map/ppermute | solution.py:546
  69.5 17.2 %collective-permute-start.5 = (bf16[512,768]{1,0:T(8,128)(2,1)}, bf16[512,768]{1,0:T(8,128)(2,1)S(1)}, u32[]{:S(2)}, u32[]{:S(2)}) collective-permute-start(bf16[512,768]{1,0:T(8,128)(2,1)} %collective-permute-done.3.refs_0_.refs_1_), channel_id=1, source_target_pairs={{0,2},{2,4},{4,6},{6,7},{7,5},{5,3},{3,1},{1,0},{8,10},{10,12},{12... | collective-permute-start | bytes 2359304 | tf_op jit(solution)/shard_map/ppermute | solution.py:546
  71.0 16.7 %collective-permute-start.6 = (bf16[512,768]{1,0:T(8,128)(2,1)}, bf16[512,768]{1,0:T(8,128)(2,1)S(1)}, u32[]{:S(2)}, u32[]{:S(2)}) collective-permute-start(bf16[512,768]{1,0:T(8,128)(2,1)} %collective-permute-done.4.refs_1_.refs_2_), channel_id=1, source_target_pairs={{0,1},{2,0},{4,2},{6,4},{7,6},{5,7},{3,5},{1,3},{8,9},{10,8},{12,1... | collective-permute-start | bytes 2359304 | tf_op jit(solution)/shard_map/ppermute | solution.py:546
  87.7 14.5 %collective-permute-start.7 = (bf16[256,768]{1,0:T(8,128)(2,1)S(1)}, bf16[256,768]{1,0:T(8,128)(2,1)S(1)}, u32[]{:S(2)}, u32[]{:S(2)}) collective-permute-start(bf16[256,768]{1,0:T(8,128)(2,1)S(1)} %slice.79), channel_id=1, source_target_pairs={{0,2},{2,4},{4,6},{6,7},{7,5},{5,3},{3,1},{1,0},{8,10},{10,12},{12... | collective-permute-start | bytes 1179656 | tf_op jit(solution)/shard_map/ppermute | solution.py:546
  89.4 12.9 %collective-permute-start.8 = (bf16[256,768]{1,0:T(8,128)(2,1)S(1)}, bf16[256,768]{1,0:T(8,128)(2,1)S(1)}, u32[]{:S(2)}, u32[]{:S(2)}) collective-permute-start(bf16[256,768]{1,0:T(8,128)(2,1)S(1)} %slice.80), channel_id=1, source_target_pairs={{0,1},{2,0},{4,2},{6,4},{7,6},{5,7},{3,5},{1,3},{8,9},{10,8},{12,1... | collective-permute-start | bytes 1179656 | tf_op jit(solution)/shard_map/ppermute | solution.py:546
  114.8 14.9 %collective-permute-start.9 = (bf16[256,768]{1,0:T(8,128)(2,1)}, bf16[256,768]{1,0:T(8,128)(2,1)S(1)}, u32[]{:S(2)}, u32[]{:S(2)}) collective-permute-start(bf16[256,768]{1,0:T(8,128)(2,1)} %get-tuple-element.221), channel_id=1, source_target_pairs={{0,2},{2,4},{4,6},{6,7},{7,5},{5,3},{3,1},{1,0},{8,10},{10,12},{12... | collective-permute-start | bytes 1179656 | tf_op jit(solution)/shard_map/ppermute | solution.py:546
  116.5 13.3 %collective-permute-start.10 = (bf16[256,768]{1,0:T(8,128)(2,1)}, bf16[256,768]{1,0:T(8,128)(2,1)S(1)}, u32[]{:S(2)}, u32[]{:S(2)}) collective-permute-start(bf16[256,768]{1,0:T(8,128)(2,1)} %get-tuple-element.222), channel_id=1, source_target_pairs={{0,1},{2,0},{4,2},{6,4},{7,6},{5,7},{3,5},{1,3},{8,9},{10,8},{12,1... | collective-permute-start | bytes 1179656 | tf_op jit(solution)/shard_map/ppermute | solution.py:546
  134.1 23.5 %collective-permute-start.11 = (bf16[512,768]{1,0:T(8,128)(2,1)}, bf16[512,768]{1,0:T(8,128)(2,1)S(1)}, u32[]{:S(2)}, u32[]{:S(2)}) collective-permute-start(bf16[512,768]{1,0:T(8,128)(2,1)} %get-tuple-element.238), channel_id=1, source_target_pairs={{0,2},{2,4},{4,6},{6,7},{7,5},{5,3},{3,1},{1,0},{8,10},{10,12},{12... | collective-permute-start | bytes 2359304 | tf_op jit(solution)/shard_map/ppermute | solution.py:546
  135.7 21.8 %collective-permute-start.12 = (bf16[512,768]{1,0:T(8,128)(2,1)}, bf16[512,768]{1,0:T(8,128)(2,1)S(1)}, u32[]{:S(2)}, u32[]{:S(2)}) collective-permute-start(bf16[512,768]{1,0:T(8,128)(2,1)} %get-tuple-element.239), channel_id=1, source_target_pairs={{0,1},{2,0},{4,2},{6,4},{7,6},{5,7},{3,5},{1,3},{8,9},{10,8},{12,1... | collective-permute-start | bytes 2359304 | tf_op jit(solution)/shard_map/ppermute | solution.py:546
  136.5 1.2 collective-permute-start.13
  137.8 19.2 %collective-permute-start.14 = (f32[2,768]{1,0:T(2,128)S(1)}, f32[2,768]{1,0:T(2,128)S(1)}, u32[]{:S(2)}, u32[]{:S(2)}) collective-permute-start(f32[2,768]{1,0:T(2,128)S(1)} %fusion.17), channel_id=1, source_target_pairs={{0,16},{8,24},{16,0},{24,8},{1,17},{9,25},{17,1},{25,9},{2,18},{10... | collective-permute-start | bytes 18440 | tf_op jit(solution)/shard_map/ppermute | solution.py:550
  159.3 19.6 %collective-permute-start.15 = (bf16[512,768]{1,0:T(8,128)(2,1)S(1)}, bf16[512,768]{1,0:T(8,128)(2,1)S(1)}, u32[]{:S(2)}, u32[]{:S(2)}) collective-permute-start(bf16[512,768]{1,0:T(8,128)(2,1)S(1)} %add_convert_fusion.6), channel_id=1, source_target_pairs={{0,2},{2,4},{4,6},{6,7},{7,5},{5,3},{3,1},{1,0},{8,10},{10,12},{12... | collective-permute-start | bytes 2359304 | tf_op jit(solution)/shard_map/ppermute | solution.py:546
  160.9 19.1 %collective-permute-start.16 = (bf16[512,768]{1,0:T(8,128)(2,1)S(1)}, bf16[512,768]{1,0:T(8,128)(2,1)S(1)}, u32[]{:S(2)}, u32[]{:S(2)}) collective-permute-start(bf16[512,768]{1,0:T(8,128)(2,1)S(1)} %add_convert_fusion.5), channel_id=1, source_target_pairs={{0,1},{2,0},{4,2},{6,4},{7,6},{5,7},{3,5},{1,3},{8,9},{10,8},{12,1... | collective-permute-start | bytes 2359304 | tf_op jit(solution)/shard_map/ppermute | solution.py:546
  181.8 18.2 %collective-permute-start.17 = (bf16[512,768]{1,0:T(8,128)(2,1)S(1)}, bf16[512,768]{1,0:T(8,128)(2,1)S(1)}, u32[]{:S(2)}, u32[]{:S(2)}) collective-permute-start(bf16[512,768]{1,0:T(8,128)(2,1)S(1)} %add_convert_fusion.4), channel_id=1, source_target_pairs={{0,2},{2,4},{4,6},{6,7},{7,5},{5,3},{3,1},{1,0},{8,10},{10,12},{12... | collective-permute-start | bytes 2359304 | tf_op jit(solution)/shard_map/ppermute | solution.py:546
  183.5 18.0 %collective-permute-start.18 = (bf16[512,768]{1,0:T(8,128)(2,1)S(1)}, bf16[512,768]{1,0:T(8,128)(2,1)S(1)}, u32[]{:S(2)}, u32[]{:S(2)}) collective-permute-start(bf16[512,768]{1,0:T(8,128)(2,1)S(1)} %add_convert_fusion.3), channel_id=1, source_target_pairs={{0,1},{2,0},{4,2},{6,4},{7,6},{5,7},{3,5},{1,3},{8,9},{10,8},{12,1... | collective-permute-start | bytes 2359304 | tf_op jit(solution)/shard_map/ppermute | solution.py:546
  206.7 17.4 %collective-permute-start.20 = (bf16[512,768]{1,0:T(8,128)(2,1)}, bf16[512,768]{1,0:T(8,128)(2,1)S(1)}, u32[]{:S(2)}, u32[]{:S(2)}) collective-permute-start(bf16[512,768]{1,0:T(8,128)(2,1)} %get-tuple-element.291.refs_2_), channel_id=1, source_target_pairs={{0,1},{2,0},{4,2},{6,4},{7,6},{5,7},{3,5},{1,3},{8,9},{10,8},{12,1... | collective-permute-start | bytes 2359304 | tf_op jit(solution)/shard_map/ppermute | solution.py:546
  207.1 17.2 %collective-permute-start.19 = (bf16[512,768]{1,0:T(8,128)(2,1)}, bf16[512,768]{1,0:T(8,128)(2,1)S(1)}, u32[]{:S(2)}, u32[]{:S(2)}) collective-permute-start(bf16[512,768]{1,0:T(8,128)(2,1)} %get-tuple-element.291.refs_2_), channel_id=1, source_target_pairs={{0,2},{2,4},{4,6},{6,7},{7,5},{5,3},{3,1},{1,0},{8,10},{10,12},{12... | collective-permute-start | bytes 2359304 | tf_op jit(solution)/shard_map/ppermute | solution.py:546
  224.3 24.8 %collective-permute-start.21 = (bf16[512,768]{1,0:T(8,128)(2,1)S(1)}, bf16[512,768]{1,0:T(8,128)(2,1)S(1)}, u32[]{:S(2)}, u32[]{:S(2)}) collective-permute-start(bf16[512,768]{1,0:T(8,128)(2,1)S(1)} %collective-permute-done.19.refs_3_), channel_id=1, source_target_pairs={{0,2},{2,4},{4,6},{6,7},{7,5},{5,3},{3,1},{1,0},{8,10},{10,12},{12... | collective-permute-start | bytes 2359304 | tf_op jit(solution)/shard_map/ppermute | solution.py:546
  226.0 23.2 %collective-permute-start.22 = (bf16[512,768]{1,0:T(8,128)(2,1)S(1)}, bf16[512,768]{1,0:T(8,128)(2,1)S(1)}, u32[]{:S(2)}, u32[]{:S(2)}) collective-permute-start(bf16[512,768]{1,0:T(8,128)(2,1)S(1)} %collective-permute-done.20.refs_4_), channel_id=1, source_target_pairs={{0,1},{2,0},{4,2},{6,4},{7,6},{5,7},{3,5},{1,3},{8,9},{10,8},{12,1... | collective-permute-start | bytes 2359304 | tf_op jit(solution)/shard_map/ppermute | solution.py:546
  249.2 25.0 %collective-permute-start.23 = (bf16[512,768]{1,0:T(8,128)(2,1)S(1)}, bf16[512,768]{1,0:T(8,128)(2,1)S(1)}, u32[]{:S(2)}, u32[]{:S(2)}) collective-permute-start(bf16[512,768]{1,0:T(8,128)(2,1)S(1)} %collective-permute-done.21.refs_3_), channel_id=1, source_target_pairs={{0,2},{2,4},{4,6},{6,7},{7,5},{5,3},{3,1},{1,0},{8,10},{10,12},{12... | collective-permute-start | bytes 2359304 | tf_op jit(solution)/shard_map/ppermute | solution.py:546
  250.9 23.3 %collective-permute-start.24 = (bf16[512,768]{1,0:T(8,128)(2,1)S(1)}, bf16[512,768]{1,0:T(8,128)(2,1)S(1)}, u32[]{:S(2)}, u32[]{:S(2)}) collective-permute-start(bf16[512,768]{1,0:T(8,128)(2,1)S(1)} %collective-permute-done.22.refs_4_), channel_id=1, source_target_pairs={{0,1},{2,0},{4,2},{6,4},{7,6},{5,7},{3,5},{1,3},{8,9},{10,8},{12,1... | collective-permute-start | bytes 2359304 | tf_op jit(solution)/shard_map/ppermute | solution.py:546
  251.3 25.3 %copy-start.35 = (f32[3072]{0:T(1024)S(1)}, f32[3072]{0:T(1024)}, u32[]{:S(2)}) copy-start(f32[3072]{0:T(1024)} %sqrt.28) | copy-start | bytes 36868
  251.3 25.2 %copy-start.50 = (f32[1,3072]{1,0:T(1,128)S(1)}, f32[1,3072]{1,0:T(1,128)}, u32[]{:S(2)}) copy-start(f32[1,3072]{1,0:T(1,128)} %get-tuple-element.336) | copy-start | bytes 36868
  274.3 7.8 %collective-permute-start.26 = (bf16[256,768]{1,0:T(8,128)(2,1)S(1)}, bf16[256,768]{1,0:T(8,128)(2,1)S(1)}, u32[]{:S(2)}, u32[]{:S(2)}) collective-permute-start(bf16[256,768]{1,0:T(8,128)(2,1)S(1)} %slice.82), channel_id=1, source_target_pairs={{0,1},{2,0},{4,2},{6,4},{7,6},{5,7},{3,5},{1,3},{8,9},{10,8},{12,1... | collective-permute-start | bytes 1179656 | tf_op jit(solution)/shard_map/ppermute | solution.py:546
  275.8 8.0 %collective-permute-start.25 = (bf16[256,768]{1,0:T(8,128)(2,1)S(1)}, bf16[256,768]{1,0:T(8,128)(2,1)S(1)}, u32[]{:S(2)}, u32[]{:S(2)}) collective-permute-start(bf16[256,768]{1,0:T(8,128)(2,1)S(1)} %slice.81), channel_id=1, source_target_pairs={{0,2},{2,4},{4,6},{6,7},{7,5},{5,3},{3,1},{1,0},{8,10},{10,12},{12... | collective-permute-start | bytes 1179656 | tf_op jit(solution)/shard_map/ppermute | solution.py:546
  298.8 15.2 %collective-permute-start.27 = (bf16[2,2,192,1024]{3,2,1,0:T(8,128)(2,1)}, bf16[2,2,192,1024]{3,2,1,0:T(8,128)(2,1)}, u32[]{:S(2)}, u32[]{:S(2)}) collective-permute-start(bf16[2,2,192,1024]{3,2,1,0:T(8,128)(2,1)} %get-tuple-element.337), channel_id=1, source_target_pairs={{0,8},{8,0},{16,24},{24,16},{1,9},{9,1},{17,25},{25,17},{2,10},{10... | collective-permute-start | bytes 4718600 | tf_op jit(solution)/shard_map/ppermute | solution.py:550
  298.9 15.1 %collective-permute-start.28 = (f32[2,3072]{1,0:T(2,128)S(1)}, f32[2,3072]{1,0:T(2,128)S(1)}, u32[]{:S(2)}, u32[]{:S(2)}) collective-permute-start(f32[2,3072]{1,0:T(2,128)S(1)} %pad_maximum_fusion), channel_id=1, source_target_pairs={{0,8},{8,0},{16,24},{24,16},{1,9},{9,1},{17,25},{25,17},{2,10},{10... | collective-permute-start | bytes 73736 | tf_op jit(solution)/shard_map/ppermute | solution.py:550
  314.0 23.1 %collective-permute-start.30 = (bf16[2,2,192,1024]{3,2,1,0:T(8,128)(2,1)}, bf16[2,2,192,1024]{3,2,1,0:T(8,128)(2,1)}, u32[]{:S(2)}, u32[]{:S(2)}) collective-permute-start(bf16[2,2,192,1024]{3,2,1,0:T(8,128)(2,1)} %get-tuple-element.348), channel_id=1, source_target_pairs={{0,8},{8,0},{16,24},{24,16},{1,9},{9,1},{17,25},{25,17},{2,10},{10... | collective-permute-start | bytes 4718600 | tf_op jit(solution)/shard_map/ppermute | solution.py:550
  316.4 20.7 %collective-permute-start.29 = (bf16[2,192,1024]{2,1,0:T(8,128)(2,1)}, bf16[2,192,1024]{2,1,0:T(8,128)(2,1)S(1)}, u32[]{:S(2)}, u32[]{:S(2)}) collective-permute-start(bf16[2,192,1024]{2,1,0:T(8,128)(2,1)} %fusion.2), channel_id=1, source_target_pairs={{0,16},{8,24},{16,0},{24,8},{1,17},{9,25},{17,1},{25,9},{2,18},{10... | collective-permute-start | bytes 2359304 | tf_op jit(solution)/shard_map/ppermute | solution.py:550
  316.8 20.2 %collective-permute-start.31 = (f32[2,3072]{1,0:T(2,128)S(1)}, f32[2,3072]{1,0:T(2,128)S(1)}, u32[]{:S(2)}, u32[]{:S(2)}) collective-permute-start(f32[2,3072]{1,0:T(2,128)S(1)} %add.333), channel_id=1, source_target_pairs={{0,16},{8,24},{16,0},{24,8},{1,17},{9,25},{17,1},{25,9},{2,18},{10... | collective-permute-start | bytes 73736 | tf_op jit(solution)/shard_map/ppermute | solution.py:550
  337.9 7.0 %collective-permute-start.32 = (f32[2,3072]{1,0:T(2,128)S(1)}, f32[2,3072]{1,0:T(2,128)S(1)}, u32[]{:S(2)}, u32[]{:S(2)}) collective-permute-start(f32[2,3072]{1,0:T(2,128)S(1)} %fusion.7), channel_id=1, source_target_pairs={{0,8},{8,0},{16,24},{24,16},{1,9},{9,1},{17,25},{25,17},{2,10},{10... | collective-permute-start | bytes 73736 | tf_op jit(solution)/shard_map/ppermute | solution.py:550
  338.0 8.7 %collective-permute-start.35 = (bf16[2,2,192,1024]{3,2,1,0:T(8,128)(2,1)}, bf16[2,2,192,1024]{3,2,1,0:T(8,128)(2,1)}, u32[]{:S(2)}, u32[]{:S(2)}) collective-permute-start(bf16[2,2,192,1024]{3,2,1,0:T(8,128)(2,1)} %get-tuple-element.380), channel_id=1, source_target_pairs={{0,8},{8,0},{16,24},{24,16},{1,9},{9,1},{17,25},{25,17},{2,10},{10... | collective-permute-start | bytes 4718600 | tf_op jit(solution)/shard_map/ppermute | solution.py:550
  340.8 23.7 %collective-permute-start.34 = (bf16[2,192,1024]{2,1,0:T(8,128)(2,1)}, bf16[2,192,1024]{2,1,0:T(8,128)(2,1)}, u32[]{:S(2)}, u32[]{:S(2)}) collective-permute-start(bf16[2,192,1024]{2,1,0:T(8,128)(2,1)} %fusion.3), channel_id=1, source_target_pairs={{0,16},{8,24},{16,0},{24,8},{1,17},{9,25},{17,1},{25,9},{2,18},{10... | collective-permute-start | bytes 2359304 | tf_op jit(solution)/shard_map/ppermute | solution.py:550
  345.0 16.9 %collective-permute-start.33 = (f32[2,3072]{1,0:T(2,128)S(1)}, f32[2,3072]{1,0:T(2,128)S(1)}, u32[]{:S(2)}, u32[]{:S(2)}) collective-permute-start(f32[2,3072]{1,0:T(2,128)S(1)} %fusion.18), channel_id=1, source_target_pairs={{0,16},{8,24},{16,0},{24,8},{1,17},{9,25},{17,1},{25,9},{2,18},{10... | collective-permute-start | bytes 73736 | tf_op jit(solution)/shard_map/ppermute | solution.py:550
  349.0 28.9 %collective-permute-start.36 = (bf16[2,192,1024]{2,1,0:T(8,128)(2,1)}, bf16[2,192,1024]{2,1,0:T(8,128)(2,1)S(1)}, u32[]{:S(2)}, u32[]{:S(2)}) collective-permute-start(bf16[2,192,1024]{2,1,0:T(8,128)(2,1)} %fusion.4), channel_id=1, source_target_pairs={{0,16},{8,24},{16,0},{24,8},{1,17},{9,25},{17,1},{25,9},{2,18},{10... | collective-permute-start | bytes 2359304 | tf_op jit(solution)/shard_map/ppermute | solution.py:550
  382.8 1.2 collective-permute-start.37
  384.0 3.7 collective-permute-start.38
  387.6 3.7 collective-permute-start.39
  391.3 5.7 %collective-permute-start.42 = (f32[16,128]{1,0:T(8,128)S(1)}, f32[16,128]{1,0:T(8,128)S(1)}, u32[]{:S(2)}, u32[]{:S(2)}) collective-permute-start(f32[16,128]{1,0:T(8,128)S(1)} %add.352), channel_id=1, source_target_pairs={{0,6},{1,7},{2,4},{3,5},{4,2},{5,3},{6,0},{7,1},{8,14},{9,15},{10,... | collective-permute-start | bytes 24584 | tf_op jit(solution)/shard_map/ppermute | solution.py:550
  394.3 4.5 %collective-permute-start.41 = (f32[16,128]{1,0:T(8,128)S(1)}, f32[16,128]{1,0:T(8,128)S(1)}, u32[]{:S(2)}, u32[]{:S(2)}) collective-permute-start(f32[16,128]{1,0:T(8,128)S(1)} %add.352), channel_id=1, source_target_pairs={{0,4},{1,5},{2,6},{3,7},{4,0},{5,1},{6,2},{7,3},{8,12},{9,13},{10,... | collective-permute-start | bytes 24584 | tf_op jit(solution)/shard_map/ppermute | solution.py:550
  394.3 4.5 %collective-permute-start.40 = (f32[16,128]{1,0:T(8,128)S(1)}, f32[16,128]{1,0:T(8,128)S(1)}, u32[]{:S(2)}, u32[]{:S(2)}) collective-permute-start(f32[16,128]{1,0:T(8,128)S(1)} %add.352), channel_id=1, source_target_pairs={{0,2},{1,3},{2,0},{3,1},{4,6},{5,7},{6,4},{7,5},{8,10},{9,11},{10,... | collective-permute-start | bytes 24584 | tf_op jit(solution)/shard_map/ppermute | solution.py:550
  407.8 5.7 %collective-permute-start.43 = (f32[1,3072]{1,0:T(1,128)S(1)}, f32[1,3072]{1,0:T(1,128)S(1)}, u32[]{:S(2)}, u32[]{:S(2)}) collective-permute-start(f32[1,3072]{1,0:T(1,128)S(1)} %bitcast.80), channel_id=1, source_target_pairs={{0,8},{8,0},{16,24},{24,16},{1,9},{9,1},{17,25},{25,17},{2,10},{10... | collective-permute-start | bytes 36872 | tf_op jit(solution)/shard_map/ppermute | solution.py:550
  413.6 3.8 collective-permute-start.44
  (69 other events, 662.6 us)
Sparse Core Ops, SparseCore 0:
  10.9 66.9 all-gather.2

commit v4 on v3

--- a/solution.py
+++ b/solution.py
@@ -61,7 +61,7 @@
     return (centred * lax.rsqrt(variance + 1e-05) * gain + shift).astype(BF16)
 
 
-def project_kernel(rows_ref, gain_ref, bias_ref, w_ref, wb_ref, out_ref, normed_s):
+def project_kernel(rows_ref, gain_ref, bias_ref, w_ref, wb_ref, out_ref, normed_s, offset_s):
     width = rows_ref.shape[1]
 
     @pl.when(pl.program_id(0) == 0)
@@ -69,8 +69,10 @@
         gain = gain_ref[...].astype(F32).reshape(1, width)
         shift = bias_ref[...].astype(F32).reshape(1, width)
         normed_s[...] = normed(rows_ref[...], gain, shift)
-
-    out_ref[...] = (dot_nn(normed_s[...], w_ref[...]) + wb_ref[...].astype(F32)).astype(BF16)
+        offset_s[...] = wb_ref[...].astype(F32).reshape(1, 3 * width)
+
+    at = pl.multiple_of(pl.program_id(0) * width, LANES)
+    out_ref[...] = (dot_nn(normed_s[...], w_ref[...]) + offset_s[:, pl.ds(at, width)]).astype(BF16)
 
 
 def project(resid, ln_gain, ln_bias, qkv_weight, qkv_bias):
@@ -85,15 +87,15 @@
             pl.BlockSpec((width,), lambda j: (0,)),
             pl.BlockSpec((width,), lambda j: (0,)),
             pl.BlockSpec((width, width), across),
-            pl.BlockSpec((1, width), across),
+            pl.BlockSpec((3 * width,), lambda j: (0,)),
         ],
         out_specs=pl.BlockSpec((rows, width), across),
         out_shape=jax.ShapeDtypeStruct((rows, 3 * width), BF16),
-        scratch_shapes=[pltpu.VMEM((rows, width), BF16)],
+        scratch_shapes=[pltpu.VMEM((rows, width), BF16), pltpu.VMEM((1, 3 * width), F32)],
         compiler_params=kernel_params(),
         cost_estimate=pl.CostEstimate(flops=6 * rows * width * width, bytes_accessed=6 * width * width, transcendentals=0),
         name="project",
-    )(resid, ln_gain, ln_bias, qkv_weight, qkv_bias[None])
+    )(resid, ln_gain, ln_bias, qkv_weight, qkv_bias)
 
 
 def attend_kernel(own_ref, tail_ref, seg_q_ref, seg_k_ref, gain_ref, bias_ref, w_ref, wb_ref, z_ref, w_s, kv_s, sem):
@@ -186,10 +188,10 @@
     )(enc, dec)
 
 
-def encode_kernel(count, rounded, *refs):
+def encode_kernel(count, *refs):
     z_refs, (keep_ref, enc_ref, bias_ref, dec_ref), rest = refs[:count], refs[count : count + 4], refs[count + 4 :]
     act_ref, rec_refs, (sum_ref, fire_ref, square_ref) = rest[0], rest[1 : 1 + count], rest[1 + count : 4 + count]
-    totals = rest[4 + count :] if rounded else rec_refs
+    totals = rest[4 + count :]
     step, last = pl.program_id(0), pl.num_programs(0) - 1
     features = enc_ref.shape[-1]
 
@@ -238,19 +240,17 @@
     sum_ref[...] = jnp.sum(sums, axis=0, keepdims=True)
     fire_ref[...] = jnp.sum(fires, axis=0, keepdims=True)
 
-    if rounded:
-
-        @pl.when(step == last)
-        def _():
-            for piece in range(count):
-                rec_refs[piece][...] = totals[piece][...].astype(BF16)
+    @pl.when(step == last)
+    def _():
+        for piece in range(count):
+            rec_refs[piece][...] = totals[piece][...].astype(BF16)
 
 
 def wide(block, columns):
     return jnp.concatenate([block] * (columns // block.shape[1]), axis=1)
 
 
-def encode(pieces, keep_wide, keep_at, weights, bias, rounded):
+def encode(pieces, keep_wide, keep_at, weights, bias):
     parts, _, rows, features = weights.shape
     width = parts * rows
     sizes = [p.shape[0] for p in pieces]
@@ -260,7 +260,7 @@
     across = lambda j: (0, j)
     keep_block = keep_at // tokens
     outs = pl.pallas_call(
-        functools.partial(encode_kernel, len(pieces), rounded),
+        functools.partial(encode_kernel, len(pieces)),
         grid=(features // fb,),
         in_specs=[pl.BlockSpec((s, width), whole) for s in sizes]
         + [
@@ -274,10 +274,10 @@
         + [pl.BlockSpec((1, fb), across)] * 2
         + [pl.BlockSpec((1, width), whole)],
         out_shape=[jax.ShapeDtypeStruct((tokens, features), BF16)]
-        + [jax.ShapeDtypeStruct((s, width), BF16 if rounded else F32) for s in sizes]
+        + [jax.ShapeDtypeStruct((s, width), BF16) for s in sizes]
         + [jax.ShapeDtypeStruct((1, features), F32)] * 2
         + [jax.ShapeDtypeStruct((1, width), F32)],
-        scratch_shapes=[pltpu.VMEM((s, width), F32) for s in sizes] if rounded else [],
+        scratch_shapes=[pltpu.VMEM((s, width), F32) for s in sizes],
         compiler_params=kernel_params(),
         cost_estimate=pl.CostEstimate(
             flops=4 * tokens * width * features // COST_SHARE,
@@ -291,16 +291,24 @@
 
 def joined_kernel(right_ref, left_ref, from_right_ref, from_left_ref, right_out, left_out):
     rows = right_ref.shape[0]
-    right_out[:rows, :] = (from_right_ref[:rows, :] + right_ref[...].astype(F32)).astype(BF16)
-    right_out[rows:, :] = from_right_ref[rows:, :].astype(BF16)
-    left_out[:rows, :] = from_left_ref[:rows, :].astype(BF16)
-    left_out[rows:, :] = (from_left_ref[rows:, :] + left_ref[...].astype(F32)).astype(BF16)
+    right_out[:rows, :] = (from_right_ref[:rows, :].astype(F32) + right_ref[...].astype(F32)).astype(BF16)
+    right_out[rows:, :] = from_right_ref[rows:, :]
+    left_out[:rows, :] = from_left_ref[:rows, :]
+    left_out[rows:, :] = (from_left_ref[rows:, :].astype(F32) + left_ref[...].astype(F32)).astype(BF16)
 
 
 def joined(right, left, from_right, from_left):
-    shape = jax.ShapeDtypeStruct(from_right.shape, BF16)
+    rows, width = from_right.shape
+    half = pl.BlockSpec((rows // 2, 2 * LANES), lambda j: (0, j))
+    full = pl.BlockSpec((rows, 2 * LANES), lambda j: (0, j))
     return pl.pallas_call(
-        joined_kernel, out_shape=[shape, shape], compiler_params=kernel_params(), name="joined"
+        joined_kernel,
+        grid=(width // (2 * LANES),),
+        in_specs=[half, half, full, full],
+        out_specs=[full, full],
+        out_shape=[jax.ShapeDtypeStruct((rows, width), BF16)] * 2,
+        compiler_params=kernel_params(),
+        name="joined",
     )(right, left, from_right, from_left)
 
 
@@ -310,32 +318,39 @@
     counted = jnp.sum(totals_ref[1:2, :], keepdims=True)
     mean_square = squares / (counted * width) + 1e-06
     unit = 2.0 / (width * mean_square * counted)
-    share = LAMBDA / counted
-    norms = norm_ref[...]
-    scaled_ref[...] = share * norms
-    penalty_ref[...] = share / norms
-    counted_ref[...] = counted + jnp.zeros(counted_ref.shape, F32)
-    residue = rec_ref[...] + right_ref[...].astype(F32) + left_ref[...].astype(F32) + bias_ref[...] - z_ref[...].astype(F32)
+    residue = rec_ref[...].astype(F32) + right_ref[...].astype(F32) + left_ref[...].astype(F32)
+    residue = residue + bias_ref[...] - z_ref[...].astype(F32)
     kept = wide(keep_ref[...], width) * residue
     grad_ref[...] = (kept * unit).astype(BF16)
     fit = jnp.sum((kept * residue).reshape(rows // 8, 8, width), axis=0)
-    fit_ref[...] = sum(fit[:, at : at + LANES] for at in range(0, width, LANES)) / (width * mean_square)
+
+    @pl.when(pl.program_id(0) == 0)
+    def _():
+        share = LAMBDA / counted
+        norms = norm_ref[...]
+        scaled_ref[...] = share * norms
+        penalty_ref[...] = share / norms
+        counted_ref[...] = counted + jnp.zeros(counted_ref.shape, F32)
+        fit_ref[...] = jnp.zeros_like(fit_ref)
+
+    fit_ref[...] += sum(fit[:, at : at + LANES] for at in range(0, width, LANES)) / (width * mean_square)
 
 
 def compared(rec, right, left, tokens_z, dec_bias, keep_wide, keep_at, totals, row_norm):
     rows, width = tokens_z.shape
     features = row_norm.shape[1]
+    block = CTX
     whole = lambda j: (0, 0)
-    own = pl.BlockSpec((rows, width), whole)
+    own = pl.BlockSpec((block, width), lambda j: (j, 0))
     line = pl.BlockSpec((1, features), whole)
     tile = pl.BlockSpec((8, LANES), whole)
     return pl.pallas_call(
         compared_kernel,
-        grid=(1,),
+        grid=(rows // block,),
         in_specs=[own] * 4
         + [
             pl.BlockSpec((1, width), whole),
-            pl.BlockSpec((rows, LANES), lambda j: (keep_at // rows, 0)),
+            pl.BlockSpec((block, LANES), lambda j: (keep_at // block + j, 0)),
             pl.BlockSpec(totals.shape, whole),
             line,
         ],
@@ -554,12 +569,7 @@
     for axis in axes:
         size, bit = lax.axis_size(axis), 1
         while bit < size:
-            if axis == "feat" and 4 * bit == size:
-                first, second, third = (swapped(block, axis, bit * i) for i in (1, 2, 3))
-                block = (block + first) + (second + third)
-                bit *= 2
-            else:
-                block = block + swapped(block, axis, bit)
+            block = block + swapped(block, axis, bit)
             bit *= 2
     return block
 
@@ -658,7 +668,7 @@
     def encoded(hop, pieces=slice(None)):
         chosen = z_stages[hop][pieces]
         at = keep_at[hop] + (own_rows if pieces == slice(1, 2) else 0)
-        act, rec, stat = encode(chosen, keep_wide, at, weights, bias_row, hop == half)
+        act, rec, stat = encode(chosen, keep_wide, at, weights, bias_row)
         if pieces == slice(1, 2):
             act, rec, stat = [*acts[hop], act], [*recs[hop], *rec], [a + b for a, b in zip(stats[hop], stat)]
         elif pieces == slice(0, 1):
@@ -695,8 +705,8 @@
         if step == 1:
             right, left = joined(right, left, from_right, from_left)
         else:
-            right = (from_right + right.astype(F32)).astype(BF16)
-            left = (from_left + left.astype(F32)).astype(BF16)
+            right = (from_right.astype(F32) + right.astype(F32)).astype(BF16)
+            left = (from_left.astype(F32) + left.astype(F32)).astype(BF16)
         following = half - step - 1
         right, left, z_stages[following] = together(right, left, z_stages[following])
     own_grad, fit_part, norm_scaled, penalty_scale, counted = compared(
@@ -704,8 +714,10 @@
     )
     own_grad, fit_part, norm_scaled = together(own_grad, fit_part, norm_scaled)
 
+    wide_by = features // LAST_PARTS
     bias_shares, out_bias_shares = [], []
-    carried = None
+    carried = middle = None
+    middle_biases = []
     grad_stages = [[own_grad]]
     right, left = own_grad, own_grad
 
@@ -723,22 +735,34 @@
         if hop == half:
             right, left = right[:rows], left[rows:]
         right, left = ring_shift(right, 1), ring_shift(left, -1)
-        if hop < half:
+        if half - 2 <= hop < half:
+            *middle, middle_bias, _ = backward(
+                group_of([hop - 1]), keep_wide, norm_scaled, weights, middle or carried, 0, features - wide_by, 0, None
+            )
+            middle_biases.append(middle_bias)
+            right, left, middle = together(right, left, middle)
+        elif hop < half:
             *carried, bias_grad, out_bias_grad = backward(
                 group_of([hop - 1]), keep_wide, norm_scaled, weights, carried, 0, features, 0, None
             )
             bias_shares.append(bias_grad)
             out_bias_shares.append(out_bias_grad)
-        right, left, carried = together(right, left, carried)
+            right, left, carried = together(right, left, carried)
+        else:
+            *ahead, ahead_bias, _ = backward(
+                group_of([half - 1]), keep_wide, norm_scaled, weights, middle, 0, wide_by, 0, None
+            )
+            right, left, ahead, ahead_bias = together(right, left, ahead, ahead_bias)
         grad_stages.append([right, left])
 
-    wide_by = features // LAST_PARTS
     kept, paired, arrived, last_bias = [], [], [], []
     grads = None
 
-    def crossed(part):
-        away = [kept[part][i] + paired[part][i].astype(F32) for i in range(1, dp_size // 2)]
-        return [swapped(block.astype(BF16), "dp", 2 * i + 2) for i, block in enumerate(away)]
+    def crossing(part):
+        return [(kept[part][i] + paired[part][i].astype(F32)).astype(BF16) for i in range(1, dp_size // 2)]
+
+    def crossed(part, blocks=None):
+        return [swapped(block, "dp", 2 * i + 2) for i, block in enumerate(blocks or crossing(part))]
 
     def rest_of(block):
         for bit in range(2, dp_size, 2):
@@ -749,34 +773,39 @@
     act_sum, fire_sum, _ = (sum(parts) for parts in zip(*stats))
     counts = jnp.concatenate([fire_sum, act_sum])
     loss_share = LAMBDA * jnp.sum(act_sum * row_norm)
-    sent = []
-    for turn in range(LAST_PARTS):
-        if turn >= 2:
-            arrived.append(crossed(turn - 2))
-        if turn == 2:
-            counts = rest_of(counts)
-        if turn >= 1:
-            paired.append(swapped(sent[turn - 1], "dp", 1))
-        if turn == 1:
-            counts = counts + swapped(counts, "dp", 1)
+    def last_tokens(part, plan, before):
         keep_part, send_part, bias_grad, out_bias_grad = backward(
-            group_of([half - 1, half]), keep_wide, norm_scaled, weights, carried, turn * wide_by, wide_by, dp_size, me
+            group_of(plan), keep_wide, norm_scaled, weights, before, part * wide_by, wide_by, dp_size, me
         )
         kept.append(keep_part)
-        sent.append(send_part)
         last_bias.append(bias_grad)
-        arrived, paired, norm_scaled, sent, kept, last_bias, counts, loss_share = together(
-            arrived, paired, norm_scaled, sent, kept, last_bias, counts, loss_share
-        )
+        return send_part, out_bias_grad
+
+    counts = counts + swapped(counts, "dp", 1)
+    send_part, _ = last_tokens(0, [half], ahead)
+    send_part, kept, norm_scaled, counts = together(send_part, kept, norm_scaled, counts)
+    counts = rest_of(counts)
+    paired.append(swapped(send_part, "dp", 1))
+    send_part, _ = last_tokens(1, [half - 1, half], middle)
+    send_part, kept, norm_scaled, counts, paired = together(send_part, kept, norm_scaled, counts, paired)
+    paired.append(swapped(send_part, "dp", 1))
+    blocks = [crossing(0), crossing(1)]
+    blocks, kept, norm_scaled, paired = together(blocks, kept, norm_scaled, paired)
+    arrived += [crossed(0, blocks[0]), crossed(1, blocks[1])]
+    send_part, out_bias_grad = last_tokens(2, [half - 3, half - 2, half - 1, half], carried)
+    send_part, kept, arrived, last_bias, out_bias_grad = together(send_part, kept, arrived, last_bias, out_bias_grad)
+    paired.append(swapped(send_part, "dp", 1))
+    block = crossing(2)
+    bias_share = jnp.concatenate([sum(middle_biases) + jnp.concatenate([ahead_bias + last_bias[0], last_bias[1]], axis=1), last_bias[2]], axis=1)
+    bias_share = sum(bias_shares) + bias_share
+    out_bias_share = jnp.pad(sum(out_bias_shares) + out_bias_grad, ((0, 0), (0, features - width)))
+    shares = jnp.concatenate([bias_share, out_bias_share])
+    shares = shares + swapped(shares, "dp", 1)
+    block, kept, paired, arrived, shares = together(block, kept, paired, arrived, shares)
     fired, act_total = counts[0], counts[1:]
     penalty = penalty_scale * act_total
-    arrived.append(crossed(LAST_PARTS - 2))
-    paired.append(swapped(sent[-1], "dp", 1))
-    arrived.append(crossed(LAST_PARTS - 1))
-    bias_share = sum(bias_shares) + jnp.concatenate(last_bias, axis=1)
-    out_bias_share = jnp.pad(sum(out_bias_shares) + out_bias_grad, ((0, 0), (0, features - width)))
-    shares = jnp.concatenate([bias_share, out_bias_share])
-    shares = rest_of(shares + swapped(shares, "dp", 1))
+    shares = rest_of(shares)
+    arrived.append(crossed(2, block))
     enc_bias_grad, dec_bias_grad = shares[0], shares[1, :width]
     first_dp = dp_at == 0
     first_both = first_dp & (feat_at == 0)
@@ -796,9 +825,12 @@
     overall_derivative_length = jnp.sqrt(jnp.sum(norms[:8]))
     factor = jnp.minimum(1.0, CLIP_NORM / (overall_derivative_length + 1e-06))
     dec_new, dec_m, dec_v = adamw(dec_weight.T, grads[1] * factor, dec_weight_m.T, dec_weight_v.T, DECAY)
+    dec_new, dec_m, dec_v = together(dec_new, dec_m, dec_v)
     row_squares = jnp.sum(dec_new * dec_new, axis=0, keepdims=True)
-    row_squares = summed(row_squares, ("dp",))
-    enc_new, enc_m, enc_v = adamw(enc_weight, grads[0] * factor, enc_weight_m, enc_weight_v, DECAY)
+    row_squares = row_squares + swapped(row_squares, "dp", 1)
+    enc_grad, row_squares = together(grads[0], row_squares)
+    row_squares = rest_of(row_squares)
+    enc_new, enc_m, enc_v = adamw(enc_weight, enc_grad * factor, enc_weight_m, enc_weight_v, DECAY)
     bias_new, bias_m, bias_v = adamw(enc_bias, enc_bias_grad * factor, enc_bias_m, enc_bias_v, 0.0)
     out_new, out_m, out_v = adamw(dec_bias, dec_bias_grad * factor, dec_bias_m, dec_bias_v, 0.0)
     dec_new = (dec_new * lax.rsqrt(row_squares + 1e-12)).T

time: 435 us -> 425 us (0.977)
  waiting for transfers between devices: 93.6 us -> 80.5 us
  Pallas kernels: 219 us -> 225 us
    ppermute x20 -> x19, waiting for transfers between devices: 37.2 us -> 29.2 us  [swapped(): lax.ppermute(block, axis, [(i, i ^ bit) for i in range(lax.axis_size(axis...]
    sub x3 -> x4, other arithmetic: 5.63 us -> 12.9 us  [adamw(): weight - LEARN * (hat_first / (jnp.sqrt(hat_second) + EPSILON) + decay *...]
    reduce_sum x1, other arithmetic: 7.41 us -> 0.2 us  [shards(): row_squares = jnp.sum(dec_new * dec_new, axis=0, keepdims=True)]
    ppermute x24, waiting for transfers between devices: 51.6 us -> 45.4 us  [ring_shift(): return lax.ppermute(block, 'feat', route)]
    pallas_call x6 -> x7, Pallas kernels: 102 us -> 107 us  [backward(): pl.pallas_call(functools.partial(backward_kernel, counts, carried is not...]
    ppermute x20 -> x19, starting transfers between devices: 14.2 us -> 13.7 us  [swapped(): lax.ppermute(block, axis, [(i, i ^ bit) for i in range(lax.axis_size(axis...]
  transfers between devices with their start and end apart: 46 -> 45, of which waited for: 24 -> 24; matrix products, arithmetic and copies ran while one was open for 8% -> 7% of each run, Pallas kernels for 42% -> 46%
where the time goes in v4:
time: 425 us; the launch traced here: 417 us
  Pallas kernels  225 us (53%)
  waiting for transfers between devices  80.5 us (19%)
  starting transfers between devices  42.7 us (10%)
  other arithmetic  38.4 us (9%)
  between operations  19.2 us (5%)
  local copies, waits for them, and re-layouts  11.8 us (3%)
    pallas_call x7, Pallas kernels, backward(): pl.pallas_call(functools.partial(backward_kernel, counts, carried is not...  107 us
    pallas_call x6, Pallas kernels, encode(): pl.pallas_call(functools.partial(encode_kernel, len(pieces)), grid=(featu...  83.8 us
    ppermute x24, waiting for transfers between devices, ring_shift(): return lax.ppermute(block, 'feat', route)  45.4 us
    ppermute x19, waiting for transfers between devices, swapped(): lax.ppermute(block, axis, [(i, i ^ bit) for i in range(lax.axis_size(axis...  29.2 us
    ppermute x24, starting transfers between devices, ring_shift(): return lax.ppermute(block, 'feat', route)  25.9 us
    ppermute x19, starting transfers between devices, swapped(): lax.ppermute(block, axis, [(i, i ^ bit) for i in range(lax.axis_size(axis...  13.7 us
    sub x4, other arithmetic, adamw(): weight - LEARN * (hat_first / (jnp.sqrt(hat_second) + EPSILON) + decay *...  12.9 us
    pallas_call x3, Pallas kernels, finished(): pl.pallas_call(functools.partial(finished_kernel, len(arrived), first), g...  9.49 us
  transfers between devices with their start and end apart: 45, of which 24 were waited for; matrix products, arithmetic and copies ran while one was open for 7% of the time, Pallas kernels for 46%

profile of v4, /device:TPU:0, one launch (start us, length us, event | category | flops | bytes accessed | tf_op | source)
XLA Modules:
  0.0 417.3 jit_solution(6274630487949250848)
XLA Ops:
  7.2 3.5 packed.1.refs_2_
  11.7 3.0 collective-permute-start
  15.4 6.3 %project.1.own_ref = bf16[512,2304]{1,0:T(8,128)(2,1)} custom-call(bf16[512,768]{1,0:T(8,128)(2,1)} %rows_ref.1, bf16[768]{0:T(1024)(128)(2,1)} %gain_ref.3, bf16[768]{0:T(1024)(128)(2,1)} %bias_ref.3, bf16[768,2304]{1,0:T(8,128)(2,1)} %w_ref.3, bf16[2304]{0:T(1024)(128)(2,1)} %wb_ref.3), custom_call_target="tpu_custom_call" | custom-call | flops 1811939328 | bytes 3538944 | tf_op jit(solution)/shard_map/project/pallas_call | solution.py:82
  23.5 6.8 %attend.1.refs_0_.z_ref.refs_1_ = bf16[512,768]{1,0:T(8,128)(2,1)} custom-call(bf16[512,2304]{1,0:T(8,128)(2,1)} %project.1.own_ref, bf16[128,768]{1,0:T(8,128)(2,1)} %copy-done.35, s32[512,128]{1,0:T(8,128)} %broadcast_in_dim.56.seg_q_ref, s32[1,640]{1,0:T(1,128)} %broadcast_in_dim.55.seg_k_ref, bf16[768]{0:T(1024)(128)(2,1)} %gain_ref.3, ...), custom_call_target="tpu_custom_call" | custom-call | flops 1207959552 | bytes 4718592 | tf_op jit(solution)/shard_map/attend/pallas_call | solution.py:152
  33.8 15.4 %collective-permute-done.2.refs_1_.refs_2_.refs_3_ = bf16[512,768]{1,0:T(8,128)(2,1)S(1)} collective-permute-done((bf16[512,768]{1,0:T(8,128)(2,1)}, bf16[512,768]{1,0:T(8,128)(2,1)S(1)}, u32[]{:S(2)}, u32[]{:S(2)}) %collective-permute-start.2) | collective-permute-done | bytes 786464 | tf_op jit(solution)/shard_map/ppermute | solution.py:561
  53.7 14.9 %collective-permute-done.3.refs_0_.refs_1_.refs_8_ = bf16[512,768]{1,0:T(8,128)(2,1)} collective-permute-done((bf16[512,768]{1,0:T(8,128)(2,1)S(1)}, bf16[512,768]{1,0:T(8,128)(2,1)}, u32[]{:S(2)}, u32[]{:S(2)}) %collective-permute-start.3) | collective-permute-done | bytes 786464 | tf_op jit(solution)/shard_map/ppermute | solution.py:561
  69.0 1.7 collective-permute-start.5
  71.0 1.8 multiply_reduce_fusion.2
  72.9 5.0 %all-gather.3.cloned.1.call-done = bf16[8,192,3072]{2,1,0:T(8,128)(2,1)} async-done(((bf16[2,192,3072]{2,1,0:T(8,128)(2,1)}), bf16[8,192,3072]{2,1,0:T(8,128)(2,1)}) %all-gather.3.cloned.1.call-update) | async-done | bytes 9437200 | tf_op jit(solution)/shard_map/all_gather | solution.py:626
  77.8 3.3 multiply_reduce_fusion
  81.7 4.2 %collective-permute-done.5.refs_0_.refs_1_.refs_2_.refs_14_ = bf16[512,768]{1,0:T(8,128)(2,1)S(1)} collective-permute-done((bf16[512,768]{1,0:T(8,128)(2,1)}, bf16[512,768]{1,0:T(8,128)(2,1)S(1)}, u32[]{:S(2)}, u32[]{:S(2)}) %collective-permute-start.5) | collective-permute-done | bytes 786464 | tf_op jit(solution)/shard_map/ppermute | solution.py:561
  86.0 1.8 collective-permute-done.6.refs_0_.refs_5_.refs_6_.refs_18_
  87.8 1.6 collective-permute-start.7
  90.2 12.3 %encode.6 = (bf16[512,3072]{1,0:T(8,128)(2,1)}, bf16[512,768]{1,0:T(8,128)(2,1)}, f32[1,3072]{1,0:T(1,128)}, f32[1,3072]{1,0:T(1,128)}, f32[1,768]{1,0:T(1,128)}) custom-call(bf16[512,768]{1,0:T(8,128)(2,1)} %copy-done.4, f32[4096,128]{1,0:T(8,128)} %copy-done, bf16[4,2,192,3072]{3,2,1,0:T(8,128)(2,1)} %bitcast.40, f32[1,3072]{1,0:T(1,128)} %bitcast.62, ...), custom_call_target="tpu_custom_call" | custom-call | flops 1207959552 | bytes 3932160 | tf_op jit(solution)/shard_map/encode/pallas_call | solution.py:262
  103.4 11.4 %encode.7 = (bf16[512,3072]{1,0:T(8,128)(2,1)}, bf16[256,768]{1,0:T(8,128)(2,1)}, bf16[256,768]{1,0:T(8,128)(2,1)}, f32[1,3072]{1,0:T(1,128)}, f32[1,3072]{1,0:T(1,128)}, /*index=5*/f32[1,768]{1,0:T(1,128)}) custom-call(bf16[256,768]{1,0:T(8,128)(2,1)} %copy-done.14, bf16[256,768]{1,0:T(8,128)(2,1)} %copy-done.15, f32[4096,128]{1,0:T(8,128)} %copy-done, ...), custom_call_target="tpu_custom_call" | custom-call | flops 1207959552 | bytes 3932160 | tf_op jit(solution)/shard_map/encode/pallas_call | solution.py:262
  114.8 1.6 collective-permute-start.9
  116.9 12.2 %encode.8 = (bf16[512,3072]{1,0:T(8,128)(2,1)}, bf16[512,768]{1,0:T(8,128)(2,1)}, f32[1,3072]{1,0:T(1,128)}, f32[1,3072]{1,0:T(1,128)}, f32[1,768]{1,0:T(1,128)}) custom-call(bf16[512,768]{1,0:T(8,128)(2,1)} %copy-done.5, f32[4096,128]{1,0:T(8,128)} %copy-done, bf16[4,2,192,3072]{3,2,1,0:T(8,128)(2,1)} %bitcast.44, f32[1,3072]{1,0:T(1,128)} %bitcast.64, ...), custom_call_target="tpu_custom_call" | custom-call | flops 1207959552 | bytes 3932160 | tf_op jit(solution)/shard_map/encode/pallas_call | solution.py:262
  130.7 3.6 joined.1
  138.2 1.6 collective-permute-start.14
  139.7 17.8 %encode.9 = (bf16[1024,3072]{1,0:T(8,128)(2,1)}, bf16[512,768]{1,0:T(8,128)(2,1)}, bf16[512,768]{1,0:T(8,128)(2,1)}, f32[1,3072]{1,0:T(1,128)}, f32[1,3072]{1,0:T(1,128)}, /*index=5*/f32[1,768]{1,0:T(1,128)}) custom-call(bf16[512,768]{1,0:T(8,128)(2,1)} %collective-permute-done.3.refs_0_.refs_1_.refs_8_, ...), custom_call_target="tpu_custom_call" | custom-call | flops 2415919104 | bytes 5505024 | tf_op jit(solution)/shard_map/encode/pallas_call | solution.py:262
  159.7 1.7 collective-permute-start.15
  161.8 17.8 %encode.10 = (bf16[1024,3072]{1,0:T(8,128)(2,1)}, bf16[512,768]{1,0:T(8,128)(2,1)}, bf16[512,768]{1,0:T(8,128)(2,1)}, f32[1,3072]{1,0:T(1,128)}, f32[1,3072]{1,0:T(1,128)}, /*index=5*/f32[1,768]{1,0:T(1,128)}) custom-call(bf16[512,768]{1,0:T(8,128)(2,1)} %copy-done.7, bf16[512,768]{1,0:T(8,128)(2,1)} %copy-done.6, f32[4096,128]{1,0:T(8,128)} %copy-done, ...), custom_call_target="tpu_custom_call" | custom-call | flops 2415919104 | bytes 5505024 | tf_op jit(solution)/shard_map/encode/pallas_call | solution.py:262
  184.9 12.3 %encode.11 = (bf16[512,3072]{1,0:T(8,128)(2,1)}, bf16[512,768]{1,0:T(8,128)(2,1)}, f32[1,3072]{1,0:T(1,128)}, f32[1,3072]{1,0:T(1,128)}, f32[1,768]{1,0:T(1,128)}) custom-call(bf16[512,768]{1,0:T(8,128)(2,1)} %attend.1.refs_0_.z_ref.refs_1_, f32[4096,128]{1,0:T(8,128)} %copy-done, bf16[4,2,192,3072]{3,2,1,0:T(8,128)(2,1)} %bitcast.50, f32[1,3072]{1,0:T(1,128)} %bitcast.67, ...), custom_call_target="tpu_custom_call" | custom-call | flops 1207959552 | bytes 3932160 | tf_op jit(solution)/shard_map/encode/pallas_call | solution.py:262
  197.2 3.1 collective-permute-done.17.right_ref
  202.5 4.4 %compared.1 = (bf16[512,768]{1,0:T(8,128)(2,1)}, f32[8,128]{1,0:T(8,128)}, f32[1,3072]{1,0:T(1,128)}, f32[1,3072]{1,0:T(1,128)}, f32[8,128]{1,0:T(8,128)}) custom-call(bf16[512,768]{1,0:T(8,128)(2,1)} %get-tuple-element.300.rec_ref, bf16[512,768]{1,0:T(8,128)(2,1)} %copy-done.28, bf16[512,768]{1,0:T(8,128)(2,1)} %copy-done.29, ...), custom_call_target="tpu_custom_call" | custom-call | tf_op jit(solution)/shard_map/compared/pallas_call | solution.py:347
  209.0 13.3 %backward.7 = (f32[768,3072]{1,0:T(8,128)}, f32[768,3072]{1,0:T(8,128)}, f32[1,3072]{1,0:T(1,128)}, f32[1,768]{1,0:T(1,128)}) custom-call(bf16[512,3072]{1,0:T(8,128)(2,1)} %get-tuple-element.309.refs_0_, bf16[512,768]{1,0:T(8,128)(2,1)} %attend.1.refs_0_.z_ref.refs_1_, bf16[512,768]{1,0:T(8,128)(2,1)} %get-tuple-element.308.refs_2_, f32[4096,128]{1,0:T(8,128)} %copy-done, ...), custom_call_target="tpu_custom_call" | custom-call | flops 1811939328 | bytes 10223616 | tf_op jit(solution)/shard_map/backward/pallas_call | solution.py:486
  222.3 2.1 collective-permute-done.20.refs_4_.refs_5_
  227.2 16.5 %backward.8 = (f32[768,2048]{1,0:T(8,128)}, f32[768,2048]{1,0:T(8,128)}, f32[1,2048]{1,0:T(1,128)}, f32[1,768]{1,0:T(1,128)}) custom-call(bf16[1024,3072]{1,0:T(8,128)(2,1)} %get-tuple-element.278.refs_0_.refs_1_, bf16[512,768]{1,0:T(8,128)(2,1)} %copy-done.7, bf16[512,768]{1,0:T(8,128)(2,1)} %copy-done.6, bf16[512,768]{1,0:T(8,128)(2,1)} %copy-done.21, ...), custom_call_target="tpu_custom_call" | custom-call | flops 2415919104 | bytes 7340032 | tf_op jit(solution)/shard_map/backward/pallas_call | solution.py:486
  246.6 16.5 %backward.9 = (f32[768,2048]{1,0:T(8,128)}, f32[768,2048]{1,0:T(8,128)}, f32[1,2048]{1,0:T(1,128)}, f32[1,768]{1,0:T(1,128)}) custom-call(bf16[1024,3072]{1,0:T(8,128)(2,1)} %get-tuple-element.315.refs_0_.refs_7_, bf16[512,768]{1,0:T(8,128)(2,1)} %collective-permute-done.3.refs_0_.refs_1_.refs_8_, ...), custom_call_target="tpu_custom_call" | custom-call | flops 2415919104 | bytes 7340032 | tf_op jit(solution)/shard_map/backward/pallas_call | solution.py:486
  265.6 10.3 %backward.10 = (f32[768,1024]{1,0:T(8,128)}, f32[768,1024]{1,0:T(8,128)}, f32[1,1024]{1,0:T(1,128)}, f32[1,768]{1,0:T(1,128)}) custom-call(bf16[512,3072]{1,0:T(8,128)(2,1)} %get-tuple-element.322.refs_0_.refs_1_.refs_13_, bf16[512,768]{1,0:T(8,128)(2,1)} %copy-done.4, bf16[512,768]{1,0:T(8,128)(2,1)} %copy-done.8, f32[4096,128]{1,0:T(8,128)} %copy-done, ...), custom_call_target="tpu_custom_call" | custom-call | flops 1207959552 | bytes 3670016 | tf_op jit(solution)/shard_map/backward/pallas_call | solution.py:486
  276.8 7.8 %backward.11 = (f32[2,2,192,1024]{3,2,1,0:T(8,128)}, bf16[2,2,192,1024]{3,2,1,0:T(8,128)(2,1)}, f32[1,1024]{1,0:T(1,128)}, f32[1,768]{1,0:T(1,128)}) custom-call(s32[1]{0:T(128)} %bitcast.refs_0_, bf16[512,3072]{1,0:T(8,128)(2,1)} %get-tuple-element.331.refs_1_.refs_9_.refs_21_, bf16[256,768]{1,0:T(8,128)(2,1)} %copy-done.14, bf16[256,768]{1,0:T(8,128)(2,1)} %copy-done.15, ...), custom_call_target="tpu_custom_call" | custom-call | flops 603979776 | bytes 3407872 | tf_op jit(solution)/shard_map/backward/pallas_call | solution.py:486
  285.1 14.6 %backward.12 = (f32[2,2,192,1024]{3,2,1,0:T(8,128)}, bf16[2,2,192,1024]{3,2,1,0:T(8,128)(2,1)}, f32[1,1024]{1,0:T(1,128)}, f32[1,768]{1,0:T(1,128)}) custom-call(s32[1]{0:T(128)} %bitcast.refs_0_, bf16[512,3072]{1,0:T(8,128)(2,1)} %get-tuple-element.322.refs_0_.refs_1_.refs_13_, bf16[512,768]{1,0:T(8,128)(2,1)} %copy-done.4, bf16[512,768]{1,0:T(8,128)(2,1)} %copy-done.8, ...), custom_call_target="tpu_custom_call" | custom-call | flops 1811939328 | bytes 3932160 | tf_op jit(solution)/shard_map/backward/pallas_call | solution.py:486
  299.8 2.4 fusion.2
  306.6 27.8 %backward.13 = (f32[2,2,192,1024]{3,2,1,0:T(8,128)}, bf16[2,2,192,1024]{3,2,1,0:T(8,128)(2,1)}, f32[1,1024]{1,0:T(1,128)}, f32[1,768]{1,0:T(1,128)}) custom-call(s32[1]{0:T(128)} %bitcast.refs_0_, bf16[1024,3072]{1,0:T(8,128)(2,1)} %get-tuple-element.278.refs_0_.refs_1_, bf16[512,768]{1,0:T(8,128)(2,1)} %copy-done.7, bf16[512,768]{1,0:T(8,128)(2,1)} %copy-done.6, ...), custom_call_target="tpu_custom_call" | custom-call | flops 4227858432 | bytes 4980736 | tf_op jit(solution)/shard_map/backward/pallas_call | solution.py:486
  334.5 6.7 %collective-permute-done.32.refs_0_ = bf16[2,192,1024]{2,1,0:T(8,128)(2,1)S(1)} collective-permute-done((bf16[2,192,1024]{2,1,0:T(8,128)(2,1)S(1)}, bf16[2,192,1024]{2,1,0:T(8,128)(2,1)S(1)}, u32[]{:S(2)}, u32[]{:S(2)}) %collective-permute-start.32) | collective-permute-done | bytes 786464 | tf_op jit(solution)/shard_map/ppermute | solution.py:565
  344.8 3.1 fusion.4
  350.6 3.1 finished.3
  353.7 3.1 finished.4
  359.3 9.7 %collective-permute-done.36.refs_0_ = bf16[2,192,1024]{2,1,0:T(8,128)(2,1)} collective-permute-done((bf16[2,192,1024]{2,1,0:T(8,128)(2,1)}, bf16[2,192,1024]{2,1,0:T(8,128)(2,1)}, u32[]{:S(2)}, u32[]{:S(2)}) %collective-permute-start.36) | collective-permute-done | bytes 786464 | tf_op jit(solution)/shard_map/ppermute | solution.py:565
  369.0 3.4 finished.5
  375.2 2.8 collective-permute-done.38
  379.2 2.5 collective-permute-done.39
  383.0 2.3 collective-permute-done.40
  385.4 2.5 collective-permute-start.41
  391.4 7.3 %multiply_subtract_fusion.1 = (f32[192,3072]{1,0:T(8,128)S(1)}, f32[192,3072]{1,0:T(8,128)}, f32[192,3072]{1,0:T(8,128)}) fusion(f32[3072,192]{0,1:T(8,128)S(1)} %copy-done.10, f32[192,3072]{1,0:T(8,128)} %get-tuple-element.415, f32[]{:T(128)S(6)} %min_shard_map.3, f32[3072,192]{0,1:T(8,128)} %param.36, f32[3072,192]{0,1:T(8,128)} %param.37), kind=kLoop, calls=%fused_computation.12 | loop fusion | flops 9437184 | bytes 16515076 | tf_op jit(solution)/shard_map/sub | solution.py:582
  400.2 1.9 pad_maximum_fusion.2
  403.0 4.4 %multiply_subtract_fusion = (f32[192,3072]{1,0:T(8,128)}, f32[192,3072]{1,0:T(8,128)}, f32[192,3072]{1,0:T(8,128)}) fusion(f32[192,3072]{1,0:T(8,128)S(1)} %copy-done.11, f32[192,3072]{1,0:T(8,128)S(1)} %copy-done.2, f32[]{:T(128)S(6)} %min_shard_map.3, f32[192,3072]{1,0:T(8,128)S(1)} %copy-done.24, f32[192,3072]{1,0:T(8,128)S(1)} %copy-done.25), kind=kLoop, calls=%fused_computation.9 | loop fusion | flops 9437184 | bytes 16515076 | tf_op jit(solution)/shard_map/sub | solution.py:582
  407.4 1.8 multiply_bitcast_fusion
  (287 shorter events, 63.2 us)
Async XLA Ops:
  7.2 70.7 %all-gather.3.cloned.1.call-start = ((), (), s32[]{:S(2)}) async-start(), calls=%async_computation | async-start | bytes 11796480 | tf_op jit(solution)/shard_map/all_gather | solution.py:626
  11.7 10.9 %collective-permute-start = (bf16[128,768]{1,0:T(8,128)(2,1)S(1)}, bf16[128,768]{1,0:T(8,128)(2,1)S(1)}, u32[]{:S(2)}, u32[]{:S(2)}) collective-permute-start(bf16[128,768]{1,0:T(8,128)(2,1)S(1)} %slice.72), channel_id=1, source_target_pairs={{0,1},{1,2},{2,3},{3,4},{4,5},{5,6},{6,7},{7,0},{8,9},{9,10},{10,1... | collective-permute-start | bytes 589832 | tf_op jit(solution)/shard_map/ppermute | solution.py:627
  30.3 18.8 %collective-permute-start.2 = (bf16[512,768]{1,0:T(8,128)(2,1)}, bf16[512,768]{1,0:T(8,128)(2,1)S(1)}, u32[]{:S(2)}, u32[]{:S(2)}) collective-permute-start(bf16[512,768]{1,0:T(8,128)(2,1)} %attend.1.refs_0_.z_ref.refs_1_), channel_id=1, source_target_pairs={{0,1},{2,0},{4,2},{6,4},{7,6},{5,7},{3,5},{1,3},{8,9},{10,8},{12,1... | collective-permute-start | bytes 2359304 | tf_op jit(solution)/shard_map/ppermute | solution.py:561
  30.9 19.0 %collective-permute-start.1 = (bf16[512,768]{1,0:T(8,128)(2,1)}, bf16[512,768]{1,0:T(8,128)(2,1)S(1)}, u32[]{:S(2)}, u32[]{:S(2)}) collective-permute-start(bf16[512,768]{1,0:T(8,128)(2,1)} %attend.1.refs_0_.z_ref.refs_1_), channel_id=1, source_target_pairs={{0,2},{2,4},{4,6},{6,7},{7,5},{5,3},{3,1},{1,0},{8,10},{10,12},{12... | collective-permute-start | bytes 2359304 | tf_op jit(solution)/shard_map/ppermute | solution.py:561
  50.5 18.1 %collective-permute-start.3 = (bf16[512,768]{1,0:T(8,128)(2,1)S(1)}, bf16[512,768]{1,0:T(8,128)(2,1)}, u32[]{:S(2)}, u32[]{:S(2)}) collective-permute-start(bf16[512,768]{1,0:T(8,128)(2,1)S(1)} %collective-permute-done.1.refs_0_.refs_1_.refs_2_), channel_id=1, source_target_pairs={{0,2},{2,4},{4,6},{6,7},{7,5},{5,3},{3,1},{1,0},{8,10},{10,12},{12... | collective-permute-start | bytes 2359304 | tf_op jit(solution)/shard_map/ppermute | solution.py:561
  51.6 17.4 %collective-permute-start.4 = (bf16[512,768]{1,0:T(8,128)(2,1)S(1)}, bf16[512,768]{1,0:T(8,128)(2,1)}, u32[]{:S(2)}, u32[]{:S(2)}) collective-permute-start(bf16[512,768]{1,0:T(8,128)(2,1)S(1)} %collective-permute-done.2.refs_1_.refs_2_.refs_3_), channel_id=1, source_target_pairs={{0,1},{2,0},{4,2},{6,4},{7,6},{5,7},{3,5},{1,3},{8,9},{10,8},{12,1... | collective-permute-start | bytes 2359304 | tf_op jit(solution)/shard_map/ppermute | solution.py:561
  69.0 17.0 %collective-permute-start.5 = (bf16[512,768]{1,0:T(8,128)(2,1)}, bf16[512,768]{1,0:T(8,128)(2,1)S(1)}, u32[]{:S(2)}, u32[]{:S(2)}) collective-permute-start(bf16[512,768]{1,0:T(8,128)(2,1)} %collective-permute-done.3.refs_0_.refs_1_.refs_8_), channel_id=1, source_target_pairs={{0,2},{2,4},{4,6},{6,7},{7,5},{5,3},{3,1},{1,0},{8,10},{10,12},{12... | collective-permute-start | bytes 2359304 | tf_op jit(solution)/shard_map/ppermute | solution.py:561
  70.7 17.0 %collective-permute-start.6 = (bf16[512,768]{1,0:T(8,128)(2,1)}, bf16[512,768]{1,0:T(8,128)(2,1)S(1)}, u32[]{:S(2)}, u32[]{:S(2)}) collective-permute-start(bf16[512,768]{1,0:T(8,128)(2,1)} %collective-permute-done.4.refs_1_.refs_2_.refs_9_), channel_id=1, source_target_pairs={{0,1},{2,0},{4,2},{6,4},{7,6},{5,7},{3,5},{1,3},{8,9},{10,8},{12,1... | collective-permute-start | bytes 2359304 | tf_op jit(solution)/shard_map/ppermute | solution.py:561
  87.8 14.7 %collective-permute-start.7 = (bf16[256,768]{1,0:T(8,128)(2,1)S(1)}, bf16[256,768]{1,0:T(8,128)(2,1)S(1)}, u32[]{:S(2)}, u32[]{:S(2)}) collective-permute-start(bf16[256,768]{1,0:T(8,128)(2,1)S(1)} %slice.79), channel_id=1, source_target_pairs={{0,2},{2,4},{4,6},{6,7},{7,5},{5,3},{3,1},{1,0},{8,10},{10,12},{12... | collective-permute-start | bytes 1179656 | tf_op jit(solution)/shard_map/ppermute | solution.py:561
  89.4 13.1 %collective-permute-start.8 = (bf16[256,768]{1,0:T(8,128)(2,1)S(1)}, bf16[256,768]{1,0:T(8,128)(2,1)S(1)}, u32[]{:S(2)}, u32[]{:S(2)}) collective-permute-start(bf16[256,768]{1,0:T(8,128)(2,1)S(1)} %slice.80), channel_id=1, source_target_pairs={{0,1},{2,0},{4,2},{6,4},{7,6},{5,7},{3,5},{1,3},{8,9},{10,8},{12,1... | collective-permute-start | bytes 1179656 | tf_op jit(solution)/shard_map/ppermute | solution.py:561
  114.8 15.0 %collective-permute-start.9 = (bf16[256,768]{1,0:T(8,128)(2,1)}, bf16[256,768]{1,0:T(8,128)(2,1)S(1)}, u32[]{:S(2)}, u32[]{:S(2)}) collective-permute-start(bf16[256,768]{1,0:T(8,128)(2,1)} %get-tuple-element.238), channel_id=1, source_target_pairs={{0,2},{2,4},{4,6},{6,7},{7,5},{5,3},{3,1},{1,0},{8,10},{10,12},{12... | collective-permute-start | bytes 1179656 | tf_op jit(solution)/shard_map/ppermute | solution.py:561
  116.4 13.4 %collective-permute-start.10 = (bf16[256,768]{1,0:T(8,128)(2,1)}, bf16[256,768]{1,0:T(8,128)(2,1)S(1)}, u32[]{:S(2)}, u32[]{:S(2)}) collective-permute-start(bf16[256,768]{1,0:T(8,128)(2,1)} %get-tuple-element.239), channel_id=1, source_target_pairs={{0,1},{2,0},{4,2},{6,4},{7,6},{5,7},{3,5},{1,3},{8,9},{10,8},{12,1... | collective-permute-start | bytes 1179656 | tf_op jit(solution)/shard_map/ppermute | solution.py:561
  134.4 23.8 %collective-permute-start.11 = (bf16[512,768]{1,0:T(8,128)(2,1)}, bf16[512,768]{1,0:T(8,128)(2,1)S(1)}, u32[]{:S(2)}, u32[]{:S(2)}) collective-permute-start(bf16[512,768]{1,0:T(8,128)(2,1)} %get-tuple-element.255), channel_id=1, source_target_pairs={{0,2},{2,4},{4,6},{6,7},{7,5},{5,3},{3,1},{1,0},{8,10},{10,12},{12... | collective-permute-start | bytes 2359304 | tf_op jit(solution)/shard_map/ppermute | solution.py:561
  135.9 22.3 %collective-permute-start.12 = (bf16[512,768]{1,0:T(8,128)(2,1)}, bf16[512,768]{1,0:T(8,128)(2,1)S(1)}, u32[]{:S(2)}, u32[]{:S(2)}) collective-permute-start(bf16[512,768]{1,0:T(8,128)(2,1)} %get-tuple-element.256), channel_id=1, source_target_pairs={{0,1},{2,0},{4,2},{6,4},{7,6},{5,7},{3,5},{1,3},{8,9},{10,8},{12,1... | collective-permute-start | bytes 2359304 | tf_op jit(solution)/shard_map/ppermute | solution.py:561
  136.9 1.2 collective-permute-start.13
  138.2 19.4 %collective-permute-start.14 = (f32[2,768]{1,0:T(2,128)S(1)}, f32[2,768]{1,0:T(2,128)S(1)}, u32[]{:S(2)}, u32[]{:S(2)}) collective-permute-start(f32[2,768]{1,0:T(2,128)S(1)} %fusion.15), channel_id=1, source_target_pairs={{0,16},{8,24},{16,0},{24,8},{1,17},{9,25},{17,1},{25,9},{2,18},{10... | collective-permute-start | bytes 18440 | tf_op jit(solution)/shard_map/ppermute | solution.py:565
  159.7 19.9 %collective-permute-start.15 = (bf16[512,768]{1,0:T(8,128)(2,1)S(1)}, bf16[512,768]{1,0:T(8,128)(2,1)S(1)}, u32[]{:S(2)}, u32[]{:S(2)}) collective-permute-start(bf16[512,768]{1,0:T(8,128)(2,1)S(1)} %add_convert_fusion.6), channel_id=1, source_target_pairs={{0,2},{2,4},{4,6},{6,7},{7,5},{5,3},{3,1},{1,0},{8,10},{10,12},{12... | collective-permute-start | bytes 2359304 | tf_op jit(solution)/shard_map/ppermute | solution.py:561
  161.4 19.1 %collective-permute-start.16 = (bf16[512,768]{1,0:T(8,128)(2,1)S(1)}, bf16[512,768]{1,0:T(8,128)(2,1)S(1)}, u32[]{:S(2)}, u32[]{:S(2)}) collective-permute-start(bf16[512,768]{1,0:T(8,128)(2,1)S(1)} %add_convert_fusion.5), channel_id=1, source_target_pairs={{0,1},{2,0},{4,2},{6,4},{7,6},{5,7},{3,5},{1,3},{8,9},{10,8},{12,1... | collective-permute-start | bytes 2359304 | tf_op jit(solution)/shard_map/ppermute | solution.py:561
  182.0 18.3 %collective-permute-start.17 = (bf16[512,768]{1,0:T(8,128)(2,1)S(1)}, bf16[512,768]{1,0:T(8,128)(2,1)S(1)}, u32[]{:S(2)}, u32[]{:S(2)}) collective-permute-start(bf16[512,768]{1,0:T(8,128)(2,1)S(1)} %add_convert_fusion.4), channel_id=1, source_target_pairs={{0,2},{2,4},{4,6},{6,7},{7,5},{5,3},{3,1},{1,0},{8,10},{10,12},{12... | collective-permute-start | bytes 2359304 | tf_op jit(solution)/shard_map/ppermute | solution.py:561
  183.3 18.3 %collective-permute-start.18 = (bf16[512,768]{1,0:T(8,128)(2,1)S(1)}, bf16[512,768]{1,0:T(8,128)(2,1)S(1)}, u32[]{:S(2)}, u32[]{:S(2)}) collective-permute-start(bf16[512,768]{1,0:T(8,128)(2,1)S(1)} %add_convert_fusion.3), channel_id=1, source_target_pairs={{0,1},{2,0},{4,2},{6,4},{7,6},{5,7},{3,5},{1,3},{8,9},{10,8},{12,1... | collective-permute-start | bytes 2359304 | tf_op jit(solution)/shard_map/ppermute | solution.py:561
  206.9 17.5 %collective-permute-start.20 = (bf16[512,768]{1,0:T(8,128)(2,1)}, bf16[512,768]{1,0:T(8,128)(2,1)S(1)}, u32[]{:S(2)}, u32[]{:S(2)}) collective-permute-start(bf16[512,768]{1,0:T(8,128)(2,1)} %get-tuple-element.308.refs_2_), channel_id=1, source_target_pairs={{0,1},{2,0},{4,2},{6,4},{7,6},{5,7},{3,5},{1,3},{8,9},{10,8},{12,1... | collective-permute-start | bytes 2359304 | tf_op jit(solution)/shard_map/ppermute | solution.py:561
  207.6 17.5 %collective-permute-start.19 = (bf16[512,768]{1,0:T(8,128)(2,1)}, bf16[512,768]{1,0:T(8,128)(2,1)S(1)}, u32[]{:S(2)}, u32[]{:S(2)}) collective-permute-start(bf16[512,768]{1,0:T(8,128)(2,1)} %get-tuple-element.308.refs_2_), channel_id=1, source_target_pairs={{0,2},{2,4},{4,6},{6,7},{7,5},{5,3},{3,1},{1,0},{8,10},{10,12},{12... | collective-permute-start | bytes 2359304 | tf_op jit(solution)/shard_map/ppermute | solution.py:561
  225.1 18.6 %collective-permute-start.21 = (bf16[512,768]{1,0:T(8,128)(2,1)S(1)}, bf16[512,768]{1,0:T(8,128)(2,1)S(1)}, u32[]{:S(2)}, u32[]{:S(2)}) collective-permute-start(bf16[512,768]{1,0:T(8,128)(2,1)S(1)} %collective-permute-done.19.refs_3_.refs_4_), channel_id=1, source_target_pairs={{0,2},{2,4},{4,6},{6,7},{7,5},{5,3},{3,1},{1,0},{8,10},{10,12},{12... | collective-permute-start | bytes 2359304 | tf_op jit(solution)/shard_map/ppermute | solution.py:561
  226.4 17.3 %collective-permute-start.22 = (bf16[512,768]{1,0:T(8,128)(2,1)S(1)}, bf16[512,768]{1,0:T(8,128)(2,1)S(1)}, u32[]{:S(2)}, u32[]{:S(2)}) collective-permute-start(bf16[512,768]{1,0:T(8,128)(2,1)S(1)} %collective-permute-done.20.refs_4_.refs_5_), channel_id=1, source_target_pairs={{0,1},{2,0},{4,2},{6,4},{7,6},{5,7},{3,5},{1,3},{8,9},{10,8},{12,1... | collective-permute-start | bytes 2359304 | tf_op jit(solution)/shard_map/ppermute | solution.py:561
  243.7 19.4 %collective-permute-start.23 = (bf16[512,768]{1,0:T(8,128)(2,1)S(1)}, bf16[512,768]{1,0:T(8,128)(2,1)S(1)}, u32[]{:S(2)}, u32[]{:S(2)}) collective-permute-start(bf16[512,768]{1,0:T(8,128)(2,1)S(1)} %collective-permute-done.21.refs_3_.refs_10_), channel_id=1, source_target_pairs={{0,2},{2,4},{4,6},{6,7},{7,5},{5,3},{3,1},{1,0},{8,10},{10,12},{12... | collective-permute-start | bytes 2359304 | tf_op jit(solution)/shard_map/ppermute | solution.py:561
  245.1 18.1 %collective-permute-start.24 = (bf16[512,768]{1,0:T(8,128)(2,1)S(1)}, bf16[512,768]{1,0:T(8,128)(2,1)S(1)}, u32[]{:S(2)}, u32[]{:S(2)}) collective-permute-start(bf16[512,768]{1,0:T(8,128)(2,1)S(1)} %collective-permute-done.22.refs_4_.refs_11_), channel_id=1, source_target_pairs={{0,1},{2,0},{4,2},{6,4},{7,6},{5,7},{3,5},{1,3},{8,9},{10,8},{12,1... | collective-permute-start | bytes 2359304 | tf_op jit(solution)/shard_map/ppermute | solution.py:561
  246.5 19.0 %collective-permute-start.27 = (f32[2,3072]{1,0:T(2,128)S(1)}, f32[2,3072]{1,0:T(2,128)S(1)}, u32[]{:S(2)}, u32[]{:S(2)}) collective-permute-start(f32[2,3072]{1,0:T(2,128)S(1)} %pad_maximum_fusion), channel_id=1, source_target_pairs={{0,8},{8,0},{16,24},{24,16},{1,9},{9,1},{17,25},{25,17},{2,10},{10... | collective-permute-start | bytes 73736 | tf_op jit(solution)/shard_map/ppermute | solution.py:565
  263.3 12.6 %collective-permute-start.26 = (bf16[256,768]{1,0:T(8,128)(2,1)S(1)}, bf16[256,768]{1,0:T(8,128)(2,1)S(1)}, u32[]{:S(2)}, u32[]{:S(2)}) collective-permute-start(bf16[256,768]{1,0:T(8,128)(2,1)S(1)} %slice.82), channel_id=1, source_target_pairs={{0,1},{2,0},{4,2},{6,4},{7,6},{5,7},{3,5},{1,3},{8,9},{10,8},{12,1... | collective-permute-start | bytes 1179656 | tf_op jit(solution)/shard_map/ppermute | solution.py:561
  264.1 11.8 %collective-permute-start.25 = (bf16[256,768]{1,0:T(8,128)(2,1)S(1)}, bf16[256,768]{1,0:T(8,128)(2,1)S(1)}, u32[]{:S(2)}, u32[]{:S(2)}) collective-permute-start(bf16[256,768]{1,0:T(8,128)(2,1)S(1)} %slice.81), channel_id=1, source_target_pairs={{0,2},{2,4},{4,6},{6,7},{7,5},{5,3},{3,1},{1,0},{8,10},{10,12},{12... | collective-permute-start | bytes 1179656 | tf_op jit(solution)/shard_map/ppermute | solution.py:561
  284.6 15.1 %collective-permute-start.29 = (bf16[2,2,192,1024]{3,2,1,0:T(8,128)(2,1)}, bf16[2,2,192,1024]{3,2,1,0:T(8,128)(2,1)}, u32[]{:S(2)}, u32[]{:S(2)}) collective-permute-start(bf16[2,2,192,1024]{3,2,1,0:T(8,128)(2,1)} %get-tuple-element.358), channel_id=1, source_target_pairs={{0,8},{8,0},{16,24},{24,16},{1,9},{9,1},{17,25},{25,17},{2,10},{10... | collective-permute-start | bytes 4718600 | tf_op jit(solution)/shard_map/ppermute | solution.py:565
  284.7 15.0 %collective-permute-start.28 = (f32[2,3072]{1,0:T(2,128)S(1)}, f32[2,3072]{1,0:T(2,128)S(1)}, u32[]{:S(2)}, u32[]{:S(2)}) collective-permute-start(f32[2,3072]{1,0:T(2,128)S(1)} %fusion.16), channel_id=1, source_target_pairs={{0,16},{8,24},{16,0},{24,8},{1,17},{9,25},{17,1},{25,9},{2,18},{10... | collective-permute-start | bytes 73736 | tf_op jit(solution)/shard_map/ppermute | solution.py:565
  299.7 3.7 collective-permute-start.30
  304.6 30.0 %collective-permute-start.31 = (bf16[2,192,1024]{2,1,0:T(8,128)(2,1)}, bf16[2,192,1024]{2,1,0:T(8,128)(2,1)S(1)}, u32[]{:S(2)}, u32[]{:S(2)}) collective-permute-start(bf16[2,192,1024]{2,1,0:T(8,128)(2,1)} %fusion.2), channel_id=1, source_target_pairs={{0,16},{8,24},{16,0},{24,8},{1,17},{9,25},{17,1},{25,9},{2,18},{10... | collective-permute-start | bytes 2359304 | tf_op jit(solution)/shard_map/ppermute | solution.py:565
  306.0 35.2 %collective-permute-start.32 = (bf16[2,192,1024]{2,1,0:T(8,128)(2,1)S(1)}, bf16[2,192,1024]{2,1,0:T(8,128)(2,1)S(1)}, u32[]{:S(2)}, u32[]{:S(2)}) collective-permute-start(bf16[2,192,1024]{2,1,0:T(8,128)(2,1)S(1)} %fusion.3), channel_id=1, source_target_pairs={{0,16},{8,24},{16,0},{24,8},{1,17},{9,25},{17,1},{25,9},{2,18},{10... | collective-permute-start | bytes 2359304 | tf_op jit(solution)/shard_map/ppermute | solution.py:565
  306.6 35.3 %copy-start.58 = (f32[1,2048]{1,0:T(1,128)S(1)}, f32[1,2048]{1,0:T(1,128)}, u32[]{:S(2)}) copy-start(f32[1,2048]{1,0:T(1,128)} %get-tuple-element.384) | copy-start | bytes 24580
  306.6 35.3 %copy-start.59 = (f32[1,2048]{1,0:T(1,128)S(1)}, f32[1,2048]{1,0:T(1,128)}, u32[]{:S(2)}) copy-start(f32[1,2048]{1,0:T(1,128)} %get-tuple-element.385) | copy-start | bytes 24580
  306.6 35.3 %copy-start.44 = (f32[1,3072]{1,0:T(1,128)S(1)}, f32[1,3072]{1,0:T(1,128)}, u32[]{:S(2)}) copy-start(f32[1,3072]{1,0:T(1,128)} %get-tuple-element.383) | copy-start | bytes 36868
  341.2 3.6 collective-permute-start.33
  342.7 1.9 collective-permute-start.34
  347.9 8.8 %collective-permute-start.35 = (f32[2,3072]{1,0:T(2,128)S(1)}, f32[2,3072]{1,0:T(2,128)S(1)}, u32[]{:S(2)}, u32[]{:S(2)}) collective-permute-start(f32[2,3072]{1,0:T(2,128)S(1)} %fusion.17), channel_id=1, source_target_pairs={{0,16},{8,24},{16,0},{24,8},{1,17},{9,25},{17,1},{25,9},{2,18},{10... | collective-permute-start | bytes 73736 | tf_op jit(solution)/shard_map/ppermute | solution.py:565
  349.4 19.6 %collective-permute-start.36 = (bf16[2,192,1024]{2,1,0:T(8,128)(2,1)}, bf16[2,192,1024]{2,1,0:T(8,128)(2,1)}, u32[]{:S(2)}, u32[]{:S(2)}) collective-permute-start(bf16[2,192,1024]{2,1,0:T(8,128)(2,1)} %fusion.4), channel_id=1, source_target_pairs={{0,16},{8,24},{16,0},{24,8},{1,17},{9,25},{17,1},{25,9},{2,18},{10... | collective-permute-start | bytes 2359304 | tf_op jit(solution)/shard_map/ppermute | solution.py:565
  373.2 1.2 collective-permute-start.37
  374.4 3.7 collective-permute-start.38
  378.0 3.7 collective-permute-start.39
  381.7 3.7 collective-permute-start.40
  385.4 4.5 %collective-permute-start.41 = (f32[16,128]{1,0:T(8,128)S(1)}, f32[16,128]{1,0:T(8,128)S(1)}, u32[]{:S(2)}, u32[]{:S(2)}) collective-permute-start(f32[16,128]{1,0:T(8,128)S(1)} %add.346), channel_id=1, source_target_pairs={{0,4},{1,5},{2,6},{3,7},{4,0},{5,1},{6,2},{7,3},{8,12},{9,13},{10,... | collective-permute-start | bytes 24584 | tf_op jit(solution)/shard_map/ppermute | solution.py:565
  398.8 3.2 collective-permute-start.42
  402.1 5.3 %collective-permute-start.43 = (f32[1,3072]{1,0:T(1,128)S(1)}, f32[1,3072]{1,0:T(1,128)S(1)}, u32[]{:S(2)}, u32[]{:S(2)}) collective-permute-start(f32[1,3072]{1,0:T(1,128)S(1)} %add.353), channel_id=1, source_target_pairs={{0,16},{8,24},{16,0},{24,8},{1,17},{9,25},{17,1},{25,9},{2,18},{10... | collective-permute-start | bytes 36872 | tf_op jit(solution)/shard_map/ppermute | solution.py:565
  (67 other events, 643.9 us)
Sparse Core Ops, SparseCore 0:
  10.9 66.9 all-gather.2
